TPU v7x, 128 devices: a whole 4x4x4 slice. The times are simulated.
128 devices in a mesh: section: 4 (over y), seq: 32 (over z, x, core).
Axes of the slice: x: 4, y: 4, z: 4, core: 2. Of those that a mesh axis runs over, the one named last changes fastest.
Arguments:
- stream: bfloat16 [4, 4096, 4096], P('section', 'seq'), may hold values from -4 to 4
- queries: bfloat16 [4, 4096, 4096], P('section', 'seq')
- span_kv: bfloat16 [4, 2, 4096, 512], P('section', None, 'seq')
- cache_kv: bfloat16 [4, 2, 4096, 512], P('section', None, 'seq'), may hold values from -6 to 6
- cache_len: int32 [32], replicated, may hold values from 48 to 80, as said below
- context_start: int32 [1], replicated, may hold values from 1 to 4096
- block_table: int32 [32, 32], replicated, may hold values from 0 to 1, as said below
Outputs:
- handed: bfloat16 [4, 4096, 4096], P('section', 'seq')
Inputs may be any that keep to these rules, and one draw needn't show every extreme that they name: `cache_len`: some index holds exactly 80 live slots. `block_table`: the diagonal is 1 and every entry above it is 0.
All inputs are finite; a program needn't handle non-finite values.
Results may differ from a plain program's by a relative error of at most 0.006.
Values may be sent and summed in bfloat16 or wider, within the bound.
No kernel may reach another device: no remote copies, remote signals or barrier semaphores. Data moves between devices by JAX's collectives and lax.ppermute only.
A program may use at most 64 MiB of HBM per device.

v0:
```python
import math

import jax
import jax.numpy as jnp
from jax import lax
from jax.sharding import PartitionSpec as P

HEAD_DIM = 128


def passed_along(value, axis, steps):
    count = lax.axis_size(axis)
    pairs = [(source, (source + steps) % count) for source in range(count)]
    return lax.ppermute(value, axis, pairs)


def shards(stream, queries, span_kv, cache_kv, cache_len, context_start, block_table):
    seq_count = lax.axis_size("seq")
    seq_index = lax.axis_index("seq")
    query_rows = queries[0]
    tok_rows = query_rows.shape[0]
    query_width = query_rows.shape[1]
    key_width = span_kv.shape[3]
    kv_count = key_width // HEAD_DIM
    group_size = query_width // key_width
    grouped = query_rows.reshape(tok_rows, kv_count, group_size, HEAD_DIM).transpose(1, 0, 2, 3)
    grouped = grouped.reshape(kv_count, tok_rows * group_size, HEAD_DIM)
    score_scale = 1.0 / math.sqrt(HEAD_DIM)
    slot_rows = cache_kv.shape[2]
    first_visible = slot_rows * seq_count - context_start[0]
    table_row = lax.dynamic_index_in_dim(block_table, seq_index, 0, keepdims=False)
    query_pos = seq_index * tok_rows + jnp.arange(tok_rows, dtype=jnp.int32)
    shard_ids = jnp.arange(seq_count, dtype=jnp.int32)

    def update(state_carry, key_values, allowed):
        row_top, row_total, accumulated = state_carry
        block_rows = key_values.shape[1]
        key_heads = key_values[0].reshape(block_rows, kv_count, HEAD_DIM)
        value_heads = key_values[1].reshape(block_rows, kv_count, HEAD_DIM)
        scores = (
            jnp.einsum("kqd,rkd->kqr", grouped, key_heads, preferred_element_type=jnp.float32)
            * score_scale
        )
        masked = jnp.where(allowed[None], scores, -1e30)
        new_top = jnp.maximum(row_top, jnp.max(masked, -1))
        weights = jnp.where(allowed[None], jnp.exp(scores - new_top[..., None]), 0.0)
        factor = jnp.exp(row_top - new_top)
        new_total = row_total * factor + jnp.sum(weights, -1)
        product = jnp.einsum(
            "kqr,rkd->kqd",
            weights.astype(jnp.bfloat16),
            value_heads,
            preferred_element_type=jnp.float32,
        )
        return (new_top, new_total, accumulated * factor[..., None] + product)

    def run_blocks(state_carry, shard_piece, shard_len, mask_rule):
        pairs = shard_piece[0]
        piece_rows = pairs.shape[1]
        shard_total = piece_rows // shard_len
        wanted = max(1, 512 // shard_len)
        shards_per = math.gcd(shard_total, wanted)
        block_rows = shards_per * shard_len
        block_count = piece_rows // block_rows

        def one_block(block, inner_carry):
            key_values = lax.dynamic_slice_in_dim(pairs, block * block_rows, block_rows, 1)
            allowed = mask_rule(block * block_rows, block_rows)

            def compute_block(given):
                return update(given, key_values, allowed)

            def leave_block(given):
                return given

            return lax.cond(jnp.any(allowed), compute_block, leave_block, inner_carry)

        return lax.fori_loop(0, block_count, one_block, state_carry)

    def cache_rule_for(shard_len):
        row_ids = jnp.arange(shard_len * seq_count, dtype=jnp.int32)
        owner = row_ids // shard_len
        slot_index = row_ids % shard_len
        live_counts = jnp.sum(
            jnp.where(owner[:, None] == shard_ids[None, :], cache_len[None, :], 0), 1
        )
        position = owner * slot_rows + slot_index
        cache_open = (slot_index < live_counts) & (position >= first_visible)

        def cache_rule(block_first, block_rows):
            return lax.dynamic_slice_in_dim(cache_open, block_first, block_rows, 0)[None, :]

        return cache_rule

    key_all = jnp.arange(tok_rows * seq_count, dtype=jnp.int32)
    key_owner = key_all // tok_rows
    table_open = (
        jnp.sum(jnp.where(key_owner[:, None] == shard_ids[None, :], table_row[None, :], 0), 1) == 1
    )

    def span_rule(block_first, block_rows):
        key_ids = block_first + jnp.arange(block_rows, dtype=jnp.int32)
        table_hits = lax.dynamic_slice_in_dim(table_open, block_first, block_rows, 0)
        allowed = (key_ids[None, :] <= query_pos[:, None]) & table_hits[None, :]
        allowed = jnp.broadcast_to(allowed[:, None, :], (tok_rows, group_size, block_rows))
        return allowed.reshape(tok_rows * group_size, block_rows)

    start_carry = (
        jnp.full((kv_count, tok_rows * group_size), -1e30, jnp.float32),
        jnp.zeros((kv_count, tok_rows * group_size), jnp.float32),
        jnp.zeros((kv_count, tok_rows * group_size, HEAD_DIM), jnp.float32),
    )
    slot_rule = cache_rule_for(slot_rows)
    after_cache = run_blocks(
        start_carry, lax.all_gather(cache_kv, "seq", axis=2, tiled=True), slot_rows, slot_rule
    )
    row_top, row_total, accumulated = run_blocks(
        after_cache, lax.all_gather(span_kv, "seq", axis=2, tiled=True), tok_rows, span_rule
    )
    mixed = accumulated / row_total[..., None]
    mixed = mixed.reshape(kv_count, tok_rows, group_size, HEAD_DIM).transpose(1, 0, 2, 3)
    attn = mixed.reshape(tok_rows, query_width).astype(jnp.bfloat16)
    layer_out = (stream[0].astype(jnp.float32) + attn.astype(jnp.float32)).astype(jnp.bfloat16)
    return passed_along(layer_out[None], "section", 1)


def solution(mesh):
    return jax.shard_map(
        shards,
        mesh=mesh,
        in_specs=(
            P("section", "seq", None),
            P("section", "seq", None),
            P("section", None, "seq", None),
            P("section", None, "seq", None),
            P(),
            P(),
            P(),
        ),
        out_specs=P("section", "seq", None),
        check_vma=False,
    )
```

profile of v0, /device:TPU:103, one launch (start us, length us, event | category | flops | bytes accessed | tf_op | source)
XLA Modules:
  0.0 313.2 jit_solution(13106420112782346071)
XLA Ops:
  13.5 55.2 %all-gather.3.cloned.1.call-done = bf16[1,2,4096,512]{2,3,1,0:T(8,128)(2,1)} async-done(((bf16[1,2,128,512]{2,3,1,0:T(8,128)(2,1)}), bf16[1,2,4096,512]{2,3,1,0:T(8,128)(2,1)}) %all-gather.3.cloned.1.call-update) | async-done | bytes 8388624 | tf_op jit(solution)/shard_map/all_gather | solution.py:115
  70.2 95.6 %while.35 = (s32[]{:T(128)}, f32[4,1024]{1,0:T(4,128)S(1)}, f32[4,1024]{1,0:T(4,128)S(1)}, f32[4,1024,128]{2,1,0:T(8,128)}, pred[4096]{0:T(1024)(128)(4,1)S(1)},...) while((s32[]{:T(128)}, f32[4,1024]{1,0:T(4,128)S(1)}, ...), condition=%wide.region_7.8_spmd, body=%wide.region_1.7_spmd.sunk | while | flops 1097867776 | bytes 33819440 | solution.py:78
  71.6 10.6 %conditional.5 = ((f32[4,1024]{1,0:T(4,128)S(1)}, f32[4,1024]{1,0:T(4,128)S(1)}, f32[4,1024,128]{2,1,0:T(8,128)})) conditional(s32[]{:T(128)} %convert_element_type.89, (f32[4,1024]{1,0:T(4,128)S(1)}, f32[4,1024]{1,0:T(4,128)S(1)}, f32[4,1024,128]{2,1,0:T(8,128)}) %tuple.87, (pred[512]{0:T(512)(128)(4,1)S(1)}, bf16[2,4096,512]{1,2,0:T(8,128)(2,1)}, ...), branch_computations={%region_3.3_spmd, %region_4.6_spmd} | conditional | flops 1097867264 | bytes 33818164 | solution.py:76
  83.5 10.6 %conditional.5 = ((f32[4,1024]{1,0:T(4,128)S(1)}, f32[4,1024]{1,0:T(4,128)S(1)}, f32[4,1024,128]{2,1,0:T(8,128)})) conditional(s32[]{:T(128)} %convert_element_type.89, (f32[4,1024]{1,0:T(4,128)S(1)}, f32[4,1024]{1,0:T(4,128)S(1)}, f32[4,1024,128]{2,1,0:T(8,128)}) %tuple.87, (pred[512]{0:T(512)(128)(4,1)S(1)}, bf16[2,4096,512]{1,2,0:T(8,128)(2,1)}, ...), branch_computations={%region_3.3_spmd, %region_4.6_spmd} | conditional | flops 1097867264 | bytes 33818164 | solution.py:76
  95.4 10.6 %conditional.5 = ((f32[4,1024]{1,0:T(4,128)S(1)}, f32[4,1024]{1,0:T(4,128)S(1)}, f32[4,1024,128]{2,1,0:T(8,128)})) conditional(s32[]{:T(128)} %convert_element_type.89, (f32[4,1024]{1,0:T(4,128)S(1)}, f32[4,1024]{1,0:T(4,128)S(1)}, f32[4,1024,128]{2,1,0:T(8,128)}) %tuple.87, (pred[512]{0:T(512)(128)(4,1)S(1)}, bf16[2,4096,512]{1,2,0:T(8,128)(2,1)}, ...), branch_computations={%region_3.3_spmd, %region_4.6_spmd} | conditional | flops 1097867264 | bytes 33818164 | solution.py:76
  100.9 5.0 %multiply_add_fusion = f32[4,1024,128]{2,1,0:T(8,128)} fusion(f32[4,1024,128]{2,1,0:T(8,128)} %get-tuple-element.339, bf16[512,4,128]{0,2,1:T(8,128)(2,1)S(1)} %bitcast.60, f32[4,512,1024]{2,1,0:T(8,128)S(1)} %get-tuple-element.443, f32[4,1024]{1,0:T(4,128)S(1)} %max.6, pred[512]{0:T(512)(128)(4,1)S(1)} %get-tuple-element.334, ...), kind=kOutput, calls=%fused_computation.10 | convolution fusion | flops 546308096 | bytes 13140480 | tf_op jit(solution)/shard_map/while/body/eval_jaxpr/cond/branch_1_fun/kqr,rkd->kqd/dot_general | solution.py:49
  107.4 10.6 %conditional.5 = ((f32[4,1024]{1,0:T(4,128)S(1)}, f32[4,1024]{1,0:T(4,128)S(1)}, f32[4,1024,128]{2,1,0:T(8,128)})) conditional(s32[]{:T(128)} %convert_element_type.89, (f32[4,1024]{1,0:T(4,128)S(1)}, f32[4,1024]{1,0:T(4,128)S(1)}, f32[4,1024,128]{2,1,0:T(8,128)}) %tuple.87, (pred[512]{0:T(512)(128)(4,1)S(1)}, bf16[2,4096,512]{1,2,0:T(8,128)(2,1)}, ...), branch_computations={%region_3.3_spmd, %region_4.6_spmd} | conditional | flops 1097867264 | bytes 33818164 | solution.py:76
  112.9 5.1 %multiply_add_fusion = f32[4,1024,128]{2,1,0:T(8,128)} fusion(f32[4,1024,128]{2,1,0:T(8,128)} %get-tuple-element.339, bf16[512,4,128]{0,2,1:T(8,128)(2,1)S(1)} %bitcast.60, f32[4,512,1024]{2,1,0:T(8,128)S(1)} %get-tuple-element.443, f32[4,1024]{1,0:T(4,128)S(1)} %max.6, pred[512]{0:T(512)(128)(4,1)S(1)} %get-tuple-element.334, ...), kind=kOutput, calls=%fused_computation.10 | convolution fusion | flops 546308096 | bytes 13140480 | tf_op jit(solution)/shard_map/while/body/eval_jaxpr/cond/branch_1_fun/kqr,rkd->kqd/dot_general | solution.py:49
  119.3 10.6 %conditional.5 = ((f32[4,1024]{1,0:T(4,128)S(1)}, f32[4,1024]{1,0:T(4,128)S(1)}, f32[4,1024,128]{2,1,0:T(8,128)})) conditional(s32[]{:T(128)} %convert_element_type.89, (f32[4,1024]{1,0:T(4,128)S(1)}, f32[4,1024]{1,0:T(4,128)S(1)}, f32[4,1024,128]{2,1,0:T(8,128)}) %tuple.87, (pred[512]{0:T(512)(128)(4,1)S(1)}, bf16[2,4096,512]{1,2,0:T(8,128)(2,1)}, ...), branch_computations={%region_3.3_spmd, %region_4.6_spmd} | conditional | flops 1097867264 | bytes 33818164 | solution.py:76
  131.3 10.6 %conditional.5 = ((f32[4,1024]{1,0:T(4,128)S(1)}, f32[4,1024]{1,0:T(4,128)S(1)}, f32[4,1024,128]{2,1,0:T(8,128)})) conditional(s32[]{:T(128)} %convert_element_type.89, (f32[4,1024]{1,0:T(4,128)S(1)}, f32[4,1024]{1,0:T(4,128)S(1)}, f32[4,1024,128]{2,1,0:T(8,128)}) %tuple.87, (pred[512]{0:T(512)(128)(4,1)S(1)}, bf16[2,4096,512]{1,2,0:T(8,128)(2,1)}, ...), branch_computations={%region_3.3_spmd, %region_4.6_spmd} | conditional | flops 1097867264 | bytes 33818164 | solution.py:76
  136.8 5.0 %multiply_add_fusion = f32[4,1024,128]{2,1,0:T(8,128)} fusion(f32[4,1024,128]{2,1,0:T(8,128)} %get-tuple-element.339, bf16[512,4,128]{0,2,1:T(8,128)(2,1)S(1)} %bitcast.60, f32[4,512,1024]{2,1,0:T(8,128)S(1)} %get-tuple-element.443, f32[4,1024]{1,0:T(4,128)S(1)} %max.6, pred[512]{0:T(512)(128)(4,1)S(1)} %get-tuple-element.334, ...), kind=kOutput, calls=%fused_computation.10 | convolution fusion | flops 546308096 | bytes 13140480 | tf_op jit(solution)/shard_map/while/body/eval_jaxpr/cond/branch_1_fun/kqr,rkd->kqd/dot_general | solution.py:49
  143.2 10.6 %conditional.5 = ((f32[4,1024]{1,0:T(4,128)S(1)}, f32[4,1024]{1,0:T(4,128)S(1)}, f32[4,1024,128]{2,1,0:T(8,128)})) conditional(s32[]{:T(128)} %convert_element_type.89, (f32[4,1024]{1,0:T(4,128)S(1)}, f32[4,1024]{1,0:T(4,128)S(1)}, f32[4,1024,128]{2,1,0:T(8,128)}) %tuple.87, (pred[512]{0:T(512)(128)(4,1)S(1)}, bf16[2,4096,512]{1,2,0:T(8,128)(2,1)}, ...), branch_computations={%region_3.3_spmd, %region_4.6_spmd} | conditional | flops 1097867264 | bytes 33818164 | solution.py:76
  148.8 5.0 %multiply_add_fusion = f32[4,1024,128]{2,1,0:T(8,128)} fusion(f32[4,1024,128]{2,1,0:T(8,128)} %get-tuple-element.339, bf16[512,4,128]{0,2,1:T(8,128)(2,1)S(1)} %bitcast.60, f32[4,512,1024]{2,1,0:T(8,128)S(1)} %get-tuple-element.443, f32[4,1024]{1,0:T(4,128)S(1)} %max.6, pred[512]{0:T(512)(128)(4,1)S(1)} %get-tuple-element.334, ...), kind=kOutput, calls=%fused_computation.10 | convolution fusion | flops 546308096 | bytes 13140480 | tf_op jit(solution)/shard_map/while/body/eval_jaxpr/cond/branch_1_fun/kqr,rkd->kqd/dot_general | solution.py:49
  155.2 10.6 %conditional.5 = ((f32[4,1024]{1,0:T(4,128)S(1)}, f32[4,1024]{1,0:T(4,128)S(1)}, f32[4,1024,128]{2,1,0:T(8,128)})) conditional(s32[]{:T(128)} %convert_element_type.89, (f32[4,1024]{1,0:T(4,128)S(1)}, f32[4,1024]{1,0:T(4,128)S(1)}, f32[4,1024,128]{2,1,0:T(8,128)}) %tuple.87, (pred[512]{0:T(512)(128)(4,1)S(1)}, bf16[2,4096,512]{1,2,0:T(8,128)(2,1)}, ...), branch_computations={%region_3.3_spmd, %region_4.6_spmd} | conditional | flops 1097867264 | bytes 33818164 | solution.py:76
  165.7 108.5 %while.36 = (s32[]{:T(128)}, f32[4,1024]{1,0:T(4,128)S(1)}, f32[4,1024]{1,0:T(4,128)S(1)}, f32[4,1024,128]{2,1,0:T(8,128)}, pred[4096]{0:T(1024)(128)(4,1)S(1)},...) while((s32[]{:T(128)}, f32[4,1024]{1,0:T(4,128)S(1)}, ...), condition=%wide.region_15.16_spmd.clone, body=%wide.region_9.15_spmd.clone.sunk | while | flops 1098523264 | bytes 37165888 | solution.py:78
  168.0 11.3 %conditional.6 = ((f32[4,1024]{1,0:T(4,128)S(1)}, f32[4,1024]{1,0:T(4,128)S(1)}, f32[4,1024,128]{2,1,0:T(8,128)})) conditional(s32[]{:T(128)} %convert_element_type.90, (f32[4,1024]{1,0:T(4,128)S(1)}, f32[4,1024]{1,0:T(4,128)S(1)}, f32[4,1024,128]{2,1,0:T(8,128)}) %tuple.90, (pred[128,8,512]{2,1,0:T(8,128)(4,1)S(1)}, ...), branch_computations={%region_11.11_spmd, %region_12.14_spmd} | conditional | flops 1097867264 | bytes 36438068 | solution.py:76
  174.0 5.3 %multiply_add_fusion.2 = f32[4,1024,128]{2,1,0:T(8,128)} fusion(f32[4,1024,128]{2,1,0:T(8,128)} %get-tuple-element.357, bf16[512,4,128]{0,2,1:T(8,128)(2,1)S(1)} %bitcast.59, f32[4,512,1024]{2,1,0:T(8,128)S(1)} %get-tuple-element.447, f32[4,1024]{1,0:T(4,128)S(1)} %max.7, pred[1024,512]{0,1:T(8,128)(4,1)S(1)} %copy.26, f32[4,1024]{1,0:T(4,128)S(1)} %get-tuple-element.439), kind=kOutput, calls=%fused_computation.29 | convolution fusion | flops 546308096 | bytes 13664256 | tf_op jit(solution)/shard_map/while/body/eval_jaxpr/cond/branch_1_fun/kqr,rkd->kqd/dot_general | solution.py:49
  181.6 11.3 %conditional.6 = ((f32[4,1024]{1,0:T(4,128)S(1)}, f32[4,1024]{1,0:T(4,128)S(1)}, f32[4,1024,128]{2,1,0:T(8,128)})) conditional(s32[]{:T(128)} %convert_element_type.90, (f32[4,1024]{1,0:T(4,128)S(1)}, f32[4,1024]{1,0:T(4,128)S(1)}, f32[4,1024,128]{2,1,0:T(8,128)}) %tuple.90, (pred[128,8,512]{2,1,0:T(8,128)(4,1)S(1)}, ...), branch_computations={%region_11.11_spmd, %region_12.14_spmd} | conditional | flops 1097867264 | bytes 36438068 | solution.py:76
  187.5 5.3 %multiply_add_fusion.2 = f32[4,1024,128]{2,1,0:T(8,128)} fusion(f32[4,1024,128]{2,1,0:T(8,128)} %get-tuple-element.357, bf16[512,4,128]{0,2,1:T(8,128)(2,1)S(1)} %bitcast.59, f32[4,512,1024]{2,1,0:T(8,128)S(1)} %get-tuple-element.447, f32[4,1024]{1,0:T(4,128)S(1)} %max.7, pred[1024,512]{0,1:T(8,128)(4,1)S(1)} %copy.26, f32[4,1024]{1,0:T(4,128)S(1)} %get-tuple-element.439), kind=kOutput, calls=%fused_computation.29 | convolution fusion | flops 546308096 | bytes 13664256 | tf_op jit(solution)/shard_map/while/body/eval_jaxpr/cond/branch_1_fun/kqr,rkd->kqd/dot_general | solution.py:49
  195.1 11.3 %conditional.6 = ((f32[4,1024]{1,0:T(4,128)S(1)}, f32[4,1024]{1,0:T(4,128)S(1)}, f32[4,1024,128]{2,1,0:T(8,128)})) conditional(s32[]{:T(128)} %convert_element_type.90, (f32[4,1024]{1,0:T(4,128)S(1)}, f32[4,1024]{1,0:T(4,128)S(1)}, f32[4,1024,128]{2,1,0:T(8,128)}) %tuple.90, (pred[128,8,512]{2,1,0:T(8,128)(4,1)S(1)}, ...), branch_computations={%region_11.11_spmd, %region_12.14_spmd} | conditional | flops 1097867264 | bytes 36438068 | solution.py:76
  201.1 5.3 %multiply_add_fusion.2 = f32[4,1024,128]{2,1,0:T(8,128)} fusion(f32[4,1024,128]{2,1,0:T(8,128)} %get-tuple-element.357, bf16[512,4,128]{0,2,1:T(8,128)(2,1)S(1)} %bitcast.59, f32[4,512,1024]{2,1,0:T(8,128)S(1)} %get-tuple-element.447, f32[4,1024]{1,0:T(4,128)S(1)} %max.7, pred[1024,512]{0,1:T(8,128)(4,1)S(1)} %copy.26, f32[4,1024]{1,0:T(4,128)S(1)} %get-tuple-element.439), kind=kOutput, calls=%fused_computation.29 | convolution fusion | flops 546308096 | bytes 13664256 | tf_op jit(solution)/shard_map/while/body/eval_jaxpr/cond/branch_1_fun/kqr,rkd->kqd/dot_general | solution.py:49
  208.7 11.3 %conditional.6 = ((f32[4,1024]{1,0:T(4,128)S(1)}, f32[4,1024]{1,0:T(4,128)S(1)}, f32[4,1024,128]{2,1,0:T(8,128)})) conditional(s32[]{:T(128)} %convert_element_type.90, (f32[4,1024]{1,0:T(4,128)S(1)}, f32[4,1024]{1,0:T(4,128)S(1)}, f32[4,1024,128]{2,1,0:T(8,128)}) %tuple.90, (pred[128,8,512]{2,1,0:T(8,128)(4,1)S(1)}, ...), branch_computations={%region_11.11_spmd, %region_12.14_spmd} | conditional | flops 1097867264 | bytes 36438068 | solution.py:76
  214.7 5.3 %multiply_add_fusion.2 = f32[4,1024,128]{2,1,0:T(8,128)} fusion(f32[4,1024,128]{2,1,0:T(8,128)} %get-tuple-element.357, bf16[512,4,128]{0,2,1:T(8,128)(2,1)S(1)} %bitcast.59, f32[4,512,1024]{2,1,0:T(8,128)S(1)} %get-tuple-element.447, f32[4,1024]{1,0:T(4,128)S(1)} %max.7, pred[1024,512]{0,1:T(8,128)(4,1)S(1)} %copy.26, f32[4,1024]{1,0:T(4,128)S(1)} %get-tuple-element.439), kind=kOutput, calls=%fused_computation.29 | convolution fusion | flops 546308096 | bytes 13664256 | tf_op jit(solution)/shard_map/while/body/eval_jaxpr/cond/branch_1_fun/kqr,rkd->kqd/dot_general | solution.py:49
  222.2 11.3 %conditional.6 = ((f32[4,1024]{1,0:T(4,128)S(1)}, f32[4,1024]{1,0:T(4,128)S(1)}, f32[4,1024,128]{2,1,0:T(8,128)})) conditional(s32[]{:T(128)} %convert_element_type.90, (f32[4,1024]{1,0:T(4,128)S(1)}, f32[4,1024]{1,0:T(4,128)S(1)}, f32[4,1024,128]{2,1,0:T(8,128)}) %tuple.90, (pred[128,8,512]{2,1,0:T(8,128)(4,1)S(1)}, ...), branch_computations={%region_11.11_spmd, %region_12.14_spmd} | conditional | flops 1097867264 | bytes 36438068 | solution.py:76
  228.2 5.3 %multiply_add_fusion.2 = f32[4,1024,128]{2,1,0:T(8,128)} fusion(f32[4,1024,128]{2,1,0:T(8,128)} %get-tuple-element.357, bf16[512,4,128]{0,2,1:T(8,128)(2,1)S(1)} %bitcast.59, f32[4,512,1024]{2,1,0:T(8,128)S(1)} %get-tuple-element.447, f32[4,1024]{1,0:T(4,128)S(1)} %max.7, pred[1024,512]{0,1:T(8,128)(4,1)S(1)} %copy.26, f32[4,1024]{1,0:T(4,128)S(1)} %get-tuple-element.439), kind=kOutput, calls=%fused_computation.29 | convolution fusion | flops 546308096 | bytes 13664256 | tf_op jit(solution)/shard_map/while/body/eval_jaxpr/cond/branch_1_fun/kqr,rkd->kqd/dot_general | solution.py:49
  235.8 11.3 %conditional.6 = ((f32[4,1024]{1,0:T(4,128)S(1)}, f32[4,1024]{1,0:T(4,128)S(1)}, f32[4,1024,128]{2,1,0:T(8,128)})) conditional(s32[]{:T(128)} %convert_element_type.90, (f32[4,1024]{1,0:T(4,128)S(1)}, f32[4,1024]{1,0:T(4,128)S(1)}, f32[4,1024,128]{2,1,0:T(8,128)}) %tuple.90, (pred[128,8,512]{2,1,0:T(8,128)(4,1)S(1)}, ...), branch_computations={%region_11.11_spmd, %region_12.14_spmd} | conditional | flops 1097867264 | bytes 36438068 | solution.py:76
  241.8 5.3 %multiply_add_fusion.2 = f32[4,1024,128]{2,1,0:T(8,128)} fusion(f32[4,1024,128]{2,1,0:T(8,128)} %get-tuple-element.357, bf16[512,4,128]{0,2,1:T(8,128)(2,1)S(1)} %bitcast.59, f32[4,512,1024]{2,1,0:T(8,128)S(1)} %get-tuple-element.447, f32[4,1024]{1,0:T(4,128)S(1)} %max.7, pred[1024,512]{0,1:T(8,128)(4,1)S(1)} %copy.26, f32[4,1024]{1,0:T(4,128)S(1)} %get-tuple-element.439), kind=kOutput, calls=%fused_computation.29 | convolution fusion | flops 546308096 | bytes 13664256 | tf_op jit(solution)/shard_map/while/body/eval_jaxpr/cond/branch_1_fun/kqr,rkd->kqd/dot_general | solution.py:49
  249.4 11.3 %conditional.6 = ((f32[4,1024]{1,0:T(4,128)S(1)}, f32[4,1024]{1,0:T(4,128)S(1)}, f32[4,1024,128]{2,1,0:T(8,128)})) conditional(s32[]{:T(128)} %convert_element_type.90, (f32[4,1024]{1,0:T(4,128)S(1)}, f32[4,1024]{1,0:T(4,128)S(1)}, f32[4,1024,128]{2,1,0:T(8,128)}) %tuple.90, (pred[128,8,512]{2,1,0:T(8,128)(4,1)S(1)}, ...), branch_computations={%region_11.11_spmd, %region_12.14_spmd} | conditional | flops 1097867264 | bytes 36438068 | solution.py:76
  255.3 5.3 %multiply_add_fusion.2 = f32[4,1024,128]{2,1,0:T(8,128)} fusion(f32[4,1024,128]{2,1,0:T(8,128)} %get-tuple-element.357, bf16[512,4,128]{0,2,1:T(8,128)(2,1)S(1)} %bitcast.59, f32[4,512,1024]{2,1,0:T(8,128)S(1)} %get-tuple-element.447, f32[4,1024]{1,0:T(4,128)S(1)} %max.7, pred[1024,512]{0,1:T(8,128)(4,1)S(1)} %copy.26, f32[4,1024]{1,0:T(4,128)S(1)} %get-tuple-element.439), kind=kOutput, calls=%fused_computation.29 | convolution fusion | flops 546308096 | bytes 13664256 | tf_op jit(solution)/shard_map/while/body/eval_jaxpr/cond/branch_1_fun/kqr,rkd->kqd/dot_general | solution.py:49
  262.9 11.3 %conditional.6 = ((f32[4,1024]{1,0:T(4,128)S(1)}, f32[4,1024]{1,0:T(4,128)S(1)}, f32[4,1024,128]{2,1,0:T(8,128)})) conditional(s32[]{:T(128)} %convert_element_type.90, (f32[4,1024]{1,0:T(4,128)S(1)}, f32[4,1024]{1,0:T(4,128)S(1)}, f32[4,1024,128]{2,1,0:T(8,128)}) %tuple.90, (pred[128,8,512]{2,1,0:T(8,128)(4,1)S(1)}, ...), branch_computations={%region_11.11_spmd, %region_12.14_spmd} | conditional | flops 1097867264 | bytes 36438068 | solution.py:76
  268.9 5.3 %multiply_add_fusion.2 = f32[4,1024,128]{2,1,0:T(8,128)} fusion(f32[4,1024,128]{2,1,0:T(8,128)} %get-tuple-element.357, bf16[512,4,128]{0,2,1:T(8,128)(2,1)S(1)} %bitcast.59, f32[4,512,1024]{2,1,0:T(8,128)S(1)} %get-tuple-element.447, f32[4,1024]{1,0:T(4,128)S(1)} %max.7, pred[1024,512]{0,1:T(8,128)(4,1)S(1)} %copy.26, f32[4,1024]{1,0:T(4,128)S(1)} %get-tuple-element.439), kind=kOutput, calls=%fused_computation.29 | convolution fusion | flops 546308096 | bytes 13664256 | tf_op jit(solution)/shard_map/while/body/eval_jaxpr/cond/branch_1_fun/kqr,rkd->kqd/dot_general | solution.py:49
  280.9 24.5 %collective-permute-done = bf16[1,128,4096]{2,1,0:T(8,128)(2,1)S(1)} collective-permute-done((bf16[1,128,4096]{2,1,0:T(8,128)(2,1)S(1)}, bf16[1,128,4096]{2,1,0:T(8,128)(2,1)S(1)}, u32[]{:S(2)}, u32[]{:S(2)}) %collective-permute-start) | collective-permute-done | bytes 1048608 | tf_op jit(solution)/shard_map/ppermute | solution.py:14
  (190 shorter events, 145.3 us)
Async XLA Ops:
  6.5 6.0 %copy-start = (s32[32,32]{1,0:T(8,128)S(1)}, s32[32,32]{1,0:T(8,128)}, u32[]{:S(2)}) copy-start(s32[32,32]{1,0:T(8,128)} %param.21) | copy-start | bytes 12292
  6.5 62.2 %all-gather.3.cloned.1.call-start = ((), (), s32[]{:S(2)}) async-start(), calls=%async_computation | async-start | bytes 8650752 | tf_op jit(solution)/shard_map/all_gather | solution.py:115
  8.4 157.4 %all-gather.5.cloned.1.call-start = ((), (), s32[]{:S(2)}) async-start(), calls=%async_computation.1 | async-start | bytes 8650752 | tf_op jit(solution)/shard_map/all_gather | solution.py:118
  274.2 3.6 %copy-start.1 = (bf16[1,128,4096]{2,1,0:T(8,128)(2,1)S(1)}, bf16[1,128,4096]{2,1,0:T(8,128)(2,1)}, u32[]{:S(2)}) copy-start(bf16[1,128,4096]{2,1,0:T(8,128)(2,1)} %param.15) | copy-start | bytes 3145732
  279.6 25.8 %collective-permute-start = (bf16[1,128,4096]{2,1,0:T(8,128)(2,1)S(1)}, bf16[1,128,4096]{2,1,0:T(8,128)(2,1)S(1)}, u32[]{:S(2)}, u32[]{:S(2)}) collective-permute-start(bf16[1,128,4096]{2,1,0:T(8,128)(2,1)S(1)} %add_convert_fusion), channel_id=1, source_target_pairs={{0,32},{32,64},{64,96},{96,0},{1,33},{33,65},{65,97},{97,1},{2,34}... | collective-permute-start | bytes 3145736 | tf_op jit(solution)/shard_map/ppermute | solution.py:14
Sparse Core Ops, SparseCore 0:
  9.5 59.1 all-gather.2
  70.9 59.3 all-gather.4
where the time goes:
time: 315 us; the launch traced here: 313 us
  matrix products  115 us (37%)
  waiting for transfers between devices  79.8 us (25%)
  other arithmetic  52 us (17%)
  local copies, waits for them, and re-layouts  40 us (13%)
  between operations  14.1 us (4%)
  loops' own time  11.2 us (4%)
    dot_general x16, matrix products, update(): jnp.einsum('kqr,rkd->kqd', weights.astype(jnp.bfloat16), value_heads, pre...  83 us
    all_gather x1, waiting for transfers between devices, shards(): lax.all_gather(cache_kv, 'seq', axis=2, tiled=True)  55.2 us
    dot_general x16, matrix products, update(): jnp.einsum('kqd,rkd->kqr', grouped, key_heads, preferred_element_type=jnp...  31.9 us
    reduce_sum x16, other arithmetic, update(): new_total = row_total * factor + jnp.sum(weights, -1)  30.6 us
    ppermute x1, waiting for transfers between devices, passed_along(): return lax.ppermute(value, axis, pairs)  24.5 us
    slice x16, local copies, waits for them, and re-layouts, update(): value_heads = key_values[1].reshape(block_rows, kv_count, HEAD_DIM)  20.5 us
    reduce_or x16, other arithmetic, one_block(): return lax.cond(jnp.any(allowed), compute_block, leave_block, inner_carry)  15.3 us
    another operation x2, loops' own time, run_blocks(): return lax.fori_loop(0, block_count, one_block, state_carry)  10.3 us
  transfers between devices with their start and end apart: 3, of which 2 were waited for; matrix products, arithmetic and copies ran while one was open for 31% of the time, Pallas kernels for 0%

commit v1 on v0

v1 whole, which is shorter than its diff:
```python
import functools
import math

import jax
import jax.numpy as jnp
from jax import lax
from jax.experimental import pallas as pl
from jax.experimental.pallas import tpu as pltpu
from jax.sharding import PartitionSpec as P

DIM = 128
GROUP = 8
TOK = 128
SLOTS = 128
LIVE = 80
SHARDS = 32
CACHE = SLOTS * SHARDS
ROWS = GROUP * TOK
PER = 4
SPAN_ROWS = PER * 2 * TOK
CACHE_ROWS = PER * 2 * LIVE
CHUNK = SPAN_ROWS + CACHE_ROWS
BLOCK = 128
TILE_BLOCKS = 2
OFFSETS = (0, -1, 1, 2)
TO_LOG2 = math.log2(math.e) / math.sqrt(DIM)
LEAST_TOTAL, MOST_TOTAL = 1e-12, 1e30
LEAST_MIXED, MOST_MIXED = 1e-20, 1e37
AXES = ("section", "seq")


def moved(value, rule):
    pairs = []
    for y in range(4):
        for z in range(4):
            for x in range(4):
                for c in range(2):
                    ty, tz, tx, tc = rule(y, z, x, c)
                    source = y * 32 + (z * 4 + x) * 2 + c
                    target = (ty % 4) * 32 + ((tz % 4) * 4 + tx % 4) * 2 + tc
                    pairs.append((source, target))
    return lax.ppermute(value, AXES, pairs)


def swapped(value):
    return moved(value, lambda y, z, x, c: (y, z, x, 1 - c))


def up(value):
    return moved(value, lambda y, z, x, c: (y + 1, z, x, c))


def up_swapped(value):
    return moved(value, lambda y, z, x, c: (y + 1, z, x, 1 - c))


def first_ring(value, k):
    return moved(value, lambda y, z, x, c: (y, z, x + k, c) if c == 0 else (y, z + k, x, c))


def second_ring(value, k):
    return moved(value, lambda y, z, x, c: (y, z + k, x, c) if c == 0 else (y, z, x + k, c))


def chip_of(place, row, col):
    z, x, c = place
    dz = jnp.where(c == 0, row, col)
    dx = jnp.where(c == 0, col, row)
    return ((z + dz + 4) % 4) * 4 + (x + dx + 4) % 4


def stage_kernel(rows_of, has_carry, last, *refs):
    refs = list(refs)
    place_ref, table_ref, len_ref, start_ref = refs[:4]
    refs = refs[4:]
    q_refs, refs = refs[:2], refs[2:]
    chunk_refs, refs = refs[: 2 * len(rows_of)], refs[2 * len(rows_of) :]
    carry_ref = None
    if has_carry:
        carry_ref, refs = refs[0], refs[1:]
    if last:
        own_ref, other_ref, bad_ref = refs[:3]
        refs = refs[3:]
        total_ref, refs = refs[0], refs[1:]
    else:
        total_ref, refs = refs[0], refs[1:]
    keys, values, queries, todo = refs
    count = len(rows_of)
    place = (place_ref[0], place_ref[1], place_ref[2])
    core = place[2]
    chip = place[0] * 4 + place[1]
    first_open = CACHE - start_ref[0]

    for n in range(count):
        base = n * CHUNK
        keys[base : base + CHUNK, :] = chunk_refs[2 * n][...]
        value_ref = chunk_refs[2 * n + 1]
        values[base : base + SPAN_ROWS, :DIM] = value_ref[:SPAN_ROWS, :]
        values[base : base + SPAN_ROWS, DIM:] = jnp.ones((SPAN_ROWS, DIM), jnp.bfloat16)
        for k in range(PER):
            there = chip_of(place, rows_of[n], OFFSETS[k])
            for e in range(2):
                shard = 2 * there + (core if e == 0 else 1 - core)
                low = first_open - shard * SLOTS
                slot = lax.broadcasted_iota(jnp.int32, (LIVE, DIM), 0)
                live = (slot >= low) & (slot < len_ref[shard])
                at = SPAN_ROWS + (2 * k + e) * LIVE
                piece = value_ref[at : at + LIVE, :].astype(jnp.float32)
                values[base + at : base + at + LIVE, :DIM] = jnp.where(live, piece, 0.0).astype(jnp.bfloat16)
                values[base + at : base + at + LIVE, DIM:] = jnp.where(live, 1.0, 0.0).astype(jnp.bfloat16)
    spare = count * CHUNK
    keys[spare : spare + BLOCK, :] = jnp.zeros((BLOCK, DIM), jnp.bfloat16)
    values[spare : spare + BLOCK, :] = jnp.zeros((BLOCK, 2 * DIM), jnp.bfloat16)

    worst_low = None
    for q in range(2):
        mine = 2 * chip + (core if q == 0 else 1 - core)
        for h in range(GROUP):
            queries[h * TOK : (h + 1) * TOK, :] = q_refs[q][:, h * DIM : (h + 1) * DIM]

        filled = jnp.int32(0)
        for n in range(count):
            for k in range(PER):
                there = chip_of(place, rows_of[n], OFFSETS[k])
                for e in range(2):
                    shard = 2 * there + (core if e == 0 else 1 - core)
                    wanted = (shard < mine) & (table_ref[mine, shard] == 1)
                    todo[filled] = n * CHUNK + (2 * k + e) * TOK
                    filled = filled + jnp.where(wanted, 1, 0)
            seen = []
            for k in range(PER):
                there = chip_of(place, rows_of[n], OFFSETS[k])
                for e in range(2):
                    shard = 2 * there + (core if e == 0 else 1 - core)
                    seen.append(shard * SLOTS + len_ref[shard] > first_open)
            for b in range(CACHE_ROWS // BLOCK):
                wanted = functools.reduce(
                    jnp.logical_or, seen[b * BLOCK // LIVE : ((b + 1) * BLOCK - 1) // LIVE + 1]
                )
                todo[filled] = n * CHUNK + SPAN_ROWS + b * BLOCK
                filled = filled + jnp.where(wanted, 1, 0)
        for b in range(TILE_BLOCKS - 1):
            todo[filled + b] = spare

        def weights_of(rows):
            scores = lax.dot_general(
                queries[...], rows, (((1,), (1,)), ((), ())), preferred_element_type=jnp.float32
            )
            return jnp.exp2(scores * TO_LOG2)

        def mix(weights, rows):
            return jnp.dot(weights.astype(jnp.bfloat16), rows, preferred_element_type=jnp.float32)

        if rows_of[0] == 0:
            at = q * TOK
            token = lax.broadcasted_iota(jnp.int32, (TOK, TOK), 0)
            key = lax.broadcasted_iota(jnp.int32, (TOK, TOK), 1)
            weights = weights_of(keys[at : at + TOK, :]).reshape(GROUP, TOK, TOK)
            weights = jnp.where((key <= token)[None], weights, 0.0).reshape(ROWS, TOK)
            part = mix(weights, values[at : at + TOK, :])
            if has_carry:
                part = part + carry_ref[q]
            total_ref[q] = part
        else:
            total_ref[q] = carry_ref[q]

        def tile(step, _):
            spots = [pl.multiple_of(todo[step * TILE_BLOCKS + b], BLOCK) for b in range(TILE_BLOCKS)]
            key_rows = jnp.concatenate([keys[pl.ds(s, BLOCK), :] for s in spots], 0)
            value_rows = jnp.concatenate([values[pl.ds(s, BLOCK), :] for s in spots], 0)
            total_ref[q] += mix(weights_of(key_rows), value_rows)
            return 0

        lax.fori_loop(0, (filled + TILE_BLOCKS - 1) // TILE_BLOCKS, tile, 0)

        if last:
            out_ref = own_ref if q == 0 else other_ref
            for h in range(GROUP):
                mixed = total_ref[q, h * TOK : (h + 1) * TOK, :DIM]
                total = total_ref[q, h * TOK : (h + 1) * TOK, DIM:]
                out_ref[:, h * DIM : (h + 1) * DIM] = (mixed / total).astype(jnp.bfloat16)
                if worst_low is None:
                    worst_low, worst_high, largest = total, total, jnp.abs(mixed)
                    strange = jnp.where((total > 0.0) & (jnp.abs(mixed) < MOST_MIXED), 0.0, 1.0)
                else:
                    worst_low = jnp.minimum(worst_low, total)
                    worst_high = jnp.maximum(worst_high, total)
                    largest = jnp.maximum(largest, jnp.abs(mixed))
                    good = (total > 0.0) & (jnp.abs(mixed) < MOST_MIXED)
                    strange = jnp.maximum(strange, jnp.where(good, 0.0, 1.0))
    if last:
        fine = (
            (jnp.max(strange) == 0.0)
            & (jnp.min(worst_low) >= LEAST_TOTAL)
            & (jnp.max(worst_high) <= MOST_TOTAL)
            & (jnp.max(largest) >= LEAST_MIXED)
        )
        bad_ref[0] = jnp.where(fine, 0, 1)


def stage(rows_of, last, scalars, queries, chunks, carry=None):
    smem = pl.BlockSpec(memory_space=pltpu.SMEM)
    vmem = pl.BlockSpec(memory_space=pltpu.VMEM)
    operands = list(scalars) + list(queries)
    for k, v in chunks:
        operands += [k, v]
    if carry is not None:
        operands.append(carry)
    specs = [smem] * 4 + [vmem] * (len(operands) - 4)
    count = len(rows_of)
    total = ((2, ROWS, 2 * DIM), jnp.float32)
    scratch = [
        pltpu.VMEM((count * CHUNK + BLOCK, DIM), jnp.bfloat16),
        pltpu.VMEM((count * CHUNK + BLOCK, 2 * DIM), jnp.bfloat16),
        pltpu.VMEM((ROWS, DIM), jnp.bfloat16),
        pltpu.SMEM((count * (PER * 2 + CACHE_ROWS // BLOCK) + TILE_BLOCKS,), jnp.int32),
    ]
    if last:
        out_shape = (
            jax.ShapeDtypeStruct((TOK, GROUP * DIM), jnp.bfloat16),
            jax.ShapeDtypeStruct((TOK, GROUP * DIM), jnp.bfloat16),
            jax.ShapeDtypeStruct((1,), jnp.int32),
        )
        out_specs = (vmem, vmem, smem)
        scratch = [pltpu.VMEM(*total)] + scratch
    else:
        out_shape = jax.ShapeDtypeStruct(*total)
        out_specs = vmem
    flops = count * 2 * ROWS * CHUNK * DIM * 6
    return pl.pallas_call(
        functools.partial(stage_kernel, tuple(rows_of), carry is not None, last),
        out_shape=out_shape,
        in_specs=specs,
        out_specs=out_specs,
        scratch_shapes=scratch,
        compiler_params=pltpu.CompilerParams(vmem_limit_bytes=40 * 1024 * 1024),
        cost_estimate=pl.CostEstimate(
            flops=flops, bytes_accessed=count * CHUNK * DIM * 4, transcendentals=count * 2 * ROWS * CHUNK
        ),
        name="stage_" + "_".join(str(r % 4) for r in rows_of),
    )(*operands)


def slow(scalars, queries, chunks):
    place, table, lengths, start = scalars
    spot = (place[0], place[1], place[2])
    core = spot[2]
    chip = spot[0] * 4 + spot[1]
    results = []
    for q in range(2):
        mine = 2 * chip + (core if q == 0 else 1 - core)
        token = mine * TOK + jnp.arange(TOK, dtype=jnp.int32)
        rows = queries[q].reshape(TOK, GROUP, DIM)
        top = jnp.full((GROUP, TOK), -jnp.inf, jnp.float32)
        total = jnp.zeros((GROUP, TOK), jnp.float32)
        mixed = jnp.zeros((GROUP, TOK, DIM), jnp.float32)
        for row in OFFSETS:
            k, v = chunks[row]
            shard = jnp.stack(
                [
                    2 * chip_of(spot, row, col) + (core if e == 0 else 1 - core)
                    for col in OFFSETS
                    for e in range(2)
                ]
            )
            key = (shard[:, None] * TOK + jnp.arange(TOK)[None]).reshape(-1)
            listed = jnp.repeat(table[mine][shard] == 1, TOK)
            span_open = (key[None] <= token[:, None]) & listed[None]
            slot = jnp.arange(LIVE)[None]
            live = (slot < lengths[shard][:, None]) & (shard[:, None] * SLOTS + slot >= CACHE - start[0])
            open_all = jnp.concatenate(
                [span_open, jnp.broadcast_to(live.reshape(1, -1), (TOK, CACHE_ROWS))], 1
            )[None]
            scores = jnp.einsum("tgd,nd->gtn", rows, k, preferred_element_type=jnp.float32)
            scores = jnp.where(open_all, scores * (1.0 / math.sqrt(DIM)), -jnp.inf)
            new_top = jnp.maximum(top, jnp.max(scores, -1))
            shift = jnp.where(new_top == -jnp.inf, 0.0, new_top)
            weights = jnp.where(open_all, jnp.exp(scores - shift[..., None]), 0.0)
            factor = jnp.exp(top - shift)
            total = total * factor + jnp.sum(weights, -1)
            mixed = mixed * factor[..., None] + jnp.einsum(
                "gtn,nd->gtd", weights.astype(jnp.bfloat16), v, preferred_element_type=jnp.float32
            )
            top = new_top
        out = (mixed / total[..., None]).astype(jnp.bfloat16)
        results.append(out.transpose(1, 0, 2).reshape(TOK, GROUP * DIM))
    return tuple(results)


def guarded(scalars, queries, chunks, own, other, bad):
    return lax.cond(
        bad[0] == 0, lambda: (own, other), lambda: slow(scalars, queries, chunks)
    )


def joined(units):
    spans = [u[:, : 2 * TOK] for u in units]
    caches = [u[:, 2 * TOK :] for u in units]
    return jnp.concatenate(spans + caches, 1)


def paired(own, other):
    return jnp.concatenate([own[:, :TOK], other[:, :TOK], own[:, TOK:], other[:, TOK:]], 1)


def gathered(unit):
    row = joined([unit] + [first_ring(unit, -k) for k in OFFSETS[1:]])
    before, after = second_ring(row, 1), second_ring(row, -1)
    far_k, far_v = second_ring(before[0], 1), second_ring(after[1], -1)
    return {
        0: (row[0], row[1]),
        -1: (before[0], before[1]),
        1: (after[0], after[1]),
        2: (far_k, far_v),
    }


def shards(stream, queries, span_kv, cache_kv, cache_len, context_start, block_table):
    seq = lax.axis_index("seq")
    core = seq % 2
    place = jnp.stack([seq // 8, (seq // 2) % 4, core]).astype(jnp.int32)
    scalars = (place, block_table, cache_len, context_start)

    def pair_of(head):
        span = lax.dynamic_slice_in_dim(span_kv[0], head * DIM, DIM, 2)
        cache = lax.dynamic_slice_in_dim(cache_kv[0, :, :LIVE], head * DIM, DIM, 2)
        return jnp.concatenate([span, cache], 1)

    def query_of(head):
        return lax.dynamic_slice_in_dim(queries[0], head * GROUP * DIM, GROUP * DIM, 1)

    near_unit = paired(pair_of(core), swapped(pair_of(1 - core)))
    late_unit = paired(up(pair_of(2 + core)), up_swapped(pair_of(3 - core)))
    near_q = (query_of(core), swapped(query_of(1 - core)))
    late_q = (up(query_of(2 + core)), up_swapped(query_of(3 - core)))
    half = GROUP * DIM * 2
    late_stream = up(stream[0, :, half:])

    near = gathered(near_unit)
    late = gathered(late_unit)

    own, other, bad = stage(OFFSETS, True, scalars, near_q, [near[r] for r in OFFSETS])
    own, other = guarded(scalars, near_q, near, own, other, bad)

    def added(own, other, base):
        received = swapped(other)
        both = jnp.where(
            core == 0, jnp.concatenate([own, received], 1), jnp.concatenate([received, own], 1)
        )
        return (base.astype(jnp.float32) + both.astype(jnp.float32)).astype(jnp.bfloat16)

    near_out = up(added(own, other, stream[0, :, :half]))

    carry = stage((0,), False, scalars, late_q, [late[0]])
    carry = stage((-1, 1), False, scalars, late_q, [late[-1], late[1]], carry)
    own, other, bad = stage((2,), True, scalars, late_q, [late[2]], carry)
    own, other = guarded(scalars, late_q, late, own, other, bad)
    late_out = added(own, other, late_stream)
    return jnp.concatenate([near_out, late_out], 1)[None]


def solution(mesh):
    return jax.shard_map(
        shards,
        mesh=mesh,
        in_specs=(
            P("section", "seq", None),
            P("section", "seq", None),
            P("section", None, "seq", None),
            P("section", None, "seq", None),
            P(),
            P(),
            P(),
        ),
        out_specs=P("section", "seq", None),
        check_vma=False,
    )
```

time: 315 us -> 307 us (0.975)
  Pallas kernels: 0 us -> 54.1 us
  waiting for transfers between devices: 79.8 us -> 35.4 us
  matrix products: 115 us -> 78.1 us
  starting transfers between devices: 1.32 us -> 25 us
  between operations: 14.1 us -> 2.4 us
  local copies, waits for them, and re-layouts: 40 us -> 48.8 us
  loops' own time: 11.2 us -> 3.87 us
    all_gather x2 -> x0, waiting for transfers between devices: 55.2 us -> none  [the longest x1 55.2 us: shards(): lax.all_gather(cache_kv, 'seq', axis=2, tiled=True)]
    pallas_call x0 -> x4, Pallas kernels: none -> 54.1 us  [stage(): pl.pallas_call(functools.partial(stage_kernel, tuple(rows_of), carry is n...]
    dot_general x32, matrix products: 115 us -> 78.1 us  [the longest x16 45.2 us: slow(): jnp.einsum('tgd,nd->gtn', rows, k, preferred_element_type=jnp.float32)]
    ppermute x1 -> x24, starting transfers between devices: 1.27 us -> 25 us  [moved(): return lax.ppermute(value, AXES, pairs)]
    slice x16 -> x7, local copies, waits for them, and re-layouts: 20.5 us -> 1.65 us  [the longest x1 0.95 us: pair_of(): cache = lax.dynamic_slice_in_dim(cache_kv[0, :, :LIVE], head * DIM, DIM, 2)]
    gather x0 -> x24, local copies, waits for them, and re-layouts: none -> 15.5 us  [the longest x16 10.4 us: slow(): listed = jnp.repeat(table[mine][shard] == 1, TOK)]
    reduce_or x16 -> x0, other arithmetic: 15.3 us -> none  [one_block(): return lax.cond(jnp.any(allowed), compute_block, leave_block, inner_carry)]
    cond x16 -> x114, local copies, waits for them, and re-layouts: 0.05 us -> 13.9 us
  transfers between devices with their start and end apart: 3 -> 24, of which waited for: 2 -> 9; matrix products, arithmetic and copies ran while one was open for 31% -> 56% of each run, Pallas kernels for 0% -> 18%
where the time goes in v1:
time: 307 us; the launch traced here: 302 us
  matrix products  78.1 us (25%)
  other arithmetic  54.4 us (18%)
  Pallas kernels  54.1 us (18%)
  local copies, waits for them, and re-layouts  48.8 us (16%)
  waiting for transfers between devices  35.4 us (12%)
  starting transfers between devices  25 us (8%)
  loops' own time  3.87 us (1%)
    pallas_call x4, Pallas kernels, stage(): pl.pallas_call(functools.partial(stage_kernel, tuple(rows_of), carry is n...  54.1 us
    dot_general x16, matrix products, slow(): jnp.einsum('tgd,nd->gtn', rows, k, preferred_element_type=jnp.float32)  45.2 us
    ppermute x24, waiting for transfers between devices, moved(): return lax.ppermute(value, AXES, pairs)  35.4 us
    dot_general x16, matrix products, slow(): jnp.einsum('gtn,nd->gtd', weights.astype(jnp.bfloat16), v, preferred_elem...  32.9 us
    reduce_sum x16, other arithmetic, slow(): total = total * factor + jnp.sum(weights, -1)  30.1 us
    ppermute x24, starting transfers between devices, moved(): return lax.ppermute(value, AXES, pairs)  25 us
    concatenate x8, other arithmetic, slow(): jnp.concatenate([span_open, jnp.broadcast_to(live.reshape(1, -1), (TOK, C...  11.6 us
    gather x16, local copies, waits for them, and re-layouts, slow(): listed = jnp.repeat(table[mine][shard] == 1, TOK)  10.4 us
  transfers between devices with their start and end apart: 24, of which 9 were waited for; matrix products, arithmetic and copies ran while one was open for 56% of the time, Pallas kernels for 18%

profile of v1, /device:TPU:103, one launch (start us, length us, event | category | flops | bytes accessed | tf_op | source)
XLA Modules:
  0.0 302.1 jit_solution(892058855247399170)
XLA Ops:
  15.4 3.3 %collective-permute-done.2 = bf16[2,416,128]{2,1,0:T(8,128)(2,1)S(1)} collective-permute-done((bf16[2,416,128]{2,1,0:T(8,128)(2,1)S(1)}, bf16[2,416,128]{2,1,0:T(8,128)(2,1)S(1)}, u32[]{:S(2)}, u32[]{:S(2)}) %collective-permute-start.2) | collective-permute-done | bytes 213024 | tf_op jit(solution)/shard_map/ppermute | solution.py:42
  22.6 2.6 collective-permute-done.4
  30.4 2.1 collective-permute-start.18
  33.1 3.6 %collective-permute-done.18 = bf16[2,416,128]{2,1,0:T(8,128)(2,1)S(1)} collective-permute-done((bf16[2,416,128]{2,1,0:T(8,128)(2,1)S(1)}, bf16[2,416,128]{2,1,0:T(8,128)(2,1)S(1)}, u32[]{:S(2)}, u32[]{:S(2)}) %collective-permute-start.18) | collective-permute-done | bytes 213024 | tf_op jit(solution)/shard_map/ppermute | solution.py:42
  38.6 8.0 %stage_0.1.refs_10_ = f32[2,1024,256]{2,1,0:T(8,128)S(1)} custom-call(s32[3]{0:T(128)S(1)} %pad_add_fusion.16.refs_0_, s32[32,32]{1,0:T(8,128)S(1)} %copy-done.44, s32[32]{0:T(128)S(1)} %copy-done, s32[1]{0:T(128)S(6)} %copy.324.refs_3_, bf16[128,1024]{1,0:T(8,128)(2,1)S(1)} %collective-permute-done.12.refs_4_, ...), custom_call_target="tpu_custom_call" | custom-call | flops 2617245696 | bytes 851968 | tf_op jit(solution)/shard_map/stage_0/pallas_call | solution.py:230
  50.1 8.8 %collective-permute-done.19 = bf16[2,1664,128]{2,1,0:T(8,128)(2,1)S(1)} collective-permute-done((bf16[2,1664,128]{2,1,0:T(8,128)(2,1)S(1)}, bf16[2,1664,128]{2,1,0:T(8,128)(2,1)S(1)}, u32[]{:S(2)}, u32[]{:S(2)}) %collective-permute-start.19) | collective-permute-done | bytes 852000 | tf_op jit(solution)/shard_map/ppermute | solution.py:42
  60.3 2.3 collective-permute-start.20
  63.8 3.3 %collective-permute-done.8.refs_13_ = bf16[1664,128]{1,0:T(8,128)(2,1)S(1)} collective-permute-done((bf16[1664,128]{1,0:T(8,128)(2,1)S(1)}, bf16[1664,128]{1,0:T(8,128)(2,1)S(1)}, u32[]{:S(2)}, u32[]{:S(2)}) %collective-permute-start.8) | collective-permute-done | bytes 426016 | tf_op jit(solution)/shard_map/ppermute | solution.py:42
  67.2 25.3 %stage_0_3_1_2.1 = (bf16[128,1024]{1,0:T(8,128)(2,1)}, bf16[128,1024]{1,0:T(8,128)(2,1)}, s32[1]{0:T(128)}) custom-call(s32[3]{0:T(128)S(1)} %pad_add_fusion.16.refs_0_, s32[32,32]{1,0:T(8,128)S(1)} %copy-done.44, s32[32]{0:T(128)S(1)} %copy-done, s32[1]{0:T(128)S(6)} %copy.324.refs_3_, bf16[128,1024]{1,0:T(8,128)(2,1)S(1)} %get-tuple-element.380.refs_4_, ...), custom_call_target="tpu_custom_call" | custom-call | flops 10468982784 | bytes 3407872 | tf_op jit(solution)/shard_map/stage_0_3_1_2/pallas_call | solution.py:230
  93.1 88.0 %conditional.2 = (bf16[128,1024]{1,0:T(8,128)(2,1)}, bf16[128,1024]{1,0:T(8,128)(2,1)}) conditional(s32[]{:T(128)} %bitcast.266, (s32[]{:T(128)}, s32[]{:T(128)}, s32[]{:T(128)}, s32[32,32]{1,0:T(8,128)S(1)}, s32[32]{0:T(128)S(1)}, /*index=5*/s32[1]{0:T(128)}, bf16[128,1024]{1,0:T(8,128)(2,1)S(1)}, bf16[1664,128]{1,0:T(8,128)(2,1)S(1)}, ...), branch_computations={%region_0.17_spmd, %region_17.18_spmd} | conditional | flops 7162764288 | bytes 291097472 | solution.py:291
  106.4 4.4 %compare_and_fusion.3 = (pred[128,1024]{0,1:T(8,128)(4,1)S(1)}, pred[128,1024]{0,1:T(8,128)(4,1)}, pred[128,1024]{0,1:T(8,128)(4,1)}, pred[128,1024]{0,1:T(8,128...) fusion(s32[128]{0:T(128)S(1)} %get-tuple-element.317, ...), kind=kLoop, calls=%fused_computation.117 | loop fusion | flops 2097152 | bytes 1074176 | tf_op jit(solution)/shard_map/cond/branch_0_fun/and | solution.py:268
  114.3 4.8 %fusion.6 = (f32[8,128]{1,0:T(8,128)S(1)}, f32[1664,128,8]{1,0,2:T(8,128)}) fusion(pred[128,1664]{0,1:T(8,128)(4,1)S(1)} %get-tuple-element.281, bf16[1664,128]{1,0:T(8,128)(2,1)} %copy-done.9, bf16[128,1024]{1,0:T(8,128)(2,1)S(1)} %get-tuple-element.92), kind=kOutput, calls=%fused_computation.46 | convolution fusion | flops 441318400 | bytes 7720960 | tf_op jit(solution)/shard_map/cond/branch_0_fun/tgd,nd->gtn/dot_general | solution.py:274
  122.6 4.9 %fusion.7 = (f32[8,128]{1,0:T(8,128)S(1)}, f32[1664,128,8]{1,0,2:T(8,128)}) fusion(pred[128,1664]{0,1:T(8,128)(4,1)S(1)} %get-tuple-element.283, bf16[1664,128]{1,0:T(8,128)(2,1)} %copy-done.28, bf16[128,1024]{1,0:T(8,128)(2,1)S(1)} %get-tuple-element.92), kind=kOutput, calls=%fused_computation.47 | convolution fusion | flops 441318400 | bytes 7720960 | tf_op jit(solution)/shard_map/cond/branch_0_fun/tgd,nd->gtn/dot_general | solution.py:274
  130.9 4.8 %fusion.5 = (f32[8,128]{1,0:T(8,128)S(1)}, f32[1664,128,8]{1,0,2:T(8,128)}) fusion(pred[128,1664]{0,1:T(8,128)(4,1)S(1)} %get-tuple-element.279, bf16[1664,128]{1,0:T(8,128)(2,1)} %copy-done.7, bf16[128,1024]{1,0:T(8,128)(2,1)S(1)} %get-tuple-element.92), kind=kOutput, calls=%fused_computation.45 | convolution fusion | flops 441318400 | bytes 7720960 | tf_op jit(solution)/shard_map/cond/branch_0_fun/tgd,nd->gtn/dot_general | solution.py:274
  138.6 2.2 fusion.4
  142.6 5.0 %fusion.22 = f32[8,128]{1,0:T(8,128)S(1)} fusion(f32[1664,128,8]{1,0,2:T(8,128)} %get-tuple-element.308, f32[8,128]{1,0:T(8,128)S(1)} %get-tuple-element.262, pred[128,1664]{0,1:T(8,128)(4,1)S(1)} %copy-done.21), kind=kLoop, calls=%fused_computation.62 | loop fusion | flops 8518656 | bytes 7036928 | tf_op jit(solution)/shard_map/cond/branch_0_fun/reduce_sum | solution.py:280
  156.4 2.4 fusion.123
  181.1 5.2 %collective-permute-start.9 = (bf16[128,1024]{1,0:T(8,128)(2,1)}, bf16[128,1024]{1,0:T(8,128)(2,1)}, u32[]{:S(2)}, u32[]{:S(2)}) collective-permute-start(bf16[128,1024]{1,0:T(8,128)(2,1)} %get-tuple-element.238), channel_id=1, source_target_pairs={{0,1},{1,0},{2,3},{3,2},{4,5},{5,4},{6,7},{7,6},{8,9},{9,8},{10,11... | collective-permute-start | bytes 786440 | tf_op jit(solution)/shard_map/ppermute | solution.py:42
  186.3 12.5 %stage_3_1.1.refs_8_ = f32[2,1024,256]{2,1,0:T(8,128)S(1)} custom-call(s32[3]{0:T(128)S(1)} %pad_add_fusion.16.refs_0_, s32[32,32]{1,0:T(8,128)S(1)} %copy-done.44, s32[32]{0:T(128)S(1)} %copy-done, s32[1]{0:T(128)S(6)} %copy.324.refs_3_, bf16[128,1024]{1,0:T(8,128)(2,1)S(1)} %collective-permute-done.12.refs_4_, ...), custom_call_target="tpu_custom_call" | custom-call | flops 5234491392 | bytes 1703936 | tf_op jit(solution)/shard_map/stage_3_1/pallas_call | solution.py:230
  198.8 8.3 %stage_2.1 = (bf16[128,1024]{1,0:T(8,128)(2,1)}, bf16[128,1024]{1,0:T(8,128)(2,1)}, s32[1]{0:T(128)}) custom-call(s32[3]{0:T(128)S(1)} %pad_add_fusion.16.refs_0_, s32[32,32]{1,0:T(8,128)S(1)} %copy-done.44, s32[32]{0:T(128)S(1)} %copy-done, s32[1]{0:T(128)S(6)} %copy.324.refs_3_, bf16[128,1024]{1,0:T(8,128)(2,1)S(1)} %collective-permute-done.12.refs_4_, ...), custom_call_target="tpu_custom_call" | custom-call | flops 2617245696 | bytes 851968 | tf_op jit(solution)/shard_map/stage_2/pallas_call | solution.py:230
  207.8 77.0 %conditional.3 = (bf16[128,1024]{1,0:T(8,128)(2,1)}, bf16[128,1024]{1,0:T(8,128)(2,1)S(1)}) conditional(s32[]{:T(128)} %bitcast.280, (s32[]{:T(128)}, s32[]{:T(128)}, s32[]{:T(128)}, s32[32,32]{1,0:T(8,128)S(1)}, s32[32]{0:T(128)S(1)}, /*index=5*/s32[1]{0:T(128)}, bf16[128,1024]{1,0:T(8,128)(2,1)S(1)}, bf16[1664,128]{1,0:T(8,128)(2,1)}, ...), branch_computations={%region_18.35_spmd, %region_35.36_spmd} | conditional | flops 7162764288 | bytes 268945920 | solution.py:291
  215.2 2.8 compare_and_fusion.11
  219.8 3.8 %fusion.228 = (f32[8,128]{1,0:T(8,128)S(1)}, f32[1664,128,8]{1,0,2:T(8,128)}) fusion(pred[128,1664]{0,1:T(8,128)(4,1)S(1)} %get-tuple-element.341, bf16[1664,128]{1,0:T(8,128)(2,1)S(1)} %get-tuple-element.104, bf16[128,1024]{1,0:T(8,128)(2,1)S(1)} %get-tuple-element.108), kind=kOutput, calls=%fused_computation.314 | convolution fusion | flops 441318400 | bytes 7720960 | tf_op jit(solution)/shard_map/cond/branch_0_fun/tgd,nd->gtn/dot_general | solution.py:274
  226.1 4.9 %fusion.229 = (f32[8,128]{1,0:T(8,128)S(1)}, f32[1664,128,8]{1,0,2:T(8,128)}) fusion(pred[128,1664]{0,1:T(8,128)(4,1)S(1)} %get-tuple-element.343, bf16[1664,128]{1,0:T(8,128)(2,1)} %get-tuple-element.106, bf16[128,1024]{1,0:T(8,128)(2,1)S(1)} %get-tuple-element.108), kind=kOutput, calls=%fused_computation.315 | convolution fusion | flops 441318400 | bytes 7720960 | tf_op jit(solution)/shard_map/cond/branch_0_fun/tgd,nd->gtn/dot_general | solution.py:274
  232.8 4.9 %fusion.227 = (f32[8,128]{1,0:T(8,128)S(1)}, f32[1664,128,8]{1,0,2:T(8,128)}) fusion(pred[128,1664]{0,1:T(8,128)(4,1)S(1)} %get-tuple-element.339, bf16[1664,128]{1,0:T(8,128)(2,1)} %get-tuple-element.102, bf16[128,1024]{1,0:T(8,128)(2,1)S(1)} %get-tuple-element.108), kind=kOutput, calls=%fused_computation.313 | convolution fusion | flops 441318400 | bytes 7720960 | tf_op jit(solution)/shard_map/cond/branch_0_fun/tgd,nd->gtn/dot_general | solution.py:274
  240.6 2.2 fusion.226
  253.4 2.7 fusion.300
  256.1 3.4 %fusion.345 = bf16[128,8,128]{0,2,1:T(8,128)(2,1)} fusion(f32[128,8,128]{0,2,1:T(8,128)S(1)} %fusion.300, f32[1664,128,8]{1,0,2:T(8,128)S(1)} %bitcast.1126, f32[8,128]{1,0:T(8,128)S(1)} %get-tuple-element.322, pred[128,1664]{0,1:T(8,128)(4,1)S(1)} %copy-done.23, bf16[1664,128]{1,0:T(8,128)(2,1)} %get-tuple-element.233, f32[128,8]{0,1:T(8,128)S(1)} %get-tuple-element.249), kind=kOutput, calls=%fused_computation.373 | convolution fusion | flops 445120512 | bytes 8249344 | tf_op jit(solution)/shard_map/cond/branch_0_fun/gtn,nd->gtd/dot_general | solution.py:281
  264.9 2.1 fusion.223
  278.3 2.7 fusion.321
  281.0 2.7 fusion.339
  289.3 11.5 %collective-permute-done.10 = bf16[128,2048]{1,0:T(8,128)(2,1)S(1)} collective-permute-done((bf16[128,2048]{1,0:T(8,128)(2,1)S(1)}, bf16[128,2048]{1,0:T(8,128)(2,1)S(1)}, u32[]{:S(2)}, u32[]{:S(2)}) %collective-permute-start.10) | collective-permute-done | bytes 524320 | tf_op jit(solution)/shard_map/ppermute | solution.py:42
  (385 shorter events, 138.0 us)
Async XLA Ops:
  0.0 38.6 %copy-start = (s32[32]{0:T(128)S(1)}, s32[32]{0:T(128)}, u32[]{:S(2)}) copy-start(s32[32]{0:T(128)} %refs_2_.7) | copy-start | bytes 388
  0.0 38.6 %copy-start.44 = (s32[32,32]{1,0:T(8,128)S(1)}, s32[32,32]{1,0:T(8,128)}, u32[]{:S(2)}) copy-start(s32[32,32]{1,0:T(8,128)} %refs_1_.7) | copy-start | bytes 12292
  2.0 10.7 %collective-permute-start.1 = (bf16[2,208,128]{2,1,0:T(8,128)(2,1)S(1)}, bf16[2,208,128]{2,1,0:T(8,128)(2,1)S(1)}, u32[]{:S(2)}, u32[]{:S(2)}) collective-permute-start(bf16[2,208,128]{2,1,0:T(8,128)(2,1)S(1)} %pad_maximum_fusion.2), channel_id=1, source_target_pairs={{0,1},{1,0},{2,3},{3,2},{4,5},{5,4},{6,7},{7,6},{8,9},{9,8},{10,11... | collective-permute-start | bytes 319496 | tf_op jit(solution)/shard_map/ppermute | solution.py:42
  4.0 59.6 %collective-permute-start = (bf16[128,1024]{1,0:T(8,128)(2,1)S(1)}, bf16[128,1024]{1,0:T(8,128)(2,1)S(1)}, u32[]{:S(2)}, u32[]{:S(2)}) collective-permute-start(bf16[128,1024]{1,0:T(8,128)(2,1)S(1)} %get-tuple-element.379), channel_id=1, source_target_pairs={{0,1},{1,0},{2,3},{3,2},{4,5},{5,4},{6,7},{7,6},{8,9},{9,8},{10,11... | collective-permute-start | bytes 786440 | tf_op jit(solution)/shard_map/ppermute | solution.py:42
  4.1 9.6 %collective-permute-start.14 = (bf16[2,208,128]{2,1,0:T(8,128)(2,1)S(1)}, bf16[2,208,128]{2,1,0:T(8,128)(2,1)S(1)}, u32[]{:S(2)}, u32[]{:S(2)}) collective-permute-start(bf16[2,208,128]{2,1,0:T(8,128)(2,1)S(1)} %pad_maximum_fusion.3), channel_id=1, source_target_pairs={{0,32},{1,33},{2,34},{3,35},{4,36},{5,37},{6,38},{7,39},{8,40},{9,... | collective-permute-start | bytes 319496 | tf_op jit(solution)/shard_map/ppermute | solution.py:42
  5.5 8.3 %collective-permute-start.15 = (bf16[2,208,128]{2,1,0:T(8,128)(2,1)S(1)}, bf16[2,208,128]{2,1,0:T(8,128)(2,1)S(1)}, u32[]{:S(2)}, u32[]{:S(2)}) collective-permute-start(bf16[2,208,128]{2,1,0:T(8,128)(2,1)S(1)} %pad_maximum_fusion.4), channel_id=1, source_target_pairs={{0,33},{1,32},{2,35},{3,34},{4,37},{5,36},{6,39},{7,38},{8,41},{9,... | collective-permute-start | bytes 319496 | tf_op jit(solution)/shard_map/ppermute | solution.py:42
  7.5 29.9 %collective-permute-start.12 = (bf16[128,1024]{1,0:T(8,128)(2,1)S(1)}, bf16[128,1024]{1,0:T(8,128)(2,1)S(1)}, u32[]{:S(2)}, u32[]{:S(2)}) collective-permute-start(bf16[128,1024]{1,0:T(8,128)(2,1)S(1)} %get-tuple-element.382), channel_id=1, source_target_pairs={{0,32},{1,33},{2,34},{3,35},{4,36},{5,37},{6,38},{7,39},{8,40},{9,... | collective-permute-start | bytes 786440 | tf_op jit(solution)/shard_map/ppermute | solution.py:42
  12.6 25.7 %collective-permute-start.13 = (bf16[128,1024]{1,0:T(8,128)(2,1)S(1)}, bf16[128,1024]{1,0:T(8,128)(2,1)S(1)}, u32[]{:S(2)}, u32[]{:S(2)}) collective-permute-start(bf16[128,1024]{1,0:T(8,128)(2,1)S(1)} %get-tuple-element.381), channel_id=1, source_target_pairs={{0,33},{1,32},{2,35},{3,34},{4,37},{5,36},{6,39},{7,38},{8,41},{9,... | collective-permute-start | bytes 786440 | tf_op jit(solution)/shard_map/ppermute | solution.py:42
  13.7 5.1 %collective-permute-start.2 = (bf16[2,416,128]{2,1,0:T(8,128)(2,1)S(1)}, bf16[2,416,128]{2,1,0:T(8,128)(2,1)S(1)}, u32[]{:S(2)}, u32[]{:S(2)}) collective-permute-start(bf16[2,416,128]{2,1,0:T(8,128)(2,1)S(1)} %pad_maximum_fusion), channel_id=1, source_target_pairs={{0,2},{1,9},{2,4},{3,11},{4,6},{5,13},{6,0},{7,15},{8,10},{9,17},{... | collective-permute-start | bytes 638984 | tf_op jit(solution)/shard_map/ppermute | solution.py:42
  13.8 6.3 %collective-permute-start.3 = (bf16[2,416,128]{2,1,0:T(8,128)(2,1)S(1)}, bf16[2,416,128]{2,1,0:T(8,128)(2,1)S(1)}, u32[]{:S(2)}, u32[]{:S(2)}) collective-permute-start(bf16[2,416,128]{2,1,0:T(8,128)(2,1)S(1)} %pad_maximum_fusion), channel_id=1, source_target_pairs={{0,6},{1,25},{2,0},{3,27},{4,2},{5,29},{6,4},{7,31},{8,14},{9,1},{... | collective-permute-start | bytes 638984 | tf_op jit(solution)/shard_map/ppermute | solution.py:42
  18.7 6.5 %collective-permute-start.4 = (bf16[2,416,128]{2,1,0:T(8,128)(2,1)S(1)}, bf16[2,416,128]{2,1,0:T(8,128)(2,1)S(1)}, u32[]{:S(2)}, u32[]{:S(2)}) collective-permute-start(bf16[2,416,128]{2,1,0:T(8,128)(2,1)S(1)} %pad_maximum_fusion), channel_id=1, source_target_pairs={{0,4},{1,17},{2,6},{3,19},{4,0},{5,21},{6,2},{7,23},{8,12},{9,25},... | collective-permute-start | bytes 638984 | tf_op jit(solution)/shard_map/ppermute | solution.py:42
  20.1 10.3 %collective-permute-start.16 = (bf16[2,416,128]{2,1,0:T(8,128)(2,1)S(1)}, bf16[2,416,128]{2,1,0:T(8,128)(2,1)S(1)}, u32[]{:S(2)}, u32[]{:S(2)}) collective-permute-start(bf16[2,416,128]{2,1,0:T(8,128)(2,1)S(1)} %pad_maximum_fusion.1), channel_id=1, source_target_pairs={{0,2},{1,9},{2,4},{3,11},{4,6},{5,13},{6,0},{7,15},{8,10},{9,17},{... | collective-permute-start | bytes 638984 | tf_op jit(solution)/shard_map/ppermute | solution.py:42
  25.2 7.3 %collective-permute-start.17 = (bf16[2,416,128]{2,1,0:T(8,128)(2,1)S(1)}, bf16[2,416,128]{2,1,0:T(8,128)(2,1)S(1)}, u32[]{:S(2)}, u32[]{:S(2)}) collective-permute-start(bf16[2,416,128]{2,1,0:T(8,128)(2,1)S(1)} %pad_maximum_fusion.1), channel_id=1, source_target_pairs={{0,6},{1,25},{2,0},{3,27},{4,2},{5,29},{6,4},{7,31},{8,14},{9,1},{... | collective-permute-start | bytes 638984 | tf_op jit(solution)/shard_map/ppermute | solution.py:42
  30.4 6.3 %collective-permute-start.18 = (bf16[2,416,128]{2,1,0:T(8,128)(2,1)S(1)}, bf16[2,416,128]{2,1,0:T(8,128)(2,1)S(1)}, u32[]{:S(2)}, u32[]{:S(2)}) collective-permute-start(bf16[2,416,128]{2,1,0:T(8,128)(2,1)S(1)} %pad_maximum_fusion.1), channel_id=1, source_target_pairs={{0,4},{1,17},{2,6},{3,19},{4,0},{5,21},{6,2},{7,23},{8,12},{9,25},... | collective-permute-start | bytes 638984 | tf_op jit(solution)/shard_map/ppermute | solution.py:42
  32.6 14.5 %collective-permute-start.5 = (bf16[2,1664,128]{2,1,0:T(8,128)(2,1)}, bf16[2,1664,128]{2,1,0:T(8,128)(2,1)S(1)}, u32[]{:S(2)}, u32[]{:S(2)}) collective-permute-start(bf16[2,1664,128]{2,1,0:T(8,128)(2,1)} %slice_dynamic-update-slice_fusion.9), channel_id=1, source_target_pairs={{0,8},{1,3},{2,10},{3,5},{4,12},{5,7},{6,14},{7,1},{8,16},{9,11},{... | collective-permute-start | bytes 2555912 | tf_op jit(solution)/shard_map/ppermute | solution.py:42
  36.7 13.4 %collective-permute-start.6 = (bf16[2,1664,128]{2,1,0:T(8,128)(2,1)}, bf16[2,1664,128]{2,1,0:T(8,128)(2,1)S(1)}, u32[]{:S(2)}, u32[]{:S(2)}) collective-permute-start(bf16[2,1664,128]{2,1,0:T(8,128)(2,1)} %slice_dynamic-update-slice_fusion.9), channel_id=1, source_target_pairs={{0,24},{1,7},{2,26},{3,1},{4,28},{5,3},{6,30},{7,5},{8,0},{9,15},{... | collective-permute-start | bytes 2555912 | tf_op jit(solution)/shard_map/ppermute | solution.py:42
  37.4 9.7 %copy-start.30 = (bf16[1664,128]{1,0:T(8,128)(2,1)}, bf16[1664,128]{1,0:T(8,128)(2,1)S(1)}, u32[]{:S(2)}) copy-start(bf16[1664,128]{1,0:T(8,128)(2,1)S(1)} %get-tuple-element.389.refs_7_) | copy-start | bytes 1277956
  37.4 22.9 %copy-start.1 = (bf16[1664,128]{1,0:T(8,128)(2,1)}, bf16[1664,128]{1,0:T(8,128)(2,1)S(1)}, u32[]{:S(2)}) copy-start(bf16[1664,128]{1,0:T(8,128)(2,1)S(1)} %get-tuple-element.390.refs_6_) | copy-start | bytes 1277956
  37.4 250.4 %collective-permute-start.11 = (bf16[128,2048]{1,0:T(8,128)(2,1)}, bf16[128,2048]{1,0:T(8,128)(2,1)}, u32[]{:S(2)}, u32[]{:S(2)}) collective-permute-start(bf16[128,2048]{1,0:T(8,128)(2,1)} %slice_bitcast_fusion), channel_id=1, source_target_pairs={{0,32},{1,33},{2,34},{3,35},{4,36},{5,37},{6,38},{7,39},{8,40},{9,... | collective-permute-start | bytes 1572872 | tf_op jit(solution)/shard_map/ppermute | solution.py:42
  38.3 22.0 %collective-permute-start.21 = (bf16[2,1664,128]{2,1,0:T(8,128)(2,1)S(1)}, bf16[2,1664,128]{2,1,0:T(8,128)(2,1)S(1)}, u32[]{:S(2)}, u32[]{:S(2)}) collective-permute-start(bf16[2,1664,128]{2,1,0:T(8,128)(2,1)S(1)} %slice_dynamic-update-slice_fusion.6), channel_id=1, source_target_pairs={{0,24},{1,7},{2,26},{3,1},{4,28},{5,3},{6,30},{7,5},{8,0},{9,15},{... | collective-permute-start | bytes 2555912 | tf_op jit(solution)/shard_map/ppermute | solution.py:42
  47.1 11.8 %collective-permute-start.19 = (bf16[2,1664,128]{2,1,0:T(8,128)(2,1)S(1)}, bf16[2,1664,128]{2,1,0:T(8,128)(2,1)S(1)}, u32[]{:S(2)}, u32[]{:S(2)}) collective-permute-start(bf16[2,1664,128]{2,1,0:T(8,128)(2,1)S(1)} %slice_dynamic-update-slice_fusion.6), channel_id=1, source_target_pairs={{0,8},{1,3},{2,10},{3,5},{4,12},{5,7},{6,14},{7,1},{8,16},{9,11},{... | collective-permute-start | bytes 2555912 | tf_op jit(solution)/shard_map/ppermute | solution.py:42
  50.0 13.8 %collective-permute-start.7 = (bf16[1664,128]{1,0:T(8,128)(2,1)S(1)}, bf16[1664,128]{1,0:T(8,128)(2,1)S(1)}, u32[]{:S(2)}, u32[]{:S(2)}) collective-permute-start(bf16[1664,128]{1,0:T(8,128)(2,1)S(1)} %get-tuple-element.386.refs_8_), channel_id=1, source_target_pairs={{0,8},{1,3},{2,10},{3,5},{4,12},{5,7},{6,14},{7,1},{8,16},{9,11},{... | collective-permute-start | bytes 1277960 | tf_op jit(solution)/shard_map/ppermute | solution.py:42
  58.9 8.3 %collective-permute-start.8 = (bf16[1664,128]{1,0:T(8,128)(2,1)S(1)}, bf16[1664,128]{1,0:T(8,128)(2,1)S(1)}, u32[]{:S(2)}, u32[]{:S(2)}) collective-permute-start(bf16[1664,128]{1,0:T(8,128)(2,1)S(1)} %get-tuple-element.383.refs_11_), channel_id=1, source_target_pairs={{0,24},{1,7},{2,26},{3,1},{4,28},{5,3},{6,30},{7,5},{8,0},{9,15},{... | collective-permute-start | bytes 1277960 | tf_op jit(solution)/shard_map/ppermute | solution.py:42
  60.3 138.5 %collective-permute-start.20 = (bf16[1664,128]{1,0:T(8,128)(2,1)}, bf16[1664,128]{1,0:T(8,128)(2,1)}, u32[]{:S(2)}, u32[]{:S(2)}) collective-permute-start(bf16[1664,128]{1,0:T(8,128)(2,1)} %get-tuple-element.394.refs_6_), channel_id=1, source_target_pairs={{0,8},{1,3},{2,10},{3,5},{4,12},{5,7},{6,14},{7,1},{8,16},{9,11},{... | collective-permute-start | bytes 1277960 | tf_op jit(solution)/shard_map/ppermute | solution.py:42
  63.6 135.2 %collective-permute-start.22 = (bf16[1664,128]{1,0:T(8,128)(2,1)}, bf16[1664,128]{1,0:T(8,128)(2,1)}, u32[]{:S(2)}, u32[]{:S(2)}) collective-permute-start(bf16[1664,128]{1,0:T(8,128)(2,1)} %get-tuple-element.392.refs_9_), channel_id=1, source_target_pairs={{0,24},{1,7},{2,26},{3,1},{4,28},{5,3},{6,30},{7,5},{8,0},{9,15},{... | collective-permute-start | bytes 1277960 | tf_op jit(solution)/shard_map/ppermute | solution.py:42
  140.8 6.7 %slice-start.8 = ((s8[6815744]{0:T(1024)(128)(4,1)}), s8[4194304]{0:T(1024)(128)(4,1)S(1)}, s32[]{:S(2)}) async-start(s8[6815744]{0:T(1024)(128)(4,1)} %bitcast.1127), calls=%async_computation.8 | async-start | bytes 8388608 | tf_op jit(solution)/shard_map/cond
  181.1 103.8 %collective-permute-start.9 = (bf16[128,1024]{1,0:T(8,128)(2,1)}, bf16[128,1024]{1,0:T(8,128)(2,1)}, u32[]{:S(2)}, u32[]{:S(2)}) collective-permute-start(bf16[128,1024]{1,0:T(8,128)(2,1)} %get-tuple-element.238), channel_id=1, source_target_pairs={{0,1},{1,0},{2,3},{3,2},{4,5},{5,4},{6,7},{7,6},{8,9},{9,8},{10,11... | collective-permute-start | bytes 786440 | tf_op jit(solution)/shard_map/ppermute | solution.py:42
  198.8 8.9 %copy-start.3 = (bf16[1664,128]{1,0:T(8,128)(2,1)S(1)}, bf16[1664,128]{1,0:T(8,128)(2,1)}, u32[]{:S(2)}) copy-start(bf16[1664,128]{1,0:T(8,128)(2,1)} %get-tuple-element.391.refs_8_) | copy-start | bytes 1277956
  207.8 15.8 %copy-start.4 = (bf16[1664,128]{1,0:T(8,128)(2,1)}, bf16[1664,128]{1,0:T(8,128)(2,1)S(1)}, u32[]{:S(2)}) copy-start(bf16[1664,128]{1,0:T(8,128)(2,1)S(1)} %get-tuple-element.104) | copy-start | bytes 1277956 | tf_op jit(solution)/shard_map/cond
  237.7 6.9 %slice-start.6 = ((s8[6815744]{0:T(1024)(128)(4,1)}), s8[2621440]{0:T(1024)(128)(4,1)S(1)}, s32[]{:S(2)}) async-start(s8[6815744]{0:T(1024)(128)(4,1)} %bitcast.1125), calls=%async_computation.6 | async-start | bytes 5242880 | tf_op jit(solution)/shard_map/cond
  284.8 3.1 %collective-permute-start.23 = (bf16[128,1024]{1,0:T(8,128)(2,1)S(1)}, bf16[128,1024]{1,0:T(8,128)(2,1)S(1)}, u32[]{:S(2)}, u32[]{:S(2)}) collective-permute-start(bf16[128,1024]{1,0:T(8,128)(2,1)S(1)} %get-tuple-element.240), channel_id=1, source_target_pairs={{0,1},{1,0},{2,3},{3,2},{4,5},{5,4},{6,7},{7,6},{8,9},{9,8},{10,11... | collective-permute-start | bytes 786440 | tf_op jit(solution)/shard_map/ppermute | solution.py:42
  286.5 14.3 %collective-permute-start.10 = (bf16[128,2048]{1,0:T(8,128)(2,1)S(1)}, bf16[128,2048]{1,0:T(8,128)(2,1)S(1)}, u32[]{:S(2)}, u32[]{:S(2)}) collective-permute-start(bf16[128,2048]{1,0:T(8,128)(2,1)S(1)} %fusion.444), channel_id=1, source_target_pairs={{0,32},{1,33},{2,34},{3,35},{4,36},{5,37},{6,38},{7,39},{8,40},{9,... | collective-permute-start | bytes 1572872 | tf_op jit(solution)/shard_map/ppermute | solution.py:42
  (52 other events, 124.3 us)

commit v2 on v1

v2 whole, which is shorter than its diff:
```python
import functools
import math

import jax
import jax.numpy as jnp
from jax import lax
from jax.experimental import pallas as pl
from jax.experimental.pallas import tpu as pltpu
from jax.sharding import PartitionSpec as P

DIM = 128
GROUP = 8
TOK = 128
SLOTS = 128
LIVE = 80
SHARDS = 32
CACHE = SLOTS * SHARDS
ROWS = GROUP * TOK
PER = 4
SPAN_ROWS = PER * 2 * TOK
CACHE_ROWS = PER * 2 * LIVE
CHUNK = SPAN_ROWS + CACHE_ROWS
BLOCK = 128
TILE_BLOCKS = 8
SUB = 256
OFFSETS = (0, -1, 1, 2)
TO_LOG2 = math.log2(math.e) / math.sqrt(DIM)
LEAST_TOTAL, MOST_TOTAL = 1e-12, 1e30
LEAST_MIXED, MOST_MIXED = 1e-20, 1e37
AXES = ("section", "seq")


def moved(value, rule):
    pairs = []
    for y in range(4):
        for z in range(4):
            for x in range(4):
                for c in range(2):
                    ty, tz, tx, tc = rule(y, z, x, c)
                    source = y * 32 + (z * 4 + x) * 2 + c
                    target = (ty % 4) * 32 + ((tz % 4) * 4 + tx % 4) * 2 + tc
                    pairs.append((source, target))
    return lax.ppermute(value, AXES, pairs)


def swapped(value):
    return moved(value, lambda y, z, x, c: (y, z, x, 1 - c))


def up(value):
    return moved(value, lambda y, z, x, c: (y + 1, z, x, c))


def up_swapped(value):
    return moved(value, lambda y, z, x, c: (y + 1, z, x, 1 - c))


def first_ring(value, k):
    return moved(value, lambda y, z, x, c: (y, z, x + k, c) if c == 0 else (y, z + k, x, c))


def second_ring(value, k):
    return moved(value, lambda y, z, x, c: (y, z + k, x, c) if c == 0 else (y, z, x + k, c))


def chip_of(place, row, col):
    z, x, c = place
    dz = jnp.where(c == 0, row, col)
    dx = jnp.where(c == 0, col, row)
    return ((z + dz + 4) % 4) * 4 + (x + dx + 4) % 4


def stage_kernel(rows_of, pieces, has_carry, last, idle, *refs):
    refs = list(refs)
    place_ref, table_ref, len_ref, start_ref = refs[:4]
    q_refs, refs = refs[4:6], refs[6:]
    chunk_refs = []
    for part in pieces:
        chunk_refs.append(refs[: len(part)])
        refs = refs[len(part) :]
    carry_ref = None
    if has_carry:
        carry_ref, refs = refs[0], refs[1:]
    all_refs = []
    if last:
        for part in last:
            all_refs.append(refs[: len(part)])
            refs = refs[len(part) :]
    refs = refs[idle:]
    if last:
        out_refs, refs = refs[:2], refs[2:]
    total_ref, keys, values, queries, todo = refs[:5]
    count = len(rows_of)
    place = (place_ref[0], place_ref[1], place_ref[2])
    core = place[2]
    chip = place[0] * 4 + place[1]
    first_open = CACHE - start_ref[0]

    def shard_at(row, k, e):
        return 2 * chip_of(place, row, OFFSETS[k]) + (core if e == 0 else 1 - core)

    for n in range(count):
        base = n * CHUNK
        values[base : base + SPAN_ROWS, DIM:] = jnp.ones((SPAN_ROWS, DIM), jnp.bfloat16)
        k = 0
        for ref, units in zip(chunk_refs[n], pieces[n]):
            for u in range(units):
                for e in range(2):
                    spot = base + (2 * k + e) * TOK
                    keys[spot : spot + TOK, :] = ref[u, e, 0, :TOK, :]
                    values[spot : spot + TOK, :DIM] = ref[u, e, 1, :TOK, :]
                    shard = shard_at(rows_of[n], k, e)
                    low = first_open - shard * SLOTS
                    slot = lax.broadcasted_iota(jnp.int32, (LIVE, DIM), 0)
                    live = (slot >= low) & (slot < len_ref[shard])
                    spot = base + SPAN_ROWS + (2 * k + e) * LIVE
                    keys[spot : spot + LIVE, :] = ref[u, e, 0, TOK:, :]
                    piece = ref[u, e, 1, TOK:, :].astype(jnp.float32)
                    values[spot : spot + LIVE, :DIM] = jnp.where(live, piece, 0.0).astype(jnp.bfloat16)
                    values[spot : spot + LIVE, DIM:] = jnp.where(live, 1.0, 0.0).astype(jnp.bfloat16)
                k += 1
    spare = count * CHUNK
    keys[spare : spare + BLOCK, :] = jnp.zeros((BLOCK, DIM), jnp.bfloat16)
    values[spare : spare + BLOCK, :] = jnp.zeros((BLOCK, 2 * DIM), jnp.bfloat16)

    for q in range(2):
        mine = 2 * chip + (core if q == 0 else 1 - core)
        for h in range(GROUP):
            queries[h * TOK : (h + 1) * TOK, :] = q_refs[q][:, h * DIM : (h + 1) * DIM]

        filled = jnp.int32(0)
        for n in range(count):
            seen = []
            for k in range(PER):
                for e in range(2):
                    shard = shard_at(rows_of[n], k, e)
                    wanted = (shard < mine) & (table_ref[mine, shard] == 1)
                    todo[filled] = n * CHUNK + (2 * k + e) * TOK
                    filled = filled + jnp.where(wanted, 1, 0)
                    seen.append(shard * SLOTS + len_ref[shard] > first_open)
            for b in range(CACHE_ROWS // BLOCK):
                wanted = functools.reduce(
                    jnp.logical_or, seen[b * BLOCK // LIVE : ((b + 1) * BLOCK - 1) // LIVE + 1]
                )
                todo[filled] = n * CHUNK + SPAN_ROWS + b * BLOCK
                filled = filled + jnp.where(wanted, 1, 0)
        for b in range(TILE_BLOCKS - 1):
            todo[filled + b] = spare

        def scores_of(first, rows):
            return lax.dot_general(
                queries[first : first + SUB, :], rows, (((1,), (1,)), ((), ())),
                preferred_element_type=jnp.float32,
            )

        def mix(weights, rows):
            return jnp.dot(weights.astype(jnp.bfloat16), rows, preferred_element_type=jnp.float32)

        if rows_of[0] == 0:
            at = q * TOK
            token = lax.broadcasted_iota(jnp.int32, (TOK, TOK), 0)
            key = lax.broadcasted_iota(jnp.int32, (TOK, TOK), 1)
            behind = (key <= token)[None]
            for first in range(0, ROWS, SUB):
                weights = jnp.exp2(scores_of(first, keys[at : at + TOK, :]) * TO_LOG2)
                weights = jnp.where(behind, weights.reshape(SUB // TOK, TOK, TOK), 0.0).reshape(SUB, TOK)
                part = mix(weights, values[at : at + TOK, :])
                if has_carry:
                    part = part + carry_ref[q, first : first + SUB, :]
                total_ref[q, first : first + SUB, :] = part
        else:
            total_ref[q] = carry_ref[q]

        def tile(blocks, begin):
            spots = [pl.multiple_of(todo[begin + b], BLOCK) for b in range(blocks)]
            key_rows = jnp.concatenate([keys[pl.ds(s, BLOCK), :] for s in spots], 0)
            value_rows = jnp.concatenate([values[pl.ds(s, BLOCK), :] for s in spots], 0)

            def finish(first, scores):
                weights = jnp.exp2(scores * TO_LOG2)
                total_ref[q, first : first + SUB, :] += mix(weights, value_rows)

            held = None
            for first in range(0, ROWS, SUB):
                scores = scores_of(first, key_rows)
                if held is not None:
                    finish(*held)
                held = (first, scores)
            finish(*held)

        whole = (filled + 3) // TILE_BLOCKS
        rest = filled - whole * TILE_BLOCKS

        def whole_tile(step, _):
            tile(TILE_BLOCKS, step * TILE_BLOCKS)
            return 0

        lax.fori_loop(0, whole, whole_tile, 0)

        @pl.when(rest > 2)
        def _():
            tile(4, whole * TILE_BLOCKS)

        @pl.when((rest > 0) & (rest <= 2))
        def _():
            tile(2, whole * TILE_BLOCKS)

        if last:
            held, top = refs[5:]

            def write_out():
                for h in range(GROUP):
                    mixed = total_ref[q, h * TOK : (h + 1) * TOK, :DIM]
                    total = total_ref[q, h * TOK : (h + 1) * TOK, DIM:]
                    out_refs[q][:, h * DIM : (h + 1) * DIM] = (mixed / total).astype(jnp.bfloat16)

            write_out()
            strange = jnp.zeros((TOK, DIM), jnp.float32)
            largest = jnp.zeros((TOK, DIM), jnp.float32)
            for h in range(GROUP):
                mixed = jnp.abs(total_ref[q, h * TOK : (h + 1) * TOK, :DIM])
                total = total_ref[q, h * TOK : (h + 1) * TOK, DIM:]
                good = (total >= LEAST_TOTAL) & (total <= MOST_TOTAL) & (mixed <= MOST_MIXED)
                strange = jnp.where(good, strange, 1.0)
                largest = jnp.maximum(largest, mixed)
            strange = jnp.where(jnp.max(largest) >= LEAST_MIXED, jnp.max(strange), 1.0)

            @pl.when(strange > 0.0)
            def _():
                careful(q, mine, place, first_open, table_ref, len_ref, last, all_refs,
                        queries, total_ref, held, top)
                write_out()


def careful(q, mine, place, first_open, table_ref, len_ref, parts, all_refs, queries, total_ref, held, top):
    core = place[2]
    total_ref[q] = jnp.zeros((ROWS, 2 * DIM), jnp.float32)
    top[...] = jnp.full((ROWS, DIM), -jnp.inf, jnp.float32)

    def add(keys, values, is_open):
        extent = keys.shape[0]

        def head(h, _):
            rows = pl.ds(pl.multiple_of(h * TOK, TOK), TOK)
            scores = lax.dot_general(
                queries[rows, :], keys, (((1,), (1,)), ((), ())), preferred_element_type=jnp.float32
            ) * (1.0 / math.sqrt(DIM))
            before = top[rows, :]
            highest = jnp.max(jnp.where(is_open, scores, -jnp.inf), -1, keepdims=True)
            after = jnp.maximum(before, highest)
            shift = jnp.where(after == -jnp.inf, 0.0, after)
            factor = jnp.exp(before - shift)
            weights = jnp.exp(jnp.minimum(scores - shift[:, :extent], 0.0))
            weights = jnp.where(is_open, weights, 0.0)
            mixed = jnp.dot(weights.astype(jnp.bfloat16), values, preferred_element_type=jnp.float32)
            total_ref[q, rows, :DIM] = total_ref[q, rows, :DIM] * factor + mixed
            total_ref[q, rows, DIM:] = total_ref[q, rows, DIM:] * factor + jnp.sum(weights, -1, keepdims=True)
            top[rows, :] = after
            return 0

        lax.fori_loop(0, GROUP, head, 0)

    for n, row in enumerate(OFFSETS):
        begin = 0
        for ref, units in zip(all_refs[n], parts[n]):

            def unit(u, _, ref=ref, row=row, begin=begin):
                pltpu.sync_copy(ref.at[u], held)
                k = begin + u
                there = chip_of(place, row, jnp.where(k < 2, -k, k - 1))

                def device(e, _):
                    shard = 2 * there + jnp.where(e == 0, core, 1 - core)
                    token = lax.broadcasted_iota(jnp.int32, (TOK, TOK), 0)
                    key = lax.broadcasted_iota(jnp.int32, (TOK, TOK), 1)
                    listed = table_ref[mine, shard] == 1
                    reach = jnp.where(shard < mine, TOK, jnp.where(shard == mine, 0, -2 * TOK))
                    reach = jnp.where(listed, reach, -2 * TOK)
                    add(held[e, 0, :TOK, :], held[e, 1, :TOK, :], key <= token + reach)
                    slot = lax.broadcasted_iota(jnp.int32, (TOK, LIVE), 1)
                    live = (slot >= first_open - shard * SLOTS) & (slot < len_ref[shard])
                    add(held[e, 0, TOK:, :], held[e, 1, TOK:, :], live)
                    return 0

                return lax.fori_loop(0, 2, device, 0)

            lax.fori_loop(0, units, unit, 0)
            begin += units


def stage(rows_of, last, scalars, queries, chunks, carry=None, after=()):
    smem = pl.BlockSpec(memory_space=pltpu.SMEM)
    vmem = pl.BlockSpec(memory_space=pltpu.VMEM)
    anywhere = pl.BlockSpec(memory_space=pl.ANY)
    operands = list(scalars) + list(queries)
    pieces = []
    for row in rows_of:
        operands += chunks[row]
        pieces.append(tuple(part.shape[0] for part in chunks[row]))
    if carry is not None:
        operands.append(carry)
    specs = [smem] * 4 + [vmem] * (len(operands) - 4)
    every = None
    if last:
        every = []
        for row in OFFSETS:
            operands += chunks[row]
            every.append(tuple(part.shape[0] for part in chunks[row]))
        every = tuple(every)
    operands += list(after)
    specs += [anywhere] * (len(operands) - len(specs))
    count = len(rows_of)
    total = ((2, ROWS, 2 * DIM), jnp.float32)
    scratch = [
        pltpu.VMEM((count * CHUNK + BLOCK, DIM), jnp.bfloat16),
        pltpu.VMEM((count * CHUNK + BLOCK, 2 * DIM), jnp.bfloat16),
        pltpu.VMEM((ROWS, DIM), jnp.bfloat16),
        pltpu.SMEM((count * (PER * 2 + CACHE_ROWS // BLOCK) + TILE_BLOCKS,), jnp.int32),
    ]
    if last:
        out_shape = (jax.ShapeDtypeStruct((TOK, GROUP * DIM), jnp.bfloat16),) * 2
        out_specs = (vmem, vmem)
        scratch = [pltpu.VMEM(*total)] + scratch + [
            pltpu.VMEM((2, 2, TOK + LIVE, DIM), jnp.bfloat16),
            pltpu.VMEM((ROWS, DIM), jnp.float32),
        ]
    else:
        out_shape = jax.ShapeDtypeStruct(*total)
        out_specs = vmem
    return pl.pallas_call(
        functools.partial(stage_kernel, tuple(rows_of), tuple(pieces), carry is not None, every, len(after)),
        out_shape=out_shape,
        in_specs=specs,
        out_specs=out_specs,
        scratch_shapes=scratch,
        compiler_params=pltpu.CompilerParams(vmem_limit_bytes=40 * 1024 * 1024),
        cost_estimate=pl.CostEstimate(
            flops=count * 2 * ROWS * CHUNK * DIM * 6,
            bytes_accessed=count * CHUNK * DIM * 4,
            transcendentals=count * 2 * ROWS * CHUNK,
        ),
        name="stage_" + "_".join(str(r % 4) for r in rows_of),
    )(*operands)


def pairs_kernel(place_ref, span_ref, cache_ref, *outs):
    core = place_ref[2]
    for out, head in zip(outs, (core, 1 - core, 2 + core, 3 - core)):
        columns = pl.ds(pl.multiple_of(head * DIM, DIM), DIM)
        for i in range(2):
            out[i, :TOK, :] = span_ref[i, :, columns]
            out[i, TOK:, :] = cache_ref[i, :LIVE, columns]


def queries_kernel(place_ref, queries_ref, stream_ref, *outs):
    core = place_ref[2]
    width = GROUP * DIM
    for out, head in zip(outs[:4], (core, 1 - core, 2 + core, 3 - core)):
        out[...] = queries_ref[:, pl.ds(pl.multiple_of(head * width, width), width)]
    outs[4][...] = stream_ref[:, 2 * width :]


def split(kernel, place, first, second, shapes, after=()):
    smem = pl.BlockSpec(memory_space=pltpu.SMEM)
    vmem = pl.BlockSpec(memory_space=pltpu.VMEM)
    anywhere = pl.BlockSpec(memory_space=pl.ANY)
    return pl.pallas_call(
        lambda place_ref, a, b, *rest: kernel(place_ref, a, b, *rest[len(after) :]),
        out_shape=tuple(jax.ShapeDtypeStruct(shape, jnp.bfloat16) for shape in shapes),
        in_specs=[smem, vmem, vmem] + [anywhere] * len(after),
        out_specs=(vmem,) * len(shapes),
        name=kernel.__name__,
    )(place, first, second, *after)


def spread(unit):
    return jnp.stack([unit] + [first_ring(unit, -k) for k in OFFSETS[1:]])


def shards(stream, queries, span_kv, cache_kv, cache_len, context_start, block_table):
    seq = lax.axis_index("seq")
    core = seq % 2
    place = jnp.stack([seq // 8, (seq // 2) % 4, core]).astype(jnp.int32)
    scalars = (place, block_table, cache_len, context_start)
    width = GROUP * DIM

    mine, theirs, late_same, late_cross = split(
        pairs_kernel, place, span_kv[0], cache_kv[0], [(2, TOK + LIVE, DIM)] * 4
    )
    near_unit = jnp.stack([mine, swapped(theirs)])
    late_unit = jnp.stack([up(late_same), up_swapped(late_cross)])
    q_mine, q_theirs, q_same, q_cross, stream_late = split(
        queries_kernel, place, queries[0], stream[0], [(TOK, width)] * 4 + [(TOK, 2 * width)]
    )
    near_q = (q_mine, swapped(q_theirs))
    late_q = (up(q_same), up_swapped(q_cross))
    late_stream = up(stream_late)

    near_row = spread(near_unit)
    near = {0: [near_row], -1: [second_ring(near_row, 1)], 1: [second_ring(near_row, -1)]}
    late_row = spread(late_unit)
    near_sum = stage((0,), False, scalars, near_q, near, after=[late_unit])
    near[2] = [second_ring(near[-1][0][:2], 1), second_ring(near[1][0][2:], -1)]
    late = {0: [late_row], -1: [second_ring(late_row, 1)], 1: [second_ring(late_row, -1)]}
    near_sum = stage((-1, 1), False, scalars, near_q, near, near_sum, after=[late_row])
    own, other = stage((2,), True, scalars, near_q, near, near_sum)

    def added(own, other, base):
        received = swapped(other)
        both = jnp.where(
            core == 0, jnp.concatenate([own, received], 1), jnp.concatenate([received, own], 1)
        )
        return (base.astype(jnp.float32) + both.astype(jnp.float32)).astype(jnp.bfloat16)

    late_sum = stage((0,), False, scalars, late_q, late, after=[own])
    near_done = added(own, other, stream[0, :, : 2 * width])
    near_out = up(near_done)
    late[2] = [second_ring(late[-1][0][:2], 1), second_ring(late[1][0][2:], -1)]
    late_sum = stage((-1, 1), False, scalars, late_q, late, late_sum, after=[near_done])
    own, other = stage((2,), True, scalars, late_q, late, late_sum, after=[near_out])
    late_out = added(own, other, late_stream)
    return jnp.concatenate([near_out, late_out], 1)[None]


def solution(mesh):
    return jax.shard_map(
        shards,
        mesh=mesh,
        in_specs=(
            P("section", "seq", None),
            P("section", "seq", None),
            P("section", None, "seq", None),
            P("section", None, "seq", None),
            P(),
            P(),
            P(),
        ),
        out_specs=P("section", "seq", None),
        check_vma=False,
    )
```

time: 307 us -> 906 us (2.95)
  Pallas kernels: 54.1 us -> 829 us
  matrix products: 78.1 us -> 0 us
  other arithmetic: 54.4 us -> 4.34 us
  local copies, waits for them, and re-layouts: 48.8 us -> 4.1 us
    pallas_call x4 -> x8, Pallas kernels: 54.1 us -> 829 us  [the longest x6 824 us: stage(): pl.pallas_call(functools.partial(stage_kernel, tuple(rows_of), tuple(piec...]
    dot_general x32 -> x0, matrix products: 78.1 us -> none  [the longest x16 45.2 us: slow(): jnp.einsum('tgd,nd->gtn', rows, k, preferred_element_type=jnp.float32)]
    reduce_sum x16 -> x0, other arithmetic: 30.1 us -> none  [slow(): total = total * factor + jnp.sum(weights, -1)]
    gather x24 -> x0, local copies, waits for them, and re-layouts: 15.5 us -> none  [the longest x16 10.4 us: slow(): listed = jnp.repeat(table[mine][shard] == 1, TOK)]
    cond x114 -> x0, local copies, waits for them, and re-layouts: 13.9 us -> none
    concatenate x13 -> x0, other arithmetic: 11.6 us -> none  [the longest x8 11.6 us: slow(): jnp.concatenate([span_open, jnp.broadcast_to(live.reshape(1, -1), (TOK, C...]
  transfers between devices with their start and end apart: 24 -> 24, of which waited for: 9 -> 10; matrix products, arithmetic and copies ran while one was open for 56% -> 1% of each run, Pallas kernels for 18% -> 92%
where the time goes in v2:
time: 906 us; the launch traced here: 896 us
  Pallas kernels  829 us (92%)
  waiting for transfers between devices  31.1 us (3%)
  starting transfers between devices  26.2 us (3%)
    pallas_call x6, Pallas kernels, stage(): pl.pallas_call(functools.partial(stage_kernel, tuple(rows_of), tuple(piec...  824 us
    ppermute x24, waiting for transfers between devices, moved(): return lax.ppermute(value, AXES, pairs)  31.1 us
    ppermute x24, starting transfers between devices, moved(): return lax.ppermute(value, AXES, pairs)  26.2 us
  transfers between devices with their start and end apart: 24, of which 10 were waited for; matrix products, arithmetic and copies ran while one was open for 1% of the time, Pallas kernels for 92%

profile of v2, /device:TPU:103, one launch (start us, length us, event | category | flops | bytes accessed | tf_op | source)
XLA Modules:
  0.0 896.0 jit_solution(7266308999904941340)
XLA Ops:
  0.6 1.9 pairs_kernel.1
  3.1 1.2 collective-permute-done.1
  5.3 1.5 collective-permute-start.3
  7.2 1.3 collective-permute-start.9
  8.5 3.3 collective-permute-start.10
  11.9 2.0 collective-permute-done.3
  14.3 1.3 collective-permute-start.7
  15.5 1.4 collective-permute-done.10
  17.1 1.5 collective-permute-start.12
  18.5 1.5 collective-permute-start.13
  20.0 2.8 queries_kernel.1
  22.8 1.6 collective-permute-done.11
  24.4 1.6 collective-permute-start
  26.7 3.8 collective-permute-done.13
  33.1 4.7 stage_0.2.refs_8_
  37.8 1.0 slice.20
  41.6 6.5 stage_3_1.2.refs_8_
  48.2 1.3 collective-permute-done.8.refs_7_.refs_13_
  49.5 403.9 %stage_2.2 = (bf16[128,1024]{1,0:T(8,128)(2,1)S(1)}, bf16[128,1024]{1,0:T(8,128)(2,1)}) custom-call(s32[3]{0:T(128)S(1)} %copy-done, s32[32,32]{1,0:T(8,128)S(1)} %copy-done.2, s32[32]{0:T(128)S(1)} %copy-done.3, s32[1]{0:T(128)S(6)} %copy.8.refs_3_, bf16[128,1024]{1,0:T(8,128)(2,1)S(1)} %copy-done.1, bf16[128,1024]{1,0:T(8,128)(2,1)S(1)} %collective-permute-done.refs_5_, ...), custom_call_target="tpu_custom_call" | custom-call | flops 2617245696 | bytes 851968 | tf_op jit(solution)/shard_map/stage_2/pallas_call | solution.py:330
  453.5 3.3 collective-permute-start.14
  456.8 1.3 collective-permute-start.17
  458.1 1.5 collective-permute-start.18
  461.9 1.3 collective-permute-start.22
  463.3 1.3 fusion.refs_9_
  464.6 1.7 collective-permute-done.17.refs_4_
  466.3 6.0 collective-permute-done.18.refs_5_
  472.3 4.7 stage_0.3.refs_8_
  476.9 6.6 stage_3_1.3.refs_8_
  483.5 10.8 %collective-permute-done.15.refs_14_ = bf16[128,2048]{1,0:T(8,128)(2,1)S(1)} collective-permute-done((bf16[128,2048]{1,0:T(8,128)(2,1)S(1)}, bf16[128,2048]{1,0:T(8,128)(2,1)S(1)}, u32[]{:S(2)}, u32[]{:S(2)}) %collective-permute-start.15) | collective-permute-done | bytes 524320 | tf_op jit(solution)/shard_map/ppermute | solution.py:43
  494.4 397.9 %stage_2.3 = (bf16[128,1024]{1,0:T(8,128)(2,1)S(1)}, bf16[128,1024]{1,0:T(8,128)(2,1)S(1)}) custom-call(s32[3]{0:T(128)S(1)} %copy-done, s32[32,32]{1,0:T(8,128)S(1)} %copy-done.2, s32[32]{0:T(128)S(1)} %copy-done.3, s32[1]{0:T(128)S(6)} %copy.8.refs_3_, bf16[128,1024]{1,0:T(8,128)(2,1)S(1)} %collective-permute-done.17.refs_4_, ...), custom_call_target="tpu_custom_call" | custom-call | flops 2617245696 | bytes 851968 | tf_op jit(solution)/shard_map/stage_2/pallas_call | solution.py:330
  893.1 1.2 collective-permute-done.23
  894.5 1.1 maximum_bitcast_fusion
  (46 shorter events, 12.0 us)
Async XLA Ops:
  2.5 1.8 collective-permute-start.1
  5.2 6.6 collective-permute-start.2
  5.3 8.6 collective-permute-start.3
  6.8 7.1 collective-permute-start.4
  7.2 8.3 collective-permute-start.9
  8.5 8.4 collective-permute-start.10
  14.0 23.8 %collective-permute-start.5 = (bf16[4,2,2,208,128]{4,3,2,1,0:T(8,128)(2,1)S(1)}, bf16[4,2,2,208,128]{4,3,2,1,0:T(8,128)(2,1)}, u32[]{:S(2)}, u32[]{:S(2)}) collective-permute-start(bf16[4,2,2,208,128]{4,3,2,1,0:T(8,128)(2,1)S(1)} %pad_maximum_fusion.refs_6_.refs_9_), channel_id=1, source_target_pairs={{0,8},{1,3},{2,10},{3,5},{4,12},{5,7},{6,14},{7,1},{8,16},{9,11},{... | collective-permute-start | bytes 2555912 | tf_op jit(solution)/shard_map/ppermute | solution.py:43
  14.3 25.5 %collective-permute-start.7 = (bf16[4,2,2,208,128]{4,3,2,1,0:T(8,128)(2,1)S(1)}, bf16[4,2,2,208,128]{4,3,2,1,0:T(8,128)(2,1)}, u32[]{:S(2)}, u32[]{:S(2)}) collective-permute-start(bf16[4,2,2,208,128]{4,3,2,1,0:T(8,128)(2,1)S(1)} %pad_maximum_fusion.refs_6_.refs_9_), channel_id=1, source_target_pairs={{0,24},{1,7},{2,26},{3,1},{4,28},{5,3},{6,30},{7,5},{8,0},{9,15},{... | collective-permute-start | bytes 2555912 | tf_op jit(solution)/shard_map/ppermute | solution.py:43
  17.0 15.2 %copy-start = (s32[3]{0:T(128)S(1)}, s32[3]{0:T(128)}, u32[]{:S(2)}) copy-start(s32[3]{0:T(128)} %pad_add_fusion.place_ref.refs_0_) | copy-start | bytes 40
  17.0 15.2 %copy-start.2 = (s32[32,32]{1,0:T(8,128)S(1)}, s32[32,32]{1,0:T(8,128)}, u32[]{:S(2)}) copy-start(s32[32,32]{1,0:T(8,128)} %refs_1_.11) | copy-start | bytes 12292
  17.0 15.2 %copy-start.3 = (s32[32]{0:T(128)S(1)}, s32[32]{0:T(128)}, u32[]{:S(2)}) copy-start(s32[32]{0:T(128)} %refs_2_.11) | copy-start | bytes 388
  17.0 7.4 collective-permute-start.11
  17.1 9.6 %collective-permute-start.12 = (bf16[2,2,208,128]{3,2,1,0:T(8,128)(2,1)S(1)}, bf16[2,2,208,128]{3,2,1,0:T(8,128)(2,1)S(1)}, u32[]{:S(2)}, u32[]{:S(2)}) collective-permute-start(bf16[2,2,208,128]{3,2,1,0:T(8,128)(2,1)S(1)} %get-tuple-element.34.refs_7_), channel_id=1, source_target_pairs={{0,6},{1,25},{2,0},{3,27},{4,2},{5,29},{6,4},{7,31},{8,14},{9,1},{... | collective-permute-start | bytes 638984 | tf_op jit(solution)/shard_map/ppermute | solution.py:43
  18.5 11.9 %collective-permute-start.13 = (bf16[2,2,208,128]{3,2,1,0:T(8,128)(2,1)S(1)}, bf16[2,2,208,128]{3,2,1,0:T(8,128)(2,1)S(1)}, u32[]{:S(2)}, u32[]{:S(2)}) collective-permute-start(bf16[2,2,208,128]{3,2,1,0:T(8,128)(2,1)S(1)} %get-tuple-element.34.refs_7_), channel_id=1, source_target_pairs={{0,4},{1,17},{2,6},{3,19},{4,0},{5,21},{6,2},{7,23},{8,12},{9,25},... | collective-permute-start | bytes 638984 | tf_op jit(solution)/shard_map/ppermute | solution.py:43
  24.4 7.7 collective-permute-start
  30.6 429.0 %collective-permute-start.19 = (bf16[4,2,2,208,128]{4,3,2,1,0:T(8,128)(2,1)S(1)}, bf16[4,2,2,208,128]{4,3,2,1,0:T(8,128)(2,1)S(1)}, u32[]{:S(2)}, u32[]{:S(2)}) collective-permute-start(bf16[4,2,2,208,128]{4,3,2,1,0:T(8,128)(2,1)S(1)} %pad_maximum_fusion.1.refs_9_.refs_6_), channel_id=1, source_target_pairs={{0,8},{1,3},{2,10},{3,5},{4,12},{5,7},{6,14},{7,1},{8,16},{9,11},{... | collective-permute-start | bytes 2555912 | tf_op jit(solution)/shard_map/ppermute | solution.py:43
  31.4 429.2 %collective-permute-start.21 = (bf16[4,2,2,208,128]{4,3,2,1,0:T(8,128)(2,1)S(1)}, bf16[4,2,2,208,128]{4,3,2,1,0:T(8,128)(2,1)}, u32[]{:S(2)}, u32[]{:S(2)}) collective-permute-start(bf16[4,2,2,208,128]{4,3,2,1,0:T(8,128)(2,1)S(1)} %pad_maximum_fusion.1.refs_9_.refs_6_), channel_id=1, source_target_pairs={{0,24},{1,7},{2,26},{3,1},{4,28},{5,3},{6,30},{7,5},{8,0},{9,15},{... | collective-permute-start | bytes 2555912 | tf_op jit(solution)/shard_map/ppermute | solution.py:43
  32.1 1.0 copy-start.1
  38.8 9.4 %collective-permute-start.6 = (bf16[2,2,2,208,128]{4,3,2,1,0:T(8,128)(2,1)S(1)}, bf16[2,2,2,208,128]{4,3,2,1,0:T(8,128)(2,1)S(1)}, u32[]{:S(2)}, u32[]{:S(2)}) collective-permute-start(bf16[2,2,2,208,128]{4,3,2,1,0:T(8,128)(2,1)S(1)} %slice.20), channel_id=1, source_target_pairs={{0,8},{1,3},{2,10},{3,5},{4,12},{5,7},{6,14},{7,1},{8,16},{9,11},{... | collective-permute-start | bytes 1277960 | tf_op jit(solution)/shard_map/ppermute | solution.py:43
  40.8 8.7 collective-permute-start.8
  48.2 411.4 %copy-start.4 = (bf16[128,2048]{1,0:T(8,128)(2,1)S(1)}, bf16[128,2048]{1,0:T(8,128)(2,1)}, u32[]{:S(2)}) copy-start(bf16[128,2048]{1,0:T(8,128)(2,1)} %get-tuple-element.26) | copy-start | bytes 1572868
  453.5 8.4 collective-permute-start.14
  456.8 9.5 %collective-permute-start.17 = (bf16[128,1024]{1,0:T(8,128)(2,1)}, bf16[128,1024]{1,0:T(8,128)(2,1)S(1)}, u32[]{:S(2)}, u32[]{:S(2)}) collective-permute-start(bf16[128,1024]{1,0:T(8,128)(2,1)} %get-tuple-element.27), channel_id=1, source_target_pairs={{0,32},{1,33},{2,34},{3,35},{4,36},{5,37},{6,38},{7,39},{8,40},{9,... | collective-permute-start | bytes 786440 | tf_op jit(solution)/shard_map/ppermute | solution.py:43
  458.1 14.2 %collective-permute-start.18 = (bf16[128,1024]{1,0:T(8,128)(2,1)}, bf16[128,1024]{1,0:T(8,128)(2,1)S(1)}, u32[]{:S(2)}, u32[]{:S(2)}) collective-permute-start(bf16[128,1024]{1,0:T(8,128)(2,1)} %get-tuple-element.28), channel_id=1, source_target_pairs={{0,33},{1,32},{2,35},{3,34},{4,37},{5,36},{6,39},{7,38},{8,41},{9,... | collective-permute-start | bytes 786440 | tf_op jit(solution)/shard_map/ppermute | solution.py:43
  459.6 433.5 %collective-permute-start.16 = (bf16[128,2048]{1,0:T(8,128)(2,1)S(1)}, bf16[128,2048]{1,0:T(8,128)(2,1)S(1)}, u32[]{:S(2)}, u32[]{:S(2)}) collective-permute-start(bf16[128,2048]{1,0:T(8,128)(2,1)S(1)} %copy-done.4), channel_id=1, source_target_pairs={{0,32},{1,33},{2,34},{3,35},{4,36},{5,37},{6,38},{7,39},{8,40},{9,... | collective-permute-start | bytes 1572872 | tf_op jit(solution)/shard_map/ppermute | solution.py:43
  460.6 22.9 %collective-permute-start.20 = (bf16[2,2,2,208,128]{4,3,2,1,0:T(8,128)(2,1)S(1)}, bf16[2,2,2,208,128]{4,3,2,1,0:T(8,128)(2,1)S(1)}, u32[]{:S(2)}, u32[]{:S(2)}) collective-permute-start(bf16[2,2,2,208,128]{4,3,2,1,0:T(8,128)(2,1)S(1)} %slice.22), channel_id=1, source_target_pairs={{0,8},{1,3},{2,10},{3,5},{4,12},{5,7},{6,14},{7,1},{8,16},{9,11},{... | collective-permute-start | bytes 1277960 | tf_op jit(solution)/shard_map/ppermute | solution.py:43
  461.9 21.6 %collective-permute-start.22 = (bf16[2,2,2,208,128]{4,3,2,1,0:T(8,128)(2,1)S(1)}, bf16[2,2,2,208,128]{4,3,2,1,0:T(8,128)(2,1)S(1)}, u32[]{:S(2)}, u32[]{:S(2)}) collective-permute-start(bf16[2,2,2,208,128]{4,3,2,1,0:T(8,128)(2,1)S(1)} %slice.23), channel_id=1, source_target_pairs={{0,24},{1,7},{2,26},{3,1},{4,28},{5,3},{6,30},{7,5},{8,0},{9,15},{... | collective-permute-start | bytes 1277960 | tf_op jit(solution)/shard_map/ppermute | solution.py:43
  466.3 28.1 %collective-permute-start.15 = (bf16[128,2048]{1,0:T(8,128)(2,1)S(1)}, bf16[128,2048]{1,0:T(8,128)(2,1)S(1)}, u32[]{:S(2)}, u32[]{:S(2)}) collective-permute-start(bf16[128,2048]{1,0:T(8,128)(2,1)S(1)} %fusion.refs_9_), channel_id=1, source_target_pairs={{0,32},{1,33},{2,34},{3,35},{4,36},{5,37},{6,38},{7,39},{8,40},{9,... | collective-permute-start | bytes 1572872 | tf_op jit(solution)/shard_map/ppermute | solution.py:43
  892.3 2.0 collective-permute-start.23

commit v3 on v2

--- a/solution.py
+++ b/solution.py
@@ -19,6 +19,7 @@
 PER = 4
 SPAN_ROWS = PER * 2 * TOK
 CACHE_ROWS = PER * 2 * LIVE
+PAIR = 2 * (TOK + LIVE)
 CHUNK = SPAN_ROWS + CACHE_ROWS
 BLOCK = 128
 TILE_BLOCKS = 8
@@ -63,6 +64,11 @@
     return moved(value, lambda y, z, x, c: (y, z + k, x, c) if c == 0 else (y, z, x + k, c))
 
 
+def own_place():
+    seq = lax.axis_index("seq")
+    return seq >> 3, (seq >> 1) & 3, seq & 1
+
+
 def chip_of(place, row, col):
     z, x, c = place
     dz = jnp.where(c == 0, row, col)
@@ -70,10 +76,10 @@
     return ((z + dz + 4) % 4) * 4 + (x + dx + 4) % 4
 
 
-def stage_kernel(rows_of, pieces, has_carry, last, idle, *refs):
+def stage_kernel(rows_of, pieces, has_carry, last, *refs):
     refs = list(refs)
-    place_ref, table_ref, len_ref, start_ref = refs[:4]
-    q_refs, refs = refs[4:6], refs[6:]
+    table_ref, len_ref, start_ref = refs[:3]
+    q_refs, refs = refs[3:5], refs[5:]
     chunk_refs = []
     for part in pieces:
         chunk_refs.append(refs[: len(part)])
@@ -86,12 +92,11 @@
         for part in last:
             all_refs.append(refs[: len(part)])
             refs = refs[len(part) :]
-    refs = refs[idle:]
     if last:
         out_refs, refs = refs[:2], refs[2:]
-    total_ref, keys, values, queries, todo = refs[:5]
+    total_ref, keys, values, todo = refs[:4]
     count = len(rows_of)
-    place = (place_ref[0], place_ref[1], place_ref[2])
+    place = own_place()
     core = place[2]
     chip = place[0] * 4 + place[1]
     first_open = CACHE - start_ref[0]
@@ -102,31 +107,29 @@
     for n in range(count):
         base = n * CHUNK
         values[base : base + SPAN_ROWS, DIM:] = jnp.ones((SPAN_ROWS, DIM), jnp.bfloat16)
-        k = 0
+        i = 0
         for ref, units in zip(chunk_refs[n], pieces[n]):
             for u in range(units):
-                for e in range(2):
-                    spot = base + (2 * k + e) * TOK
-                    keys[spot : spot + TOK, :] = ref[u, e, 0, :TOK, :]
-                    values[spot : spot + TOK, :DIM] = ref[u, e, 1, :TOK, :]
-                    shard = shard_at(rows_of[n], k, e)
-                    low = first_open - shard * SLOTS
-                    slot = lax.broadcasted_iota(jnp.int32, (LIVE, DIM), 0)
-                    live = (slot >= low) & (slot < len_ref[shard])
-                    spot = base + SPAN_ROWS + (2 * k + e) * LIVE
-                    keys[spot : spot + LIVE, :] = ref[u, e, 0, TOK:, :]
-                    piece = ref[u, e, 1, TOK:, :].astype(jnp.float32)
-                    values[spot : spot + LIVE, :DIM] = jnp.where(live, piece, 0.0).astype(jnp.bfloat16)
-                    values[spot : spot + LIVE, DIM:] = jnp.where(live, 1.0, 0.0).astype(jnp.bfloat16)
-                k += 1
+                spot = base + i * TOK
+                keys[spot : spot + TOK, :] = ref[u, 0, :TOK, :]
+                values[spot : spot + TOK, :DIM] = ref[u, 1, :TOK, :]
+                shard = shard_at(rows_of[n], i // 2, i % 2)
+                low = first_open - shard * SLOTS
+                slot = lax.broadcasted_iota(jnp.int32, (LIVE, DIM), 0)
+                live = (slot >= low) & (slot < len_ref[shard])
+                spot = base + SPAN_ROWS + i * LIVE
+                keys[spot : spot + LIVE, :] = ref[u, 0, TOK:, :]
+                piece = ref[u, 1, TOK:, :].astype(jnp.float32)
+                values[spot : spot + LIVE, :DIM] = jnp.where(live, piece, 0.0).astype(jnp.bfloat16)
+                values[spot : spot + LIVE, DIM:] = jnp.where(live, 1.0, 0.0).astype(jnp.bfloat16)
+                i += 1
     spare = count * CHUNK
     keys[spare : spare + BLOCK, :] = jnp.zeros((BLOCK, DIM), jnp.bfloat16)
     values[spare : spare + BLOCK, :] = jnp.zeros((BLOCK, 2 * DIM), jnp.bfloat16)
 
     for q in range(2):
         mine = 2 * chip + (core if q == 0 else 1 - core)
-        for h in range(GROUP):
-            queries[h * TOK : (h + 1) * TOK, :] = q_refs[q][:, h * DIM : (h + 1) * DIM]
+        queries = q_refs[q].at[pl.ds(q_refs[q].shape[0] - ROWS, ROWS), :]
 
         filled = jnp.int32(0)
         for n in range(count):
@@ -206,7 +209,7 @@
             tile(2, whole * TILE_BLOCKS)
 
         if last:
-            held, top = refs[5:]
+            held, top = refs[4:]
 
             def write_out():
                 for h in range(GROUP):
@@ -266,29 +269,24 @@
 
             def unit(u, _, ref=ref, row=row, begin=begin):
                 pltpu.sync_copy(ref.at[u], held)
-                k = begin + u
+                k, e = (begin + u) >> 1, (begin + u) & 1
                 there = chip_of(place, row, jnp.where(k < 2, -k, k - 1))
-
-                def device(e, _):
-                    shard = 2 * there + jnp.where(e == 0, core, 1 - core)
-                    token = lax.broadcasted_iota(jnp.int32, (TOK, TOK), 0)
-                    key = lax.broadcasted_iota(jnp.int32, (TOK, TOK), 1)
-                    listed = table_ref[mine, shard] == 1
-                    reach = jnp.where(shard < mine, TOK, jnp.where(shard == mine, 0, -2 * TOK))
-                    reach = jnp.where(listed, reach, -2 * TOK)
-                    add(held[e, 0, :TOK, :], held[e, 1, :TOK, :], key <= token + reach)
-                    slot = lax.broadcasted_iota(jnp.int32, (TOK, LIVE), 1)
-                    live = (slot >= first_open - shard * SLOTS) & (slot < len_ref[shard])
-                    add(held[e, 0, TOK:, :], held[e, 1, TOK:, :], live)
-                    return 0
-
-                return lax.fori_loop(0, 2, device, 0)
+                shard = 2 * there + jnp.where(e == 0, core, 1 - core)
+                token = lax.broadcasted_iota(jnp.int32, (TOK, TOK), 0)
+                key = lax.broadcasted_iota(jnp.int32, (TOK, TOK), 1)
+                reach = jnp.where(shard < mine, TOK, jnp.where(shard == mine, 0, -2 * TOK))
+                reach = jnp.where(table_ref[mine, shard] == 1, reach, -2 * TOK)
+                add(held[0, :TOK, :], held[1, :TOK, :], key <= token + reach)
+                slot = lax.broadcasted_iota(jnp.int32, (TOK, LIVE), 1)
+                live = (slot >= first_open - shard * SLOTS) & (slot < len_ref[shard])
+                add(held[0, TOK:, :], held[1, TOK:, :], live)
+                return 0
 
             lax.fori_loop(0, units, unit, 0)
             begin += units
 
 
-def stage(rows_of, last, scalars, queries, chunks, carry=None, after=()):
+def stage(rows_of, last, scalars, queries, chunks, carry=None):
     smem = pl.BlockSpec(memory_space=pltpu.SMEM)
     vmem = pl.BlockSpec(memory_space=pltpu.VMEM)
     anywhere = pl.BlockSpec(memory_space=pl.ANY)
@@ -299,7 +297,7 @@
         pieces.append(tuple(part.shape[0] for part in chunks[row]))
     if carry is not None:
         operands.append(carry)
-    specs = [smem] * 4 + [vmem] * (len(operands) - 4)
+    specs = [smem] * 3 + [vmem] * (len(operands) - 3)
     every = None
     if last:
         every = []
@@ -307,28 +305,26 @@
             operands += chunks[row]
             every.append(tuple(part.shape[0] for part in chunks[row]))
         every = tuple(every)
-    operands += list(after)
     specs += [anywhere] * (len(operands) - len(specs))
     count = len(rows_of)
     total = ((2, ROWS, 2 * DIM), jnp.float32)
     scratch = [
         pltpu.VMEM((count * CHUNK + BLOCK, DIM), jnp.bfloat16),
         pltpu.VMEM((count * CHUNK + BLOCK, 2 * DIM), jnp.bfloat16),
-        pltpu.VMEM((ROWS, DIM), jnp.bfloat16),
         pltpu.SMEM((count * (PER * 2 + CACHE_ROWS // BLOCK) + TILE_BLOCKS,), jnp.int32),
     ]
     if last:
         out_shape = (jax.ShapeDtypeStruct((TOK, GROUP * DIM), jnp.bfloat16),) * 2
         out_specs = (vmem, vmem)
         scratch = [pltpu.VMEM(*total)] + scratch + [
-            pltpu.VMEM((2, 2, TOK + LIVE, DIM), jnp.bfloat16),
+            pltpu.VMEM((2, TOK + LIVE, DIM), jnp.bfloat16),
             pltpu.VMEM((ROWS, DIM), jnp.float32),
         ]
     else:
         out_shape = jax.ShapeDtypeStruct(*total)
         out_specs = vmem
     return pl.pallas_call(
-        functools.partial(stage_kernel, tuple(rows_of), tuple(pieces), carry is not None, every, len(after)),
+        functools.partial(stage_kernel, tuple(rows_of), tuple(pieces), carry is not None, every),
         out_shape=out_shape,
         in_specs=specs,
         out_specs=out_specs,
@@ -343,67 +339,88 @@
     )(*operands)
 
 
-def pairs_kernel(place_ref, span_ref, cache_ref, *outs):
-    core = place_ref[2]
-    for out, head in zip(outs, (core, 1 - core, 2 + core, 3 - core)):
+def ordered(value, *after):
+    return lax.optimization_barrier((value, after))[0]
+
+
+def split_kernel(span_ref, cache_ref, queries_ref, stream_ref, own_ref, own_q_ref, *rest):
+    packs, stream_out, done = rest[:3], rest[3], rest[4]
+    width = GROUP * DIM
+    move = pltpu.make_async_copy(stream_ref.at[:, 2 * width :], stream_out, done)
+    move.start()
+    core = own_place()[2]
+
+    def pairs_at(head, out, at):
         columns = pl.ds(pl.multiple_of(head * DIM, DIM), DIM)
         for i in range(2):
-            out[i, :TOK, :] = span_ref[i, :, columns]
-            out[i, TOK:, :] = cache_ref[i, :LIVE, columns]
-
-
-def queries_kernel(place_ref, queries_ref, stream_ref, *outs):
-    core = place_ref[2]
-    width = GROUP * DIM
-    for out, head in zip(outs[:4], (core, 1 - core, 2 + core, 3 - core)):
-        out[...] = queries_ref[:, pl.ds(pl.multiple_of(head * width, width), width)]
-    outs[4][...] = stream_ref[:, 2 * width :]
-
-
-def split(kernel, place, first, second, shapes, after=()):
-    smem = pl.BlockSpec(memory_space=pltpu.SMEM)
+            begin = at + i * (TOK + LIVE)
+            out[begin : begin + TOK, :] = span_ref[i, :, columns]
+            out[begin + TOK : begin + TOK + LIVE, :] = cache_ref[i, :LIVE, columns]
+
+    def queries_at(head, out, at):
+        for h in range(GROUP):
+            columns = pl.ds(pl.multiple_of(head * width + h * DIM, DIM), DIM)
+            out[at + h * TOK : at + (h + 1) * TOK, :] = queries_ref[:, columns]
+
+    pairs_at(core, own_ref, 0)
+    queries_at(core, own_q_ref, 0)
+    for out, head in zip(packs, (1 - core, 2 + core, 3 - core)):
+        pairs_at(head, out, 0)
+        queries_at(head, out, PAIR)
+    move.wait()
+
+
+def split(span, cache, queries, stream):
     vmem = pl.BlockSpec(memory_space=pltpu.VMEM)
     anywhere = pl.BlockSpec(memory_space=pl.ANY)
+    shapes = [(PAIR, DIM), (ROWS, DIM)] + [(PAIR + ROWS, DIM)] * 3 + [(TOK, 2 * GROUP * DIM)]
     return pl.pallas_call(
-        lambda place_ref, a, b, *rest: kernel(place_ref, a, b, *rest[len(after) :]),
+        split_kernel,
         out_shape=tuple(jax.ShapeDtypeStruct(shape, jnp.bfloat16) for shape in shapes),
-        in_specs=[smem, vmem, vmem] + [anywhere] * len(after),
-        out_specs=(vmem,) * len(shapes),
-        name=kernel.__name__,
-    )(place, first, second, *after)
-
-
-def spread(unit):
-    return jnp.stack([unit] + [first_ring(unit, -k) for k in OFFSETS[1:]])
+        in_specs=[vmem, vmem, vmem, anywhere],
+        out_specs=(vmem,) * 5 + (anywhere,),
+        scratch_shapes=[pltpu.SemaphoreType.DMA],
+        cost_estimate=pl.CostEstimate(flops=0, bytes_accessed=8 * 1024 * 1024, transcendentals=0),
+        name="split",
+    )(span, cache, queries, stream)
+
+
+def unit_of(first, second):
+    return jnp.concatenate([first[:PAIR], second[:PAIR]]).reshape(2, 2, TOK + LIVE, DIM)
 
 
 def shards(stream, queries, span_kv, cache_kv, cache_len, context_start, block_table):
-    seq = lax.axis_index("seq")
-    core = seq % 2
-    place = jnp.stack([seq // 8, (seq // 2) % 4, core]).astype(jnp.int32)
-    scalars = (place, block_table, cache_len, context_start)
+    core = lax.axis_index("seq") % 2
+    scalars = (block_table, cache_len, context_start)
     width = GROUP * DIM
 
-    mine, theirs, late_same, late_cross = split(
-        pairs_kernel, place, span_kv[0], cache_kv[0], [(2, TOK + LIVE, DIM)] * 4
+    mine, q_mine, theirs, late_same, late_cross, stream_late = split(
+        span_kv[0], cache_kv[0], queries[0], stream[0]
     )
-    near_unit = jnp.stack([mine, swapped(theirs)])
-    late_unit = jnp.stack([up(late_same), up_swapped(late_cross)])
-    q_mine, q_theirs, q_same, q_cross, stream_late = split(
-        queries_kernel, place, queries[0], stream[0], [(TOK, width)] * 4 + [(TOK, 2 * width)]
-    )
-    near_q = (q_mine, swapped(q_theirs))
-    late_q = (up(q_same), up_swapped(q_cross))
+    received = swapped(theirs)
+    near_unit = unit_of(mine, received)
+    near_q = (q_mine, received)
+    late_parts = (up(late_same), up_swapped(late_cross))
+    before, after = first_ring(near_unit, 1), first_ring(near_unit, -1)
+    far = [first_ring(before[:1], 1), first_ring(after[1:], -1)]
+    near_row = jnp.concatenate([near_unit, before, after] + far)
+    near = {0: [near_row], -1: [second_ring(near_row, 1)], 1: [second_ring(near_row, -1)]}
+
+    late_parts = ordered(late_parts, near_row)
+    late_unit = unit_of(*late_parts)
+    late_q = late_parts
     late_stream = up(stream_late)
-
-    near_row = spread(near_unit)
-    near = {0: [near_row], -1: [second_ring(near_row, 1)], 1: [second_ring(near_row, -1)]}
-    late_row = spread(late_unit)
-    near_sum = stage((0,), False, scalars, near_q, near, after=[late_unit])
-    near[2] = [second_ring(near[-1][0][:2], 1), second_ring(near[1][0][2:], -1)]
+    late_pieces = [first_ring(late_unit, -k) for k in OFFSETS[1:]]
+    near_sum = stage((0,), False, scalars, ordered(near_q, late_unit), near)
+    late_pieces = ordered(late_pieces, near_sum)
+    near[-1] = ordered(near[-1], near_sum)
+    near[2] = [second_ring(near[-1][0], 1)]
+    late_row = jnp.concatenate([late_unit] + late_pieces)
     late = {0: [late_row], -1: [second_ring(late_row, 1)], 1: [second_ring(late_row, -1)]}
-    near_sum = stage((-1, 1), False, scalars, near_q, near, near_sum, after=[late_row])
-    own, other = stage((2,), True, scalars, near_q, near, near_sum)
+    near_sum = stage((-1, 1), False, scalars, ordered(near_q, late_row), near, near_sum)
+    late[1] = ordered(late[1], near_sum)
+    late[2] = [second_ring(late[1][0], -1)]
+    own, other = stage((2,), True, scalars, ordered(near_q, late[1], late_stream), near, near_sum)
 
     def added(own, other, base):
         received = swapped(other)
@@ -412,12 +429,11 @@
         )
         return (base.astype(jnp.float32) + both.astype(jnp.float32)).astype(jnp.bfloat16)
 
-    late_sum = stage((0,), False, scalars, late_q, late, after=[own])
     near_done = added(own, other, stream[0, :, : 2 * width])
     near_out = up(near_done)
-    late[2] = [second_ring(late[-1][0][:2], 1), second_ring(late[1][0][2:], -1)]
-    late_sum = stage((-1, 1), False, scalars, late_q, late, late_sum, after=[near_done])
-    own, other = stage((2,), True, scalars, late_q, late, late_sum, after=[near_out])
+    late_sum = stage((0, -1, 1), False, scalars, ordered(late_q, near_done), late)
+    late_sum, near_out = lax.optimization_barrier((late_sum, near_out))
+    own, other = stage((2,), True, scalars, late_q, late, late_sum)
     late_out = added(own, other, late_stream)
     return jnp.concatenate([near_out, late_out], 1)[None]
 

time: 906 us -> 891 us (0.983)
  starting transfers between devices: 26.2 us -> 15.3 us
    pallas_call x2 -> x1, Pallas kernels: 4.64 us -> 19.5 us  [split(): pl.pallas_call(split_kernel, out_shape=tuple((jax.ShapeDtypeStruct(shape,...]
    pallas_call x6 -> x5, Pallas kernels: 824 us -> 809 us  [stage(): pl.pallas_call(functools.partial(stage_kernel, tuple(rows_of), tuple(piec...]
    ppermute x24 -> x20, starting transfers between devices: 26.2 us -> 15.3 us  [moved(): return lax.ppermute(value, AXES, pairs)]
    ppermute x24 -> x20, waiting for transfers between devices: 31.1 us -> 31 us  [moved(): return lax.ppermute(value, AXES, pairs)]
  transfers between devices with their start and end apart: 24 -> 20, of which waited for: 10 -> 11; matrix products, arithmetic and copies ran while one was open for 1% -> 0% of each run, Pallas kernels for 92% -> 47%
where the time goes in v3:
time: 891 us; the launch traced here: 882 us
  Pallas kernels  829 us (93%)
  waiting for transfers between devices  31 us (3%)
  starting transfers between devices  15.3 us (2%)
    pallas_call x5, Pallas kernels, stage(): pl.pallas_call(functools.partial(stage_kernel, tuple(rows_of), tuple(piec...  809 us
    ppermute x20, waiting for transfers between devices, moved(): return lax.ppermute(value, AXES, pairs)  31 us
    pallas_call x1, Pallas kernels, split(): pl.pallas_call(split_kernel, out_shape=tuple((jax.ShapeDtypeStruct(shape,...  19.5 us
  transfers between devices with their start and end apart: 20, of which 11 were waited for; matrix products, arithmetic and copies ran while one was open for 0% of the time, Pallas kernels for 47%

profile of v3, /device:TPU:103, one launch (start us, length us, event | category | flops | bytes accessed | tf_op | source)
XLA Modules:
  0.0 881.9 jit_solution(575239134562192470)
XLA Ops:
  0.0 19.5 %split.1 = (bf16[416,128]{1,0:T(8,128)(2,1)}, bf16[1024,128]{1,0:T(8,128)(2,1)}, bf16[1440,128]{1,0:T(8,128)(2,1)}, bf16[1440,128]{1,0:T(8,128)(2,1)}, bf16[1440...) custom-call(bf16[2,128,512]{2,1,0:T(8,128)(2,1)} %bitcast.20, bf16[2,128,512]{2,1,0:T(8,128)(2,1)} %bitcast.21, ...), custom_call_target="tpu_custom_call" | custom-call | bytes 8388608 | tf_op jit(solution)/shard_map/split/pallas_call | solution.py:377
  19.6 0.8 collective-permute-start.2
  20.3 1.5 collective-permute-done.2.refs_4_
  21.9 0.9 pad_maximum_fusion.1
  22.9 1.5 collective-permute-start.4
  24.3 1.3 collective-permute-start
  25.6 2.4 collective-permute-start.1
  28.1 1.1 collective-permute-start.5
  29.7 2.2 collective-permute-done.5
  32.0 2.3 collective-permute-done.6
  35.4 1.1 collective-permute-start.12
  36.6 7.7 collective-permute-done.1.refs_4_
  44.4 1.5 collective-permute-start.8
  46.1 4.7 stage_0.1.refs_7_
  50.7 0.8 collective-permute-done.7
  51.5 3.8 collective-permute-done.8
  55.5 2.7 collective-permute-start.14
  58.2 0.8 collective-permute-start.13
  59.3 6.5 stage_3_1.1.refs_6_
  65.7 2.8 collective-permute-done.10.refs_7_.refs_9_
  68.6 3.7 collective-permute-done.13
  72.3 394.4 %stage_2.2 = (bf16[128,1024]{1,0:T(8,128)(2,1)S(1)}, bf16[128,1024]{1,0:T(8,128)(2,1)}) custom-call(s32[32,32]{1,0:T(8,128)S(1)} %copy-done.1, s32[32]{0:T(128)S(1)} %copy-done.3, s32[1]{0:T(128)S(6)} %copy.12.refs_2_, bf16[1024,128]{1,0:T(8,128)(2,1)S(1)} %copy-done, bf16[1440,128]{1,0:T(8,128)(2,1)S(1)} %collective-permute-done.2.refs_4_, ...), custom_call_target="tpu_custom_call" | custom-call | flops 2617245696 | bytes 851968 | tf_op jit(solution)/shard_map/stage_2/pallas_call | solution.py:326
  466.7 1.9 collective-permute-done.15
  468.6 1.4 fusion
  470.1 0.7 copy-done.2
  470.9 0.7 copy-done.4
  471.5 10.1 %stage_0_3_1.1.refs_6_ = f32[2,1024,256]{2,1,0:T(8,128)S(1)} custom-call(s32[32,32]{1,0:T(8,128)S(1)} %copy-done.2, s32[32]{0:T(128)S(1)} %copy-done.4, s32[1]{0:T(128)S(6)} %copy.12.refs_2_, bf16[1440,128]{1,0:T(8,128)(2,1)S(1)} %collective-permute-done.refs_3_, bf16[1440,128]{1,0:T(8,128)(2,1)S(1)} %collective-permute-done.1.refs_4_, ...), custom_call_target="tpu_custom_call" | custom-call | flops 7851737088 | bytes 2555904 | tf_op jit(solution)/shard_map/stage_0_3_1/pallas_call | solution.py:326
  481.6 3.1 collective-permute-done.17
  484.7 393.8 %stage_2.3 = (bf16[128,1024]{1,0:T(8,128)(2,1)S(1)}, bf16[128,1024]{1,0:T(8,128)(2,1)S(1)}) custom-call(s32[32,32]{1,0:T(8,128)S(1)} %copy-done.2, s32[32]{0:T(128)S(1)} %copy-done.4, s32[1]{0:T(128)S(6)} %copy.12.refs_2_, bf16[1440,128]{1,0:T(8,128)(2,1)S(1)} %collective-permute-done.refs_3_, bf16[1440,128]{1,0:T(8,128)(2,1)S(1)} %collective-permute-done.1.refs_4_, ...), custom_call_target="tpu_custom_call" | custom-call | flops 2617245696 | bytes 851968 | tf_op jit(solution)/shard_map/stage_2/pallas_call | solution.py:326
  878.5 0.5 collective-permute-start.19
  879.0 1.2 collective-permute-done.19
  880.4 1.1 maximum_bitcast_fusion
  (46 shorter events, 2.3 us)
Async XLA Ops:
  19.5 26.5 %copy-start = (bf16[1024,128]{1,0:T(8,128)(2,1)S(1)}, bf16[1024,128]{1,0:T(8,128)(2,1)}, u32[]{:S(2)}) copy-start(bf16[1024,128]{1,0:T(8,128)(2,1)} %get-tuple-element.49.refs_3_) | copy-start | bytes 786436
  19.5 26.5 %copy-start.1 = (s32[32,32]{1,0:T(8,128)S(1)}, s32[32,32]{1,0:T(8,128)}, u32[]{:S(2)}) copy-start(s32[32,32]{1,0:T(8,128)} %refs_0_.9) | copy-start | bytes 12292
  19.6 26.5 %copy-start.3 = (s32[32]{0:T(128)S(1)}, s32[32]{0:T(128)}, u32[]{:S(2)}) copy-start(s32[32]{0:T(128)} %refs_1_.9) | copy-start | bytes 388
  19.6 2.3 collective-permute-start.2
  22.8 5.3 collective-permute-start.3
  22.9 6.3 collective-permute-start.4
  24.3 12.2 %collective-permute-start = (bf16[1440,128]{1,0:T(8,128)(2,1)}, bf16[1440,128]{1,0:T(8,128)(2,1)S(1)}, u32[]{:S(2)}, u32[]{:S(2)}) collective-permute-start(bf16[1440,128]{1,0:T(8,128)(2,1)} %get-tuple-element.32), channel_id=1, source_target_pairs={{0,32},{1,33},{2,34},{3,35},{4,36},{5,37},{6,38},{7,39},{8,40},{9,... | collective-permute-start | bytes 1105928 | tf_op jit(solution)/shard_map/ppermute | solution.py:44
  25.6 18.7 %collective-permute-start.1 = (bf16[1440,128]{1,0:T(8,128)(2,1)}, bf16[1440,128]{1,0:T(8,128)(2,1)S(1)}, u32[]{:S(2)}, u32[]{:S(2)}) collective-permute-start(bf16[1440,128]{1,0:T(8,128)(2,1)} %get-tuple-element.33), channel_id=1, source_target_pairs={{0,33},{1,32},{2,35},{3,34},{4,37},{5,36},{6,39},{7,38},{8,41},{9,... | collective-permute-start | bytes 1105928 | tf_op jit(solution)/shard_map/ppermute | solution.py:44
  28.1 3.9 collective-permute-start.5
  29.1 5.1 collective-permute-start.6
  34.3 21.2 %collective-permute-start.11 = (bf16[8,2,208,128]{3,2,1,0:T(8,128)(2,1)S(1)}, bf16[8,2,208,128]{3,2,1,0:T(8,128)(2,1)S(1)}, u32[]{:S(2)}, u32[]{:S(2)}) collective-permute-start(bf16[8,2,208,128]{3,2,1,0:T(8,128)(2,1)S(1)} %constant_dynamic-update-slice_fusion.refs_5_.refs_7_), channel_id=1, source_target_pairs={{0,8},{1,3},{2,10},{3,5},{4,12},{5,7},{6,14},{7,1},{8,16},{9,11},{... | collective-permute-start | bytes 2555912 | tf_op jit(solution)/shard_map/ppermute | solution.py:44
  35.4 23.8 %collective-permute-start.12 = (bf16[8,2,208,128]{3,2,1,0:T(8,128)(2,1)S(1)}, bf16[8,2,208,128]{3,2,1,0:T(8,128)(2,1)S(1)}, u32[]{:S(2)}, u32[]{:S(2)}) collective-permute-start(bf16[8,2,208,128]{3,2,1,0:T(8,128)(2,1)S(1)} %constant_dynamic-update-slice_fusion.refs_5_.refs_7_), channel_id=1, source_target_pairs={{0,24},{1,7},{2,26},{3,1},{4,28},{5,3},{6,30},{7,5},{8,0},{9,15},{... | collective-permute-start | bytes 2555912 | tf_op jit(solution)/shard_map/ppermute | solution.py:44
  44.4 7.2 collective-permute-start.7
  44.4 10.9 %collective-permute-start.8 = (bf16[2,2,208,128]{3,2,1,0:T(8,128)(2,1)S(1)}, bf16[2,2,208,128]{3,2,1,0:T(8,128)(2,1)S(1)}, u32[]{:S(2)}, u32[]{:S(2)}) collective-permute-start(bf16[2,2,208,128]{3,2,1,0:T(8,128)(2,1)S(1)} %bitcast.17), channel_id=1, source_target_pairs={{0,6},{1,25},{2,0},{3,27},{4,2},{5,29},{6,4},{7,31},{8,14},{9,1},{... | collective-permute-start | bytes 638984 | tf_op jit(solution)/shard_map/ppermute | solution.py:44
  45.9 9.4 %collective-permute-start.9 = (bf16[2,2,208,128]{3,2,1,0:T(8,128)(2,1)S(1)}, bf16[2,2,208,128]{3,2,1,0:T(8,128)(2,1)S(1)}, u32[]{:S(2)}, u32[]{:S(2)}) collective-permute-start(bf16[2,2,208,128]{3,2,1,0:T(8,128)(2,1)S(1)} %bitcast.18), channel_id=1, source_target_pairs={{0,4},{1,17},{2,6},{3,19},{4,0},{5,21},{6,2},{7,23},{8,12},{9,25},... | collective-permute-start | bytes 638984 | tf_op jit(solution)/shard_map/ppermute | solution.py:44
  46.0 12.2 %copy-start.7 = (bf16[128,2048]{1,0:T(8,128)(2,1)S(1)}, bf16[128,2048]{1,0:T(8,128)(2,1)}, u32[]{:S(2)}) copy-start(bf16[128,2048]{1,0:T(8,128)(2,1)} %get-tuple-element.48) | copy-start | bytes 1572868
  55.5 13.1 %collective-permute-start.10 = (bf16[8,2,208,128]{3,2,1,0:T(8,128)(2,1)S(1)}, bf16[8,2,208,128]{3,2,1,0:T(8,128)(2,1)S(1)}, u32[]{:S(2)}, u32[]{:S(2)}) collective-permute-start(bf16[8,2,208,128]{3,2,1,0:T(8,128)(2,1)S(1)} %pad_maximum_fusion.refs_5_.refs_7_), channel_id=1, source_target_pairs={{0,24},{1,7},{2,26},{3,1},{4,28},{5,3},{6,30},{7,5},{8,0},{9,15},{... | collective-permute-start | bytes 2555912 | tf_op jit(solution)/shard_map/ppermute | solution.py:44
  55.5 16.7 %collective-permute-start.14 = (bf16[8,2,208,128]{3,2,1,0:T(8,128)(2,1)S(1)}, bf16[8,2,208,128]{3,2,1,0:T(8,128)(2,1)S(1)}, u32[]{:S(2)}, u32[]{:S(2)}) collective-permute-start(bf16[8,2,208,128]{3,2,1,0:T(8,128)(2,1)S(1)} %collective-permute-done.11.refs_5_.refs_8_), channel_id=1, source_target_pairs={{0,8},{1,3},{2,10},{3,5},{4,12},{5,7},{6,14},{7,1},{8,16},{9,11},{... | collective-permute-start | bytes 2555912 | tf_op jit(solution)/shard_map/ppermute | solution.py:44
  58.2 14.1 %collective-permute-start.13 = (bf16[128,2048]{1,0:T(8,128)(2,1)S(1)}, bf16[128,2048]{1,0:T(8,128)(2,1)S(1)}, u32[]{:S(2)}, u32[]{:S(2)}) collective-permute-start(bf16[128,2048]{1,0:T(8,128)(2,1)S(1)} %copy-done.7), channel_id=1, source_target_pairs={{0,32},{1,33},{2,34},{3,35},{4,36},{5,37},{6,38},{7,39},{8,40},{9,... | collective-permute-start | bytes 1572872 | tf_op jit(solution)/shard_map/ppermute | solution.py:44
  59.0 411.1 %collective-permute-start.16 = (bf16[8,2,208,128]{3,2,1,0:T(8,128)(2,1)S(1)}, bf16[8,2,208,128]{3,2,1,0:T(8,128)(2,1)S(1)}, u32[]{:S(2)}, u32[]{:S(2)}) collective-permute-start(bf16[8,2,208,128]{3,2,1,0:T(8,128)(2,1)S(1)} %pad_maximum_fusion.refs_5_.refs_7_), channel_id=1, source_target_pairs={{0,8},{1,3},{2,10},{3,5},{4,12},{5,7},{6,14},{7,1},{8,16},{9,11},{... | collective-permute-start | bytes 2555912 | tf_op jit(solution)/shard_map/ppermute | solution.py:44
  72.3 394.5 %copy-start.5 = (bf16[128,2048]{1,0:T(8,128)(2,1)}, bf16[128,2048]{1,0:T(8,128)(2,1)S(1)}, u32[]{:S(2)}) copy-start(bf16[128,2048]{1,0:T(8,128)(2,1)S(1)} %collective-permute-done.13) | copy-start | bytes 1572868
  466.7 1.9 collective-permute-start.15
  466.7 18.0 %collective-permute-start.18 = (bf16[8,2,208,128]{3,2,1,0:T(8,128)(2,1)S(1)}, bf16[8,2,208,128]{3,2,1,0:T(8,128)(2,1)S(1)}, u32[]{:S(2)}, u32[]{:S(2)}) collective-permute-start(bf16[8,2,208,128]{3,2,1,0:T(8,128)(2,1)S(1)} %collective-permute-done.10.refs_7_.refs_9_), channel_id=1, source_target_pairs={{0,24},{1,7},{2,26},{3,1},{4,28},{5,3},{6,30},{7,5},{8,0},{9,15},{... | collective-permute-start | bytes 2555912 | tf_op jit(solution)/shard_map/ppermute | solution.py:44
  470.0 14.7 %collective-permute-start.17 = (bf16[128,2048]{1,0:T(8,128)(2,1)S(1)}, bf16[128,2048]{1,0:T(8,128)(2,1)S(1)}, u32[]{:S(2)}, u32[]{:S(2)}) collective-permute-start(bf16[128,2048]{1,0:T(8,128)(2,1)S(1)} %fusion), channel_id=1, source_target_pairs={{0,32},{1,33},{2,34},{3,35},{4,36},{5,37},{6,38},{7,39},{8,40},{9,... | collective-permute-start | bytes 1572872 | tf_op jit(solution)/shard_map/ppermute | solution.py:44
  470.1 0.7 copy-start.2
  470.9 0.7 copy-start.4
  481.6 398.6 %copy-start.6 = (bf16[128,2048]{1,0:T(8,128)(2,1)S(1)}, bf16[128,2048]{1,0:T(8,128)(2,1)}, u32[]{:S(2)}) copy-start(bf16[128,2048]{1,0:T(8,128)(2,1)} %copy-done.5) | copy-start | bytes 1572868
  878.5 1.7 collective-permute-start.19

commit v4 on v3

--- a/solution.py
+++ b/solution.py
@@ -191,7 +191,7 @@
                 held = (first, scores)
             finish(*held)
 
-        whole = (filled + 3) // TILE_BLOCKS
+        whole = (filled + 1) // TILE_BLOCKS
         rest = filled - whole * TILE_BLOCKS
 
         def whole_tile(step, _):
@@ -204,9 +204,11 @@
         def _():
             tile(4, whole * TILE_BLOCKS)
 
-        @pl.when((rest > 0) & (rest <= 2))
+        left = jnp.where(rest > 2, rest - 4, rest)
+
+        @pl.when(left > 0)
         def _():
-            tile(2, whole * TILE_BLOCKS)
+            tile(2, filled - left)
 
         if last:
             held, top = refs[4:]
@@ -343,17 +345,15 @@
     return lax.optimization_barrier((value, after))[0]
 
 
-def split_kernel(span_ref, cache_ref, queries_ref, stream_ref, own_ref, own_q_ref, *rest):
-    packs, stream_out, done = rest[:3], rest[3], rest[4]
+def split_kernel(span_ref, cache_ref, queries_ref, stream_ref, *outs):
+    own, own_q, pack, same, cross, same_q, cross_q, late_stream = outs
+    core = own_place()[2]
     width = GROUP * DIM
-    move = pltpu.make_async_copy(stream_ref.at[:, 2 * width :], stream_out, done)
-    move.start()
-    core = own_place()[2]
-
-    def pairs_at(head, out, at):
+
+    def pairs_at(head, out):
         columns = pl.ds(pl.multiple_of(head * DIM, DIM), DIM)
         for i in range(2):
-            begin = at + i * (TOK + LIVE)
+            begin = i * (TOK + LIVE)
             out[begin : begin + TOK, :] = span_ref[i, :, columns]
             out[begin + TOK : begin + TOK + LIVE, :] = cache_ref[i, :LIVE, columns]
 
@@ -362,24 +362,26 @@
             columns = pl.ds(pl.multiple_of(head * width + h * DIM, DIM), DIM)
             out[at + h * TOK : at + (h + 1) * TOK, :] = queries_ref[:, columns]
 
-    pairs_at(core, own_ref, 0)
-    queries_at(core, own_q_ref, 0)
-    for out, head in zip(packs, (1 - core, 2 + core, 3 - core)):
-        pairs_at(head, out, 0)
-        queries_at(head, out, PAIR)
-    move.wait()
+    pairs_at(core, own)
+    queries_at(core, own_q, 0)
+    pairs_at(1 - core, pack)
+    queries_at(1 - core, pack, PAIR)
+    pairs_at(2 + core, same)
+    queries_at(2 + core, same_q, 0)
+    late_stream[...] = stream_ref[:, 2 * width :]
+    pairs_at(3 - core, cross)
+    queries_at(3 - core, cross_q, 0)
 
 
 def split(span, cache, queries, stream):
     vmem = pl.BlockSpec(memory_space=pltpu.VMEM)
-    anywhere = pl.BlockSpec(memory_space=pl.ANY)
-    shapes = [(PAIR, DIM), (ROWS, DIM)] + [(PAIR + ROWS, DIM)] * 3 + [(TOK, 2 * GROUP * DIM)]
+    shapes = [(PAIR, DIM), (ROWS, DIM), (PAIR + ROWS, DIM)] + [(PAIR, DIM)] * 2
+    shapes += [(ROWS, DIM)] * 2 + [(TOK, 2 * GROUP * DIM)]
     return pl.pallas_call(
         split_kernel,
         out_shape=tuple(jax.ShapeDtypeStruct(shape, jnp.bfloat16) for shape in shapes),
-        in_specs=[vmem, vmem, vmem, anywhere],
-        out_specs=(vmem,) * 5 + (anywhere,),
-        scratch_shapes=[pltpu.SemaphoreType.DMA],
+        in_specs=[vmem] * 4,
+        out_specs=(vmem,) * len(shapes),
         cost_estimate=pl.CostEstimate(flops=0, bytes_accessed=8 * 1024 * 1024, transcendentals=0),
         name="split",
     )(span, cache, queries, stream)
@@ -394,33 +396,32 @@
     scalars = (block_table, cache_len, context_start)
     width = GROUP * DIM
 
-    mine, q_mine, theirs, late_same, late_cross, stream_late = split(
+    mine, q_mine, theirs, late_same, late_cross, q_same, q_cross, late_stream = split(
         span_kv[0], cache_kv[0], queries[0], stream[0]
     )
     received = swapped(theirs)
     near_unit = unit_of(mine, received)
     near_q = (q_mine, received)
+    near_pieces = [first_ring(near_unit, -k) for k in OFFSETS[1:]]
     late_parts = (up(late_same), up_swapped(late_cross))
-    before, after = first_ring(near_unit, 1), first_ring(near_unit, -1)
-    far = [first_ring(before[:1], 1), first_ring(after[1:], -1)]
-    near_row = jnp.concatenate([near_unit, before, after] + far)
+    near_pieces, late_parts = lax.optimization_barrier((near_pieces, late_parts))
+    near_row = jnp.concatenate([near_unit] + near_pieces)
     near = {0: [near_row], -1: [second_ring(near_row, 1)], 1: [second_ring(near_row, -1)]}
 
-    late_parts = ordered(late_parts, near_row)
-    late_unit = unit_of(*late_parts)
-    late_q = late_parts
-    late_stream = up(stream_late)
+    late_unit = unit_of(*ordered(late_parts, near_row))
     late_pieces = [first_ring(late_unit, -k) for k in OFFSETS[1:]]
     near_sum = stage((0,), False, scalars, ordered(near_q, late_unit), near)
     late_pieces = ordered(late_pieces, near_sum)
-    near[-1] = ordered(near[-1], near_sum)
-    near[2] = [second_ring(near[-1][0], 1)]
     late_row = jnp.concatenate([late_unit] + late_pieces)
     late = {0: [late_row], -1: [second_ring(late_row, 1)], 1: [second_ring(late_row, -1)]}
+    near[-1] = ordered(near[-1], late_row)
+    near[2] = [second_ring(near[-1][0], 1)]
+    q_same, q_cross = ordered((q_same, q_cross), near_sum)
+    late_q = (up(q_same), up_swapped(q_cross))
     near_sum = stage((-1, 1), False, scalars, ordered(near_q, late_row), near, near_sum)
     late[1] = ordered(late[1], near_sum)
     late[2] = [second_ring(late[1][0], -1)]
-    own, other = stage((2,), True, scalars, ordered(near_q, late[1], late_stream), near, near_sum)
+    own, other = stage((2,), True, scalars, ordered(near_q, late[1], late_q), near, near_sum)
 
     def added(own, other, base):
         received = swapped(other)
@@ -429,11 +430,11 @@
         )
         return (base.astype(jnp.float32) + both.astype(jnp.float32)).astype(jnp.bfloat16)
 
+    late_stream = up(ordered(late_stream, late_q))
     near_done = added(own, other, stream[0, :, : 2 * width])
     near_out = up(near_done)
-    late_sum = stage((0, -1, 1), False, scalars, ordered(late_q, near_done), late)
-    late_sum, near_out = lax.optimization_barrier((late_sum, near_out))
-    own, other = stage((2,), True, scalars, late_q, late, late_sum)
+    own, other = stage(OFFSETS, True, scalars, ordered(late_q, near_done, late[2]), late)
+    other = ordered(other, near_out, late_stream)
     late_out = added(own, other, late_stream)
     return jnp.concatenate([near_out, late_out], 1)[None]
 

time: 891 us -> 882 us (0.990)
  waiting for transfers between devices: 31 us -> 18.3 us
    pallas_call x5 -> x4, Pallas kernels: 809 us -> 831 us  [stage(): pl.pallas_call(functools.partial(stage_kernel, tuple(rows_of), tuple(piec...]
    pallas_call x1, Pallas kernels: 19.5 us -> 3.27 us  [split(): pl.pallas_call(split_kernel, out_shape=tuple((jax.ShapeDtypeStruct(shape,...]
    ppermute x20 -> x21, waiting for transfers between devices: 31 us -> 18.3 us  [moved(): return lax.ppermute(value, AXES, pairs)]
    ppermute x20 -> x21, starting transfers between devices: 15.3 us -> 20 us  [moved(): return lax.ppermute(value, AXES, pairs)]
  transfers between devices with their start and end apart: 20 -> 21, of which waited for: 11 -> 9; matrix products, arithmetic and copies ran while one was open for 0% -> 0% of each run, Pallas kernels for 47% -> 95%
where the time goes in v4:
time: 882 us; the launch traced here: 878 us
  Pallas kernels  835 us (95%)
  starting transfers between devices  20 us (2%)
  waiting for transfers between devices  18.3 us (2%)
    pallas_call x4, Pallas kernels, stage(): pl.pallas_call(functools.partial(stage_kernel, tuple(rows_of), tuple(piec...  831 us
    ppermute x21, starting transfers between devices, moved(): return lax.ppermute(value, AXES, pairs)  20 us
    ppermute x21, waiting for transfers between devices, moved(): return lax.ppermute(value, AXES, pairs)  18.3 us
  transfers between devices with their start and end apart: 21, of which 9 were waited for; matrix products, arithmetic and copies ran while one was open for 0% of the time, Pallas kernels for 95%

profile of v4, /device:TPU:103, one launch (start us, length us, event | category | flops | bytes accessed | tf_op | source)
XLA Modules:
  0.0 878.0 jit_solution(14596432597243255871)
XLA Ops:
  0.0 3.3 split.1
  3.3 0.7 collective-permute-start
  4.0 1.5 collective-permute-done.refs_4_
  5.5 0.9 pad_maximum_fusion.2
  6.5 1.5 collective-permute-start.2
  7.9 0.4 collective-permute-start.3
  8.4 1.3 collective-permute-start.4
  9.7 3.4 collective-permute-start.5
  13.0 0.7 collective-permute-done.4
  13.7 4.4 collective-permute-done.5
  18.2 0.1 pad_maximum_fusion.refs_5_.refs_7_
  18.3 1.9 collective-permute-start.10
  21.0 1.5 collective-permute-start.7
  22.5 1.1 collective-permute-start.8
  23.6 4.7 stage_0.1.refs_7_
  28.3 1.5 collective-permute-done.7
  29.9 4.0 collective-permute-done.8
  33.8 0.1 pad_maximum_fusion.1.refs_5_.refs_9_
  34.1 0.7 collective-permute-done.10.refs_5_.refs_8_
  34.8 3.0 collective-permute-start.14
  37.9 3.2 collective-permute-start.13
  41.1 0.5 collective-permute-start.19
  41.6 8.0 stage_3_1.1.refs_6_
  49.6 1.0 collective-permute-start.18
  50.7 2.0 collective-permute-done.13.refs_4_
  52.6 402.9 %stage_2.1 = (bf16[128,1024]{1,0:T(8,128)(2,1)S(1)}, bf16[128,1024]{1,0:T(8,128)(2,1)}) custom-call(s32[32,32]{1,0:T(8,128)S(1)} %copy-done.1, s32[32]{0:T(128)S(1)} %copy-done.2, s32[1]{0:T(128)S(6)} %copy.8.refs_2_, bf16[1024,128]{1,0:T(8,128)(2,1)S(1)} %copy-done, bf16[1440,128]{1,0:T(8,128)(2,1)S(1)} %collective-permute-done.refs_4_, ...), custom_call_target="tpu_custom_call" | custom-call | flops 2617245696 | bytes 851968 | tf_op jit(solution)/shard_map/stage_2/pallas_call | solution.py:328
  455.6 1.9 collective-permute-done.15
  457.4 1.5 fusion
  459.0 415.9 %stage_0_3_1_2.1 = (bf16[128,1024]{1,0:T(8,128)(2,1)S(1)}, bf16[128,1024]{1,0:T(8,128)(2,1)S(1)}) custom-call(s32[32,32]{1,0:T(8,128)S(1)} %copy-done.1, s32[32]{0:T(128)S(1)} %copy-done.2, s32[1]{0:T(128)S(6)} %copy.8.refs_2_, bf16[1024,128]{1,0:T(8,128)(2,1)S(1)} %collective-permute-done.12.refs_3_, bf16[1024,128]{1,0:T(8,128)(2,1)S(1)} %collective-permute-done.13.refs_4_, ...), custom_call_target="tpu_custom_call" | custom-call | flops 10468982784 | bytes 3407872 | tf_op jit(solution)/shard_map/stage_0_3_1_2/pallas_call | solution.py:328
  875.0 1.5 collective-permute-done.20
  876.5 0.2 add_convert_fusion
  876.7 1.1 maximum_bitcast_fusion
  (33 shorter events, 0.7 us)
Async XLA Ops:
  0.0 23.6 %copy-start.1 = (s32[32,32]{1,0:T(8,128)S(1)}, s32[32,32]{1,0:T(8,128)}, u32[]{:S(2)}) copy-start(s32[32,32]{1,0:T(8,128)} %refs_0_.7) | copy-start | bytes 12292
  0.0 23.6 %copy-start.2 = (s32[32]{0:T(128)S(1)}, s32[32]{0:T(128)}, u32[]{:S(2)}) copy-start(s32[32]{0:T(128)} %refs_1_.7) | copy-start | bytes 388
  3.3 20.3 %copy-start = (bf16[1024,128]{1,0:T(8,128)(2,1)S(1)}, bf16[1024,128]{1,0:T(8,128)(2,1)}, u32[]{:S(2)}) copy-start(bf16[1024,128]{1,0:T(8,128)(2,1)} %get-tuple-element.66.refs_3_) | copy-start | bytes 786436
  3.3 2.2 collective-permute-start
  6.4 11.8 %collective-permute-start.1 = (bf16[2,2,208,128]{3,2,1,0:T(8,128)(2,1)S(1)}, bf16[2,2,208,128]{3,2,1,0:T(8,128)(2,1)S(1)}, u32[]{:S(2)}, u32[]{:S(2)}) collective-permute-start(bf16[2,2,208,128]{3,2,1,0:T(8,128)(2,1)S(1)} %bitcast.13), channel_id=1, source_target_pairs={{0,2},{1,9},{2,4},{3,11},{4,6},{5,13},{6,0},{7,15},{8,10},{9,17},{... | collective-permute-start | bytes 638984 | tf_op jit(solution)/shard_map/ppermute | solution.py:44
  6.5 11.7 %collective-permute-start.2 = (bf16[2,2,208,128]{3,2,1,0:T(8,128)(2,1)S(1)}, bf16[2,2,208,128]{3,2,1,0:T(8,128)(2,1)S(1)}, u32[]{:S(2)}, u32[]{:S(2)}) collective-permute-start(bf16[2,2,208,128]{3,2,1,0:T(8,128)(2,1)S(1)} %bitcast.14), channel_id=1, source_target_pairs={{0,6},{1,25},{2,0},{3,27},{4,2},{5,29},{6,4},{7,31},{8,14},{9,1},{... | collective-permute-start | bytes 638984 | tf_op jit(solution)/shard_map/ppermute | solution.py:44
  7.9 10.2 %collective-permute-start.3 = (bf16[2,2,208,128]{3,2,1,0:T(8,128)(2,1)S(1)}, bf16[2,2,208,128]{3,2,1,0:T(8,128)(2,1)S(1)}, u32[]{:S(2)}, u32[]{:S(2)}) collective-permute-start(bf16[2,2,208,128]{3,2,1,0:T(8,128)(2,1)S(1)} %bitcast.15), channel_id=1, source_target_pairs={{0,4},{1,17},{2,6},{3,19},{4,0},{5,21},{6,2},{7,23},{8,12},{9,25},... | collective-permute-start | bytes 638984 | tf_op jit(solution)/shard_map/ppermute | solution.py:44
  8.4 5.3 collective-permute-start.4
  9.7 8.5 collective-permute-start.5
  18.3 16.5 %collective-permute-start.10 = (bf16[8,2,208,128]{3,2,1,0:T(8,128)(2,1)S(1)}, bf16[8,2,208,128]{3,2,1,0:T(8,128)(2,1)S(1)}, u32[]{:S(2)}, u32[]{:S(2)}) collective-permute-start(bf16[8,2,208,128]{3,2,1,0:T(8,128)(2,1)S(1)} %pad_maximum_fusion.refs_5_.refs_7_), channel_id=1, source_target_pairs={{0,8},{1,3},{2,10},{3,5},{4,12},{5,7},{6,14},{7,1},{8,16},{9,11},{... | collective-permute-start | bytes 2555912 | tf_op jit(solution)/shard_map/ppermute | solution.py:44
  20.8 20.3 %collective-permute-start.11 = (bf16[8,2,208,128]{3,2,1,0:T(8,128)(2,1)S(1)}, bf16[8,2,208,128]{3,2,1,0:T(8,128)(2,1)S(1)}, u32[]{:S(2)}, u32[]{:S(2)}) collective-permute-start(bf16[8,2,208,128]{3,2,1,0:T(8,128)(2,1)S(1)} %pad_maximum_fusion.refs_5_.refs_7_), channel_id=1, source_target_pairs={{0,24},{1,7},{2,26},{3,1},{4,28},{5,3},{6,30},{7,5},{8,0},{9,15},{... | collective-permute-start | bytes 2555912 | tf_op jit(solution)/shard_map/ppermute | solution.py:44
  20.9 7.4 collective-permute-start.6
  21.0 8.9 %collective-permute-start.7 = (bf16[2,2,208,128]{3,2,1,0:T(8,128)(2,1)S(1)}, bf16[2,2,208,128]{3,2,1,0:T(8,128)(2,1)S(1)}, u32[]{:S(2)}, u32[]{:S(2)}) collective-permute-start(bf16[2,2,208,128]{3,2,1,0:T(8,128)(2,1)S(1)} %bitcast.18), channel_id=1, source_target_pairs={{0,6},{1,25},{2,0},{3,27},{4,2},{5,29},{6,4},{7,31},{8,14},{9,1},{... | collective-permute-start | bytes 638984 | tf_op jit(solution)/shard_map/ppermute | solution.py:44
  22.5 11.4 %collective-permute-start.8 = (bf16[2,2,208,128]{3,2,1,0:T(8,128)(2,1)S(1)}, bf16[2,2,208,128]{3,2,1,0:T(8,128)(2,1)S(1)}, u32[]{:S(2)}, u32[]{:S(2)}) collective-permute-start(bf16[2,2,208,128]{3,2,1,0:T(8,128)(2,1)S(1)} %bitcast.19), channel_id=1, source_target_pairs={{0,4},{1,17},{2,6},{3,19},{4,0},{5,21},{6,2},{7,23},{8,12},{9,25},... | collective-permute-start | bytes 638984 | tf_op jit(solution)/shard_map/ppermute | solution.py:44
  23.6 14.2 %copy-start.4 = (bf16[1024,128]{1,0:T(8,128)(2,1)S(1)}, bf16[1024,128]{1,0:T(8,128)(2,1)}, u32[]{:S(2)}) copy-start(bf16[1024,128]{1,0:T(8,128)(2,1)} %get-tuple-element.64) | copy-start | bytes 786436
  23.6 14.3 %copy-start.3 = (bf16[1024,128]{1,0:T(8,128)(2,1)S(1)}, bf16[1024,128]{1,0:T(8,128)(2,1)}, u32[]{:S(2)}) copy-start(bf16[1024,128]{1,0:T(8,128)(2,1)} %get-tuple-element.65) | copy-start | bytes 786436
  34.0 15.7 %collective-permute-start.9 = (bf16[8,2,208,128]{3,2,1,0:T(8,128)(2,1)S(1)}, bf16[8,2,208,128]{3,2,1,0:T(8,128)(2,1)S(1)}, u32[]{:S(2)}, u32[]{:S(2)}) collective-permute-start(bf16[8,2,208,128]{3,2,1,0:T(8,128)(2,1)S(1)} %pad_maximum_fusion.1.refs_5_.refs_9_), channel_id=1, source_target_pairs={{0,24},{1,7},{2,26},{3,1},{4,28},{5,3},{6,30},{7,5},{8,0},{9,15},{... | collective-permute-start | bytes 2555912 | tf_op jit(solution)/shard_map/ppermute | solution.py:44
  34.8 17.9 %collective-permute-start.14 = (bf16[8,2,208,128]{3,2,1,0:T(8,128)(2,1)S(1)}, bf16[8,2,208,128]{3,2,1,0:T(8,128)(2,1)S(1)}, u32[]{:S(2)}, u32[]{:S(2)}) collective-permute-start(bf16[8,2,208,128]{3,2,1,0:T(8,128)(2,1)S(1)} %collective-permute-done.10.refs_5_.refs_8_), channel_id=1, source_target_pairs={{0,8},{1,3},{2,10},{3,5},{4,12},{5,7},{6,14},{7,1},{8,16},{9,11},{... | collective-permute-start | bytes 2555912 | tf_op jit(solution)/shard_map/ppermute | solution.py:44
  37.8 12.9 %collective-permute-start.12 = (bf16[1024,128]{1,0:T(8,128)(2,1)S(1)}, bf16[1024,128]{1,0:T(8,128)(2,1)S(1)}, u32[]{:S(2)}, u32[]{:S(2)}) collective-permute-start(bf16[1024,128]{1,0:T(8,128)(2,1)S(1)} %copy-done.4), channel_id=1, source_target_pairs={{0,32},{1,33},{2,34},{3,35},{4,36},{5,37},{6,38},{7,39},{8,40},{9,... | collective-permute-start | bytes 786440 | tf_op jit(solution)/shard_map/ppermute | solution.py:44
  37.9 14.8 %collective-permute-start.13 = (bf16[1024,128]{1,0:T(8,128)(2,1)S(1)}, bf16[1024,128]{1,0:T(8,128)(2,1)S(1)}, u32[]{:S(2)}, u32[]{:S(2)}) collective-permute-start(bf16[1024,128]{1,0:T(8,128)(2,1)S(1)} %copy-done.3), channel_id=1, source_target_pairs={{0,33},{1,32},{2,35},{3,34},{4,37},{5,36},{6,39},{7,38},{8,41},{9,... | collective-permute-start | bytes 786440 | tf_op jit(solution)/shard_map/ppermute | solution.py:44
  41.1 417.9 %collective-permute-start.19 = (bf16[8,2,208,128]{3,2,1,0:T(8,128)(2,1)S(1)}, bf16[8,2,208,128]{3,2,1,0:T(8,128)(2,1)S(1)}, u32[]{:S(2)}, u32[]{:S(2)}) collective-permute-start(bf16[8,2,208,128]{3,2,1,0:T(8,128)(2,1)S(1)} %pad_maximum_fusion.1.refs_5_.refs_9_), channel_id=1, source_target_pairs={{0,8},{1,3},{2,10},{3,5},{4,12},{5,7},{6,14},{7,1},{8,16},{9,11},{... | collective-permute-start | bytes 2555912 | tf_op jit(solution)/shard_map/ppermute | solution.py:44
  49.6 409.3 %collective-permute-start.18 = (bf16[8,2,208,128]{3,2,1,0:T(8,128)(2,1)S(1)}, bf16[8,2,208,128]{3,2,1,0:T(8,128)(2,1)}, u32[]{:S(2)}, u32[]{:S(2)}) collective-permute-start(bf16[8,2,208,128]{3,2,1,0:T(8,128)(2,1)S(1)} %collective-permute-done.9.refs_7_.refs_11_), channel_id=1, source_target_pairs={{0,24},{1,7},{2,26},{3,1},{4,28},{5,3},{6,30},{7,5},{8,0},{9,15},{... | collective-permute-start | bytes 2555912 | tf_op jit(solution)/shard_map/ppermute | solution.py:44
  455.5 1.9 collective-permute-start.15
  455.5 419.3 %collective-permute-start.17 = (bf16[128,2048]{1,0:T(8,128)(2,1)}, bf16[128,2048]{1,0:T(8,128)(2,1)S(1)}, u32[]{:S(2)}, u32[]{:S(2)}) collective-permute-start(bf16[128,2048]{1,0:T(8,128)(2,1)} %get-tuple-element.71), channel_id=1, source_target_pairs={{0,32},{1,33},{2,34},{3,35},{4,36},{5,37},{6,38},{7,39},{8,40},{9,... | collective-permute-start | bytes 1572872 | tf_op jit(solution)/shard_map/ppermute | solution.py:44
  458.9 416.0 %collective-permute-start.16 = (bf16[128,2048]{1,0:T(8,128)(2,1)S(1)}, bf16[128,2048]{1,0:T(8,128)(2,1)S(1)}, u32[]{:S(2)}, u32[]{:S(2)}) collective-permute-start(bf16[128,2048]{1,0:T(8,128)(2,1)S(1)} %fusion), channel_id=1, source_target_pairs={{0,32},{1,33},{2,34},{3,35},{4,36},{5,37},{6,38},{7,39},{8,40},{9,... | collective-permute-start | bytes 1572872 | tf_op jit(solution)/shard_map/ppermute | solution.py:44
  874.9 1.6 collective-permute-start.20

commit v5 on v4

--- a/solution.py
+++ b/solution.py
@@ -408,20 +408,22 @@
     near_row = jnp.concatenate([near_unit] + near_pieces)
     near = {0: [near_row], -1: [second_ring(near_row, 1)], 1: [second_ring(near_row, -1)]}
 
-    late_unit = unit_of(*ordered(late_parts, near_row))
+    q_same, q_cross = ordered((q_same, q_cross), near_row)
+    late_q = (up(q_same), up_swapped(q_cross))
+    near_sum = stage((0,), False, scalars, near_q, near)
+    late_q = ordered(late_q, near_sum)
+    late_unit = unit_of(*ordered(late_parts, near_sum))
     late_pieces = [first_ring(late_unit, -k) for k in OFFSETS[1:]]
-    near_sum = stage((0,), False, scalars, ordered(near_q, late_unit), near)
+    late_stream = up(ordered(late_stream, near_sum))
+    near[-1] = ordered(near[-1], near_sum)
+    near[2] = [second_ring(near[-1][0], 1)]
+    near_sum = stage((-1, 1), False, scalars, ordered(near_q, late_unit, late_q), near, near_sum)
     late_pieces = ordered(late_pieces, near_sum)
     late_row = jnp.concatenate([late_unit] + late_pieces)
     late = {0: [late_row], -1: [second_ring(late_row, 1)], 1: [second_ring(late_row, -1)]}
-    near[-1] = ordered(near[-1], late_row)
-    near[2] = [second_ring(near[-1][0], 1)]
-    q_same, q_cross = ordered((q_same, q_cross), near_sum)
-    late_q = (up(q_same), up_swapped(q_cross))
-    near_sum = stage((-1, 1), False, scalars, ordered(near_q, late_row), near, near_sum)
-    late[1] = ordered(late[1], near_sum)
+    own, other = stage((2,), True, scalars, ordered(near_q, late_row, late_stream), near, near_sum)
+    late[1] = ordered(late[1], own)
     late[2] = [second_ring(late[1][0], -1)]
-    own, other = stage((2,), True, scalars, ordered(near_q, late[1], late_q), near, near_sum)
 
     def added(own, other, base):
         received = swapped(other)
@@ -430,11 +432,11 @@
         )
         return (base.astype(jnp.float32) + both.astype(jnp.float32)).astype(jnp.bfloat16)
 
-    late_stream = up(ordered(late_stream, late_q))
     near_done = added(own, other, stream[0, :, : 2 * width])
     near_out = up(near_done)
-    own, other = stage(OFFSETS, True, scalars, ordered(late_q, near_done, late[2]), late)
-    other = ordered(other, near_out, late_stream)
+    late_sum = stage((0, -1, 1), False, scalars, ordered(late_q, near_done), late)
+    late_sum, near_out = lax.optimization_barrier((late_sum, near_out))
+    own, other = stage((2,), True, scalars, late_q, late, late_sum)
     late_out = added(own, other, late_stream)
     return jnp.concatenate([near_out, late_out], 1)[None]
 

time: 882 us -> 873 us (0.990)
  Pallas kernels: 835 us -> 813 us
    pallas_call x4 -> x5, Pallas kernels: 831 us -> 810 us  [stage(): pl.pallas_call(functools.partial(stage_kernel, tuple(rows_of), tuple(piec...]
  transfers between devices with their start and end apart: 21 -> 21, of which waited for: 9 -> 9; matrix products, arithmetic and copies ran while one was open for 0% -> 0% of each run, Pallas kernels for 95% -> 48%
where the time goes in v5:
time: 873 us; the launch traced here: 863 us
  Pallas kernels  813 us (93%)
  waiting for transfers between devices  26.7 us (3%)
  starting transfers between devices  17.8 us (2%)
    pallas_call x5, Pallas kernels, stage(): pl.pallas_call(functools.partial(stage_kernel, tuple(rows_of), tuple(piec...  810 us
    ppermute x21, waiting for transfers between devices, moved(): return lax.ppermute(value, AXES, pairs)  26.7 us
    ppermute x21, starting transfers between devices, moved(): return lax.ppermute(value, AXES, pairs)  17.8 us
  transfers between devices with their start and end apart: 21, of which 9 were waited for; matrix products, arithmetic and copies ran while one was open for 0% of the time, Pallas kernels for 48%

profile of v5, /device:TPU:103, one launch (start us, length us, event | category | flops | bytes accessed | tf_op | source)
XLA Modules:
  0.0 862.8 jit_solution(10665951216365566005)
XLA Ops:
  0.0 3.3 split.1
  3.3 0.8 collective-permute-start
  4.0 1.5 collective-permute-done.refs_4_
  5.6 0.9 pad_maximum_fusion.2
  6.6 1.5 collective-permute-start.2
  8.0 0.4 collective-permute-start.3
  8.5 1.3 collective-permute-start.4
  9.8 3.4 collective-permute-start.5
  13.1 0.7 collective-permute-done.4
  13.8 4.4 collective-permute-done.5
  18.4 1.9 collective-permute-start.11
  20.9 0.2 collective-permute-start.6
  21.1 1.7 collective-permute-start.7
  22.8 4.6 stage_0.1.refs_7_
  27.5 0.4 collective-permute-start.8
  27.8 1.6 collective-permute-done.6.refs_3_
  29.5 0.1 collective-permute-start.9
  29.6 6.3 collective-permute-done.7.refs_4_
  35.8 1.1 collective-permute-start.10
  37.0 2.1 collective-permute-start.14
  39.0 6.6 stage_3_1.1.refs_6_
  45.8 2.7 collective-permute-start.16
  48.5 3.3 collective-permute-done.13
  51.8 395.2 %stage_2.2 = (bf16[128,1024]{1,0:T(8,128)(2,1)S(1)}, bf16[128,1024]{1,0:T(8,128)(2,1)}) custom-call(s32[32,32]{1,0:T(8,128)S(1)} %copy-done.1, s32[32]{0:T(128)S(1)} %copy-done.2, s32[1]{0:T(128)S(6)} %copy.8.refs_2_, bf16[1024,128]{1,0:T(8,128)(2,1)S(1)} %copy-done, bf16[1440,128]{1,0:T(8,128)(2,1)S(1)} %collective-permute-done.refs_4_, ...), custom_call_target="tpu_custom_call" | custom-call | flops 2617245696 | bytes 851968 | tf_op jit(solution)/shard_map/stage_2/pallas_call | solution.py:328
  447.0 1.8 collective-permute-done.15
  448.8 1.5 fusion
  450.4 9.0 %stage_0_3_1.1.refs_6_ = f32[2,1024,256]{2,1,0:T(8,128)S(1)} custom-call(s32[32,32]{1,0:T(8,128)S(1)} %copy-done.1, s32[32]{0:T(128)S(1)} %copy-done.2, s32[1]{0:T(128)S(6)} %copy.8.refs_2_, bf16[1024,128]{1,0:T(8,128)(2,1)S(1)} %collective-permute-done.6.refs_3_, bf16[1024,128]{1,0:T(8,128)(2,1)S(1)} %collective-permute-done.7.refs_4_, ...), custom_call_target="tpu_custom_call" | custom-call | flops 7851737088 | bytes 2555904 | tf_op jit(solution)/shard_map/stage_0_3_1/pallas_call | solution.py:328
  459.4 5.5 collective-permute-done.18
  465.0 394.5 %stage_2.3 = (bf16[128,1024]{1,0:T(8,128)(2,1)S(1)}, bf16[128,1024]{1,0:T(8,128)(2,1)S(1)}) custom-call(s32[32,32]{1,0:T(8,128)S(1)} %copy-done.1, s32[32]{0:T(128)S(1)} %copy-done.2, s32[1]{0:T(128)S(6)} %copy.8.refs_2_, bf16[1024,128]{1,0:T(8,128)(2,1)S(1)} %collective-permute-done.6.refs_3_, bf16[1024,128]{1,0:T(8,128)(2,1)S(1)} %collective-permute-done.7.refs_4_, ...), custom_call_target="tpu_custom_call" | custom-call | flops 2617245696 | bytes 851968 | tf_op jit(solution)/shard_map/stage_2/pallas_call | solution.py:328
  859.6 1.5 collective-permute-done.20
  861.1 0.2 add_convert_fusion
  861.3 1.1 maximum_bitcast_fusion
  (40 shorter events, 0.7 us)
Async XLA Ops:
  0.0 22.8 %copy-start.1 = (s32[32,32]{1,0:T(8,128)S(1)}, s32[32,32]{1,0:T(8,128)}, u32[]{:S(2)}) copy-start(s32[32,32]{1,0:T(8,128)} %refs_0_.9) | copy-start | bytes 12292
  0.0 22.8 %copy-start.2 = (s32[32]{0:T(128)S(1)}, s32[32]{0:T(128)}, u32[]{:S(2)}) copy-start(s32[32]{0:T(128)} %refs_1_.9) | copy-start | bytes 388
  3.3 17.6 %copy-start.7 = (bf16[1024,128]{1,0:T(8,128)(2,1)S(1)}, bf16[1024,128]{1,0:T(8,128)(2,1)}, u32[]{:S(2)}) copy-start(bf16[1024,128]{1,0:T(8,128)(2,1)} %get-tuple-element.51) | copy-start | bytes 786436
  3.3 17.8 %copy-start.6 = (bf16[1024,128]{1,0:T(8,128)(2,1)S(1)}, bf16[1024,128]{1,0:T(8,128)(2,1)}, u32[]{:S(2)}) copy-start(bf16[1024,128]{1,0:T(8,128)(2,1)} %get-tuple-element.52) | copy-start | bytes 786436
  3.3 19.5 %copy-start = (bf16[1024,128]{1,0:T(8,128)(2,1)S(1)}, bf16[1024,128]{1,0:T(8,128)(2,1)}, u32[]{:S(2)}) copy-start(bf16[1024,128]{1,0:T(8,128)(2,1)} %get-tuple-element.68.refs_3_) | copy-start | bytes 786436
  3.3 2.3 collective-permute-start
  6.5 11.8 %collective-permute-start.1 = (bf16[2,2,208,128]{3,2,1,0:T(8,128)(2,1)S(1)}, bf16[2,2,208,128]{3,2,1,0:T(8,128)(2,1)S(1)}, u32[]{:S(2)}, u32[]{:S(2)}) collective-permute-start(bf16[2,2,208,128]{3,2,1,0:T(8,128)(2,1)S(1)} %bitcast.17), channel_id=1, source_target_pairs={{0,2},{1,9},{2,4},{3,11},{4,6},{5,13},{6,0},{7,15},{8,10},{9,17},{... | collective-permute-start | bytes 638984 | tf_op jit(solution)/shard_map/ppermute | solution.py:44
  6.6 11.7 %collective-permute-start.2 = (bf16[2,2,208,128]{3,2,1,0:T(8,128)(2,1)S(1)}, bf16[2,2,208,128]{3,2,1,0:T(8,128)(2,1)S(1)}, u32[]{:S(2)}, u32[]{:S(2)}) collective-permute-start(bf16[2,2,208,128]{3,2,1,0:T(8,128)(2,1)S(1)} %bitcast.18), channel_id=1, source_target_pairs={{0,6},{1,25},{2,0},{3,27},{4,2},{5,29},{6,4},{7,31},{8,14},{9,1},{... | collective-permute-start | bytes 638984 | tf_op jit(solution)/shard_map/ppermute | solution.py:44
  8.0 10.2 %collective-permute-start.3 = (bf16[2,2,208,128]{3,2,1,0:T(8,128)(2,1)S(1)}, bf16[2,2,208,128]{3,2,1,0:T(8,128)(2,1)S(1)}, u32[]{:S(2)}, u32[]{:S(2)}) collective-permute-start(bf16[2,2,208,128]{3,2,1,0:T(8,128)(2,1)S(1)} %bitcast.19), channel_id=1, source_target_pairs={{0,4},{1,17},{2,6},{3,19},{4,0},{5,21},{6,2},{7,23},{8,12},{9,25},... | collective-permute-start | bytes 638984 | tf_op jit(solution)/shard_map/ppermute | solution.py:44
  8.5 5.3 collective-permute-start.4
  9.8 8.5 collective-permute-start.5
  18.4 18.6 %collective-permute-start.11 = (bf16[8,2,208,128]{3,2,1,0:T(8,128)(2,1)S(1)}, bf16[8,2,208,128]{3,2,1,0:T(8,128)(2,1)S(1)}, u32[]{:S(2)}, u32[]{:S(2)}) collective-permute-start(bf16[8,2,208,128]{3,2,1,0:T(8,128)(2,1)S(1)} %pad_maximum_fusion.refs_5_.refs_7_), channel_id=1, source_target_pairs={{0,8},{1,3},{2,10},{3,5},{4,12},{5,7},{6,14},{7,1},{8,16},{9,11},{... | collective-permute-start | bytes 2555912 | tf_op jit(solution)/shard_map/ppermute | solution.py:44
  20.3 16.7 %collective-permute-start.12 = (bf16[8,2,208,128]{3,2,1,0:T(8,128)(2,1)S(1)}, bf16[8,2,208,128]{3,2,1,0:T(8,128)(2,1)S(1)}, u32[]{:S(2)}, u32[]{:S(2)}) collective-permute-start(bf16[8,2,208,128]{3,2,1,0:T(8,128)(2,1)S(1)} %pad_maximum_fusion.refs_5_.refs_7_), channel_id=1, source_target_pairs={{0,24},{1,7},{2,26},{3,1},{4,28},{5,3},{6,30},{7,5},{8,0},{9,15},{... | collective-permute-start | bytes 2555912 | tf_op jit(solution)/shard_map/ppermute | solution.py:44
  20.9 8.5 collective-permute-start.6
  21.1 14.8 %collective-permute-start.7 = (bf16[1024,128]{1,0:T(8,128)(2,1)S(1)}, bf16[1024,128]{1,0:T(8,128)(2,1)S(1)}, u32[]{:S(2)}, u32[]{:S(2)}) collective-permute-start(bf16[1024,128]{1,0:T(8,128)(2,1)S(1)} %copy-done.6), channel_id=1, source_target_pairs={{0,33},{1,32},{2,35},{3,34},{4,37},{5,36},{6,39},{7,38},{8,41},{9,... | collective-permute-start | bytes 786440 | tf_op jit(solution)/shard_map/ppermute | solution.py:44
  22.8 14.1 %copy-start.5 = (bf16[128,2048]{1,0:T(8,128)(2,1)S(1)}, bf16[128,2048]{1,0:T(8,128)(2,1)}, u32[]{:S(2)}) copy-start(bf16[128,2048]{1,0:T(8,128)(2,1)} %get-tuple-element.67) | copy-start | bytes 1572868
  27.5 18.1 %collective-permute-start.8 = (bf16[2,2,208,128]{3,2,1,0:T(8,128)(2,1)S(1)}, bf16[2,2,208,128]{3,2,1,0:T(8,128)(2,1)S(1)}, u32[]{:S(2)}, u32[]{:S(2)}) collective-permute-start(bf16[2,2,208,128]{3,2,1,0:T(8,128)(2,1)S(1)} %bitcast.13), channel_id=1, source_target_pairs={{0,2},{1,9},{2,4},{3,11},{4,6},{5,13},{6,0},{7,15},{8,10},{9,17},{... | collective-permute-start | bytes 638984 | tf_op jit(solution)/shard_map/ppermute | solution.py:44
  29.5 16.2 %collective-permute-start.9 = (bf16[2,2,208,128]{3,2,1,0:T(8,128)(2,1)S(1)}, bf16[2,2,208,128]{3,2,1,0:T(8,128)(2,1)S(1)}, u32[]{:S(2)}, u32[]{:S(2)}) collective-permute-start(bf16[2,2,208,128]{3,2,1,0:T(8,128)(2,1)S(1)} %bitcast.14), channel_id=1, source_target_pairs={{0,6},{1,25},{2,0},{3,27},{4,2},{5,29},{6,4},{7,31},{8,14},{9,1},{... | collective-permute-start | bytes 638984 | tf_op jit(solution)/shard_map/ppermute | solution.py:44
  35.8 9.8 %collective-permute-start.10 = (bf16[2,2,208,128]{3,2,1,0:T(8,128)(2,1)S(1)}, bf16[2,2,208,128]{3,2,1,0:T(8,128)(2,1)S(1)}, u32[]{:S(2)}, u32[]{:S(2)}) collective-permute-start(bf16[2,2,208,128]{3,2,1,0:T(8,128)(2,1)S(1)} %bitcast.15), channel_id=1, source_target_pairs={{0,4},{1,17},{2,6},{3,19},{4,0},{5,21},{6,2},{7,23},{8,12},{9,25},... | collective-permute-start | bytes 638984 | tf_op jit(solution)/shard_map/ppermute | solution.py:44
  37.0 14.8 %collective-permute-start.13 = (bf16[128,2048]{1,0:T(8,128)(2,1)S(1)}, bf16[128,2048]{1,0:T(8,128)(2,1)S(1)}, u32[]{:S(2)}, u32[]{:S(2)}) collective-permute-start(bf16[128,2048]{1,0:T(8,128)(2,1)S(1)} %copy-done.5), channel_id=1, source_target_pairs={{0,32},{1,33},{2,34},{3,35},{4,36},{5,37},{6,38},{7,39},{8,40},{9,... | collective-permute-start | bytes 1572872 | tf_op jit(solution)/shard_map/ppermute | solution.py:44
  37.0 14.8 %collective-permute-start.14 = (bf16[8,2,208,128]{3,2,1,0:T(8,128)(2,1)S(1)}, bf16[8,2,208,128]{3,2,1,0:T(8,128)(2,1)S(1)}, u32[]{:S(2)}, u32[]{:S(2)}) collective-permute-start(bf16[8,2,208,128]{3,2,1,0:T(8,128)(2,1)S(1)} %collective-permute-done.11.refs_5_.refs_8_), channel_id=1, source_target_pairs={{0,8},{1,3},{2,10},{3,5},{4,12},{5,7},{6,14},{7,1},{8,16},{9,11},{... | collective-permute-start | bytes 2555912 | tf_op jit(solution)/shard_map/ppermute | solution.py:44
  45.8 401.2 %collective-permute-start.17 = (bf16[8,2,208,128]{3,2,1,0:T(8,128)(2,1)S(1)}, bf16[8,2,208,128]{3,2,1,0:T(8,128)(2,1)S(1)}, u32[]{:S(2)}, u32[]{:S(2)}) collective-permute-start(bf16[8,2,208,128]{3,2,1,0:T(8,128)(2,1)S(1)} %pad_maximum_fusion.1.refs_5_.refs_7_), channel_id=1, source_target_pairs={{0,24},{1,7},{2,26},{3,1},{4,28},{5,3},{6,30},{7,5},{8,0},{9,15},{... | collective-permute-start | bytes 2555912 | tf_op jit(solution)/shard_map/ppermute | solution.py:44
  45.8 404.5 %collective-permute-start.16 = (bf16[8,2,208,128]{3,2,1,0:T(8,128)(2,1)S(1)}, bf16[8,2,208,128]{3,2,1,0:T(8,128)(2,1)S(1)}, u32[]{:S(2)}, u32[]{:S(2)}) collective-permute-start(bf16[8,2,208,128]{3,2,1,0:T(8,128)(2,1)S(1)} %pad_maximum_fusion.1.refs_5_.refs_7_), channel_id=1, source_target_pairs={{0,8},{1,3},{2,10},{3,5},{4,12},{5,7},{6,14},{7,1},{8,16},{9,11},{... | collective-permute-start | bytes 2555912 | tf_op jit(solution)/shard_map/ppermute | solution.py:44
  51.8 395.2 %copy-start.3 = (bf16[128,2048]{1,0:T(8,128)(2,1)}, bf16[128,2048]{1,0:T(8,128)(2,1)S(1)}, u32[]{:S(2)}) copy-start(bf16[128,2048]{1,0:T(8,128)(2,1)S(1)} %collective-permute-done.13) | copy-start | bytes 1572868
  446.9 1.9 collective-permute-start.15
  446.9 18.0 %collective-permute-start.19 = (bf16[8,2,208,128]{3,2,1,0:T(8,128)(2,1)S(1)}, bf16[8,2,208,128]{3,2,1,0:T(8,128)(2,1)S(1)}, u32[]{:S(2)}, u32[]{:S(2)}) collective-permute-start(bf16[8,2,208,128]{3,2,1,0:T(8,128)(2,1)S(1)} %collective-permute-done.17.refs_7_.refs_9_), channel_id=1, source_target_pairs={{0,24},{1,7},{2,26},{3,1},{4,28},{5,3},{6,30},{7,5},{8,0},{9,15},{... | collective-permute-start | bytes 2555912 | tf_op jit(solution)/shard_map/ppermute | solution.py:44
  450.3 14.7 %collective-permute-start.18 = (bf16[128,2048]{1,0:T(8,128)(2,1)S(1)}, bf16[128,2048]{1,0:T(8,128)(2,1)S(1)}, u32[]{:S(2)}, u32[]{:S(2)}) collective-permute-start(bf16[128,2048]{1,0:T(8,128)(2,1)S(1)} %fusion), channel_id=1, source_target_pairs={{0,32},{1,33},{2,34},{3,35},{4,36},{5,37},{6,38},{7,39},{8,40},{9,... | collective-permute-start | bytes 1572872 | tf_op jit(solution)/shard_map/ppermute | solution.py:44
  459.4 401.7 %copy-start.4 = (bf16[128,2048]{1,0:T(8,128)(2,1)S(1)}, bf16[128,2048]{1,0:T(8,128)(2,1)}, u32[]{:S(2)}) copy-start(bf16[128,2048]{1,0:T(8,128)(2,1)} %copy-done.3) | copy-start | bytes 1572868
  859.5 1.6 collective-permute-start.20

commit v6 on v5

--- a/solution.py
+++ b/solution.py
@@ -69,6 +69,14 @@
     return seq >> 3, (seq >> 1) & 3, seq & 1
 
 
+def first_exchange(value):
+    return moved(value, lambda y, z, x, c: (y, z, x ^ 1, c) if c == 0 else (y, z ^ 1, x, c))
+
+
+def second_exchange(value):
+    return moved(value, lambda y, z, x, c: (y, z, 3 - x, c) if c == 0 else (y, 3 - z, x, c))
+
+
 def chip_of(place, row, col):
     z, x, c = place
     dz = jnp.where(c == 0, row, col)
@@ -76,7 +84,7 @@
     return ((z + dz + 4) % 4) * 4 + (x + dx + 4) % 4
 
 
-def stage_kernel(rows_of, pieces, has_carry, last, *refs):
+def stage_kernel(rows_of, pieces, has_carry, last, paired, *refs):
     refs = list(refs)
     table_ref, len_ref, start_ref = refs[:3]
     q_refs, refs = refs[3:5], refs[5:]
@@ -101,8 +109,13 @@
     chip = place[0] * 4 + place[1]
     first_open = CACHE - start_ref[0]
 
+    sign = 1
+    if paired:
+        sign = 2 * (jnp.where(core == 0, place[1], place[0]) & 1) - 1
+
     def shard_at(row, k, e):
-        return 2 * chip_of(place, row, OFFSETS[k]) + (core if e == 0 else 1 - core)
+        step = OFFSETS[k] * sign if k in (1, 2) else OFFSETS[k]
+        return 2 * chip_of(place, row, step) + (core if e == 0 else 1 - core)
 
     for n in range(count):
         base = n * CHUNK
@@ -232,12 +245,12 @@
 
             @pl.when(strange > 0.0)
             def _():
-                careful(q, mine, place, first_open, table_ref, len_ref, last, all_refs,
+                careful(q, mine, place, sign, first_open, table_ref, len_ref, last, all_refs,
                         queries, total_ref, held, top)
                 write_out()
 
 
-def careful(q, mine, place, first_open, table_ref, len_ref, parts, all_refs, queries, total_ref, held, top):
+def careful(q, mine, place, sign, first_open, table_ref, len_ref, parts, all_refs, queries, total_ref, held, top):
     core = place[2]
     total_ref[q] = jnp.zeros((ROWS, 2 * DIM), jnp.float32)
     top[...] = jnp.full((ROWS, DIM), -jnp.inf, jnp.float32)
@@ -272,7 +285,7 @@
             def unit(u, _, ref=ref, row=row, begin=begin):
                 pltpu.sync_copy(ref.at[u], held)
                 k, e = (begin + u) >> 1, (begin + u) & 1
-                there = chip_of(place, row, jnp.where(k < 2, -k, k - 1))
+                there = chip_of(place, row, jnp.where(k == 3, 2, jnp.where(k < 2, -k, k - 1) * sign))
                 shard = 2 * there + jnp.where(e == 0, core, 1 - core)
                 token = lax.broadcasted_iota(jnp.int32, (TOK, TOK), 0)
                 key = lax.broadcasted_iota(jnp.int32, (TOK, TOK), 1)
@@ -288,7 +301,7 @@
             begin += units
 
 
-def stage(rows_of, last, scalars, queries, chunks, carry=None):
+def stage(rows_of, last, scalars, queries, chunks, carry=None, paired=False):
     smem = pl.BlockSpec(memory_space=pltpu.SMEM)
     vmem = pl.BlockSpec(memory_space=pltpu.VMEM)
     anywhere = pl.BlockSpec(memory_space=pl.ANY)
@@ -326,7 +339,7 @@
         out_shape = jax.ShapeDtypeStruct(*total)
         out_specs = vmem
     return pl.pallas_call(
-        functools.partial(stage_kernel, tuple(rows_of), tuple(pieces), carry is not None, every),
+        functools.partial(stage_kernel, tuple(rows_of), tuple(pieces), carry is not None, every, paired),
         out_shape=out_shape,
         in_specs=specs,
         out_specs=out_specs,
@@ -345,46 +358,46 @@
     return lax.optimization_barrier((value, after))[0]
 
 
-def split_kernel(span_ref, cache_ref, queries_ref, stream_ref, *outs):
-    own, own_q, pack, same, cross, same_q, cross_q, late_stream = outs
+def pairs_at(span_ref, cache_ref, head, out):
+    columns = pl.ds(pl.multiple_of(head * DIM, DIM), DIM)
+    for i in range(2):
+        begin = i * (TOK + LIVE)
+        out[begin : begin + TOK, :] = span_ref[i, :, columns]
+        out[begin + TOK : begin + TOK + LIVE, :] = cache_ref[i, :LIVE, columns]
+
+
+def queries_at(queries_ref, head, out, at):
+    for h in range(GROUP):
+        columns = pl.ds(pl.multiple_of((head * GROUP + h) * DIM, DIM), DIM)
+        out[at + h * TOK : at + (h + 1) * TOK, :] = queries_ref[:, columns]
+
+
+def near_kernel(span_ref, cache_ref, queries_ref, own, own_q, pack, same, cross):
     core = own_place()[2]
-    width = GROUP * DIM
-
-    def pairs_at(head, out):
-        columns = pl.ds(pl.multiple_of(head * DIM, DIM), DIM)
-        for i in range(2):
-            begin = i * (TOK + LIVE)
-            out[begin : begin + TOK, :] = span_ref[i, :, columns]
-            out[begin + TOK : begin + TOK + LIVE, :] = cache_ref[i, :LIVE, columns]
-
-    def queries_at(head, out, at):
-        for h in range(GROUP):
-            columns = pl.ds(pl.multiple_of(head * width + h * DIM, DIM), DIM)
-            out[at + h * TOK : at + (h + 1) * TOK, :] = queries_ref[:, columns]
-
-    pairs_at(core, own)
-    queries_at(core, own_q, 0)
-    pairs_at(1 - core, pack)
-    queries_at(1 - core, pack, PAIR)
-    pairs_at(2 + core, same)
-    queries_at(2 + core, same_q, 0)
-    late_stream[...] = stream_ref[:, 2 * width :]
-    pairs_at(3 - core, cross)
-    queries_at(3 - core, cross_q, 0)
-
-
-def split(span, cache, queries, stream):
-    vmem = pl.BlockSpec(memory_space=pltpu.VMEM)
-    shapes = [(PAIR, DIM), (ROWS, DIM), (PAIR + ROWS, DIM)] + [(PAIR, DIM)] * 2
-    shapes += [(ROWS, DIM)] * 2 + [(TOK, 2 * GROUP * DIM)]
+    for head, out in ((core, own), (1 - core, pack), (2 + core, same), (3 - core, cross)):
+        pairs_at(span_ref, cache_ref, head, out)
+    queries_at(queries_ref, core, own_q, 0)
+    queries_at(queries_ref, 1 - core, pack, PAIR)
+
+
+def late_kernel(queries_ref, stream_ref, same_q, cross_q, late_stream):
+    core = own_place()[2]
+    queries_at(queries_ref, core, same_q, 0)
+    queries_at(queries_ref, 1 - core, cross_q, 0)
+    late_stream[...] = stream_ref[...]
+
+
+def cut(kernel, operands, specs, shapes):
+    whole = lambda shape: pl.BlockSpec(shape, lambda i: (0,) * len(shape))
     return pl.pallas_call(
-        split_kernel,
+        kernel,
+        grid=(1,),
         out_shape=tuple(jax.ShapeDtypeStruct(shape, jnp.bfloat16) for shape in shapes),
-        in_specs=[vmem] * 4,
-        out_specs=(vmem,) * len(shapes),
+        in_specs=specs,
+        out_specs=tuple(whole(shape) for shape in shapes),
         cost_estimate=pl.CostEstimate(flops=0, bytes_accessed=8 * 1024 * 1024, transcendentals=0),
-        name="split",
-    )(span, cache, queries, stream)
+        name=kernel.__name__,
+    )(*operands)
 
 
 def unit_of(first, second):
@@ -396,30 +409,42 @@
     scalars = (block_table, cache_len, context_start)
     width = GROUP * DIM
 
-    mine, q_mine, theirs, late_same, late_cross, q_same, q_cross, late_stream = split(
-        span_kv[0], cache_kv[0], queries[0], stream[0]
+    half = 2 * width
+    left = pl.BlockSpec((TOK, half), lambda i: (0, 0))
+    right = pl.BlockSpec((TOK, half), lambda i: (0, 1))
+    mine, q_mine, theirs, late_same, late_cross = cut(
+        near_kernel,
+        (span_kv[0], cache_kv[0], queries[0]),
+        [pl.BlockSpec((2, TOK, 4 * DIM), lambda i: (0, 0, 0))] * 2 + [left],
+        [(PAIR, DIM), (ROWS, DIM), (PAIR + ROWS, DIM)] + [(PAIR, DIM)] * 2,
     )
     received = swapped(theirs)
     near_unit = unit_of(mine, received)
     near_q = (q_mine, received)
+    late_queries, late_base = ordered((queries[0], stream[0]), near_unit)
+    q_same, q_cross, late_stream = cut(
+        late_kernel, (late_queries, late_base), [right, right], [(ROWS, DIM)] * 2 + [(TOK, half)]
+    )
     near_pieces = [first_ring(near_unit, -k) for k in OFFSETS[1:]]
     late_parts = (up(late_same), up_swapped(late_cross))
-    near_pieces, late_parts = lax.optimization_barrier((near_pieces, late_parts))
+    near_pieces, late_parts, (q_same, q_cross) = lax.optimization_barrier(
+        (near_pieces, late_parts, (q_same, q_cross))
+    )
     near_row = jnp.concatenate([near_unit] + near_pieces)
     near = {0: [near_row], -1: [second_ring(near_row, 1)], 1: [second_ring(near_row, -1)]}
 
-    q_same, q_cross = ordered((q_same, q_cross), near_row)
+    late_parts, q_same, q_cross = ordered((late_parts, q_same, q_cross), near_row)
+    late_unit = unit_of(*late_parts)
     late_q = (up(q_same), up_swapped(q_cross))
-    near_sum = stage((0,), False, scalars, near_q, near)
-    late_q = ordered(late_q, near_sum)
-    late_unit = unit_of(*ordered(late_parts, near_sum))
-    late_pieces = [first_ring(late_unit, -k) for k in OFFSETS[1:]]
+    late_mate = first_exchange(late_unit)
+    near_sum = stage((0,), False, scalars, ordered(near_q, late_unit), near)
+    late_pair = jnp.concatenate([late_unit, ordered(late_mate, near_sum)])
+    late_others = second_exchange(late_pair)
     late_stream = up(ordered(late_stream, near_sum))
     near[-1] = ordered(near[-1], near_sum)
     near[2] = [second_ring(near[-1][0], 1)]
-    near_sum = stage((-1, 1), False, scalars, ordered(near_q, late_unit, late_q), near, near_sum)
-    late_pieces = ordered(late_pieces, near_sum)
-    late_row = jnp.concatenate([late_unit] + late_pieces)
+    near_sum = stage((-1, 1), False, scalars, ordered(near_q, late_q, late_pair), near, near_sum)
+    late_row = jnp.concatenate([late_pair, ordered(late_others, near_sum)])
     late = {0: [late_row], -1: [second_ring(late_row, 1)], 1: [second_ring(late_row, -1)]}
     own, other = stage((2,), True, scalars, ordered(near_q, late_row, late_stream), near, near_sum)
     late[1] = ordered(late[1], own)
@@ -434,9 +459,9 @@
 
     near_done = added(own, other, stream[0, :, : 2 * width])
     near_out = up(near_done)
-    late_sum = stage((0, -1, 1), False, scalars, ordered(late_q, near_done), late)
+    late_sum = stage((0, -1, 1), False, scalars, ordered(late_q, near_done), late, paired=True)
     late_sum, near_out = lax.optimization_barrier((late_sum, near_out))
-    own, other = stage((2,), True, scalars, late_q, late, late_sum)
+    own, other = stage((2,), True, scalars, late_q, late, late_sum, paired=True)
     late_out = added(own, other, late_stream)
     return jnp.concatenate([near_out, late_out], 1)[None]
 

time: 873 us -> 871 us (level)
    ppermute x21 -> x20, waiting for transfers between devices: 26.7 us -> 18.5 us  [moved(): return lax.ppermute(value, AXES, pairs)]
    ppermute x21 -> x20, starting transfers between devices: 17.8 us -> 18.4 us  [moved(): return lax.ppermute(value, AXES, pairs)]
  transfers between devices with their start and end apart: 21 -> 20, of which waited for: 9 -> 7; matrix products, arithmetic and copies ran while one was open for 0% -> 0% of each run, Pallas kernels for 48% -> 49%
where the time goes in v6:
time: 871 us; the launch traced here: 858 us
  Pallas kernels  814 us (93%)
  waiting for transfers between devices  18.5 us (2%)
  starting transfers between devices  18.4 us (2%)
    pallas_call x5, Pallas kernels, stage(): pl.pallas_call(functools.partial(stage_kernel, tuple(rows_of), tuple(piec...  810 us
    ppermute x20, waiting for transfers between devices, moved(): return lax.ppermute(value, AXES, pairs)  18.5 us
    ppermute x20, starting transfers between devices, moved(): return lax.ppermute(value, AXES, pairs)  18.4 us
  transfers between devices with their start and end apart: 20, of which 7 were waited for; matrix products, arithmetic and copies ran while one was open for 0% of the time, Pallas kernels for 49%

profile of v6, /device:TPU:103, one launch (start us, length us, event | category | flops | bytes accessed | tf_op | source)
XLA Modules:
  0.0 858.3 jit_solution(10831646763051770795)
XLA Ops:
  0.0 2.3 near_kernel.1
  2.3 0.7 collective-permute-start
  3.0 1.5 collective-permute-done.refs_4_
  4.5 0.9 pad_maximum_fusion.3
  5.5 1.5 collective-permute-start.2
  7.0 0.4 collective-permute-start.3
  7.4 1.3 collective-permute-start.4
  8.7 3.4 collective-permute-start.5
  12.1 2.3 late_kernel.1
  14.4 2.8 collective-permute-done.5
  17.3 1.9 collective-permute-start.10
  20.2 2.7 collective-permute-start.7
  22.9 4.6 stage_0.1.refs_7_
  27.7 1.3 collective-permute-start.9
  29.0 8.4 collective-permute-done.7.refs_4_
  37.4 1.2 collective-permute-start.13
  38.6 7.1 stage_3_1.1.refs_6_
  45.9 2.7 collective-permute-start.15
  48.6 0.6 collective-permute-done.13.refs_5_.refs_10_
  49.2 394.4 %stage_2.2 = (bf16[128,1024]{1,0:T(8,128)(2,1)S(1)}, bf16[128,1024]{1,0:T(8,128)(2,1)}) custom-call(s32[32,32]{1,0:T(8,128)S(1)} %copy-done.5, s32[32]{0:T(128)S(1)} %copy-done.6, s32[1]{0:T(128)S(6)} %copy.8.refs_2_, bf16[1024,128]{1,0:T(8,128)(2,1)S(1)} %copy-done, bf16[1440,128]{1,0:T(8,128)(2,1)S(1)} %collective-permute-done.refs_4_, ...), custom_call_target="tpu_custom_call" | custom-call | flops 2617245696 | bytes 851968 | tf_op jit(solution)/shard_map/stage_2/pallas_call | solution.py:341
  443.7 0.4 collective-permute-start.18
  444.1 1.3 collective-permute-done.14
  445.4 1.3 fusion
  446.8 0.9 copy-done.2
  447.7 0.9 copy-done.4
  448.7 10.1 %stage_0_3_1.1.refs_6_ = f32[2,1024,256]{2,1,0:T(8,128)S(1)} custom-call(s32[32,32]{1,0:T(8,128)S(1)} %copy-done.5, s32[32]{0:T(128)S(1)} %copy-done.6, s32[1]{0:T(128)S(6)} %copy.8.refs_2_, bf16[1024,128]{1,0:T(8,128)(2,1)S(1)} %copy-done.2, bf16[1024,128]{1,0:T(8,128)(2,1)S(1)} %copy-done.4, ...), custom_call_target="tpu_custom_call" | custom-call | flops 7851737088 | bytes 2555904 | tf_op jit(solution)/shard_map/stage_0_3_1/pallas_call | solution.py:341
  458.8 2.6 collective-permute-done.17
  461.4 393.6 %stage_2.3 = (bf16[128,1024]{1,0:T(8,128)(2,1)S(1)}, bf16[128,1024]{1,0:T(8,128)(2,1)S(1)}) custom-call(s32[32,32]{1,0:T(8,128)S(1)} %copy-done.5, s32[32]{0:T(128)S(1)} %copy-done.6, s32[1]{0:T(128)S(6)} %copy.8.refs_2_, bf16[1024,128]{1,0:T(8,128)(2,1)S(1)} %copy-done.2, bf16[1024,128]{1,0:T(8,128)(2,1)S(1)} %copy-done.4, ...), custom_call_target="tpu_custom_call" | custom-call | flops 2617245696 | bytes 851968 | tf_op jit(solution)/shard_map/stage_2/pallas_call | solution.py:341
  854.9 0.4 collective-permute-start.19
  855.3 1.2 collective-permute-done.19
  856.5 0.2 add_convert_fusion
  856.8 1.1 maximum_bitcast_fusion
  (48 shorter events, 0.9 us)
Async XLA Ops:
  2.3 2.2 collective-permute-start
  5.4 11.8 %collective-permute-start.1 = (bf16[2,2,208,128]{3,2,1,0:T(8,128)(2,1)S(1)}, bf16[2,2,208,128]{3,2,1,0:T(8,128)(2,1)S(1)}, u32[]{:S(2)}, u32[]{:S(2)}) collective-permute-start(bf16[2,2,208,128]{3,2,1,0:T(8,128)(2,1)S(1)} %bitcast.17), channel_id=1, source_target_pairs={{0,2},{1,9},{2,4},{3,11},{4,6},{5,13},{6,0},{7,15},{8,10},{9,17},{... | collective-permute-start | bytes 638984 | tf_op jit(solution)/shard_map/ppermute | solution.py:44
  5.5 11.7 %collective-permute-start.2 = (bf16[2,2,208,128]{3,2,1,0:T(8,128)(2,1)S(1)}, bf16[2,2,208,128]{3,2,1,0:T(8,128)(2,1)S(1)}, u32[]{:S(2)}, u32[]{:S(2)}) collective-permute-start(bf16[2,2,208,128]{3,2,1,0:T(8,128)(2,1)S(1)} %bitcast.18), channel_id=1, source_target_pairs={{0,6},{1,25},{2,0},{3,27},{4,2},{5,29},{6,4},{7,31},{8,14},{9,1},{... | collective-permute-start | bytes 638984 | tf_op jit(solution)/shard_map/ppermute | solution.py:44
  7.0 10.2 %collective-permute-start.3 = (bf16[2,2,208,128]{3,2,1,0:T(8,128)(2,1)S(1)}, bf16[2,2,208,128]{3,2,1,0:T(8,128)(2,1)S(1)}, u32[]{:S(2)}, u32[]{:S(2)}) collective-permute-start(bf16[2,2,208,128]{3,2,1,0:T(8,128)(2,1)S(1)} %bitcast.19), channel_id=1, source_target_pairs={{0,4},{1,17},{2,6},{3,19},{4,0},{5,21},{6,2},{7,23},{8,12},{9,25},... | collective-permute-start | bytes 638984 | tf_op jit(solution)/shard_map/ppermute | solution.py:44
  7.4 7.0 collective-permute-start.4
  8.7 8.5 collective-permute-start.5
  12.1 10.9 %copy-start = (bf16[1024,128]{1,0:T(8,128)(2,1)S(1)}, bf16[1024,128]{1,0:T(8,128)(2,1)}, u32[]{:S(2)}) copy-start(bf16[1024,128]{1,0:T(8,128)(2,1)} %get-tuple-element.74.refs_3_) | copy-start | bytes 786436
  12.1 10.9 %copy-start.5 = (s32[32,32]{1,0:T(8,128)S(1)}, s32[32,32]{1,0:T(8,128)}, u32[]{:S(2)}) copy-start(s32[32,32]{1,0:T(8,128)} %refs_0_.9) | copy-start | bytes 12292
  12.1 10.9 %copy-start.6 = (s32[32]{0:T(128)S(1)}, s32[32]{0:T(128)}, u32[]{:S(2)}) copy-start(s32[32]{0:T(128)} %refs_1_.9) | copy-start | bytes 388
  14.4 5.7 copy-start.11
  14.4 5.8 copy-start.10
  17.3 20.1 %collective-permute-start.10 = (bf16[8,2,208,128]{3,2,1,0:T(8,128)(2,1)S(1)}, bf16[8,2,208,128]{3,2,1,0:T(8,128)(2,1)S(1)}, u32[]{:S(2)}, u32[]{:S(2)}) collective-permute-start(bf16[8,2,208,128]{3,2,1,0:T(8,128)(2,1)S(1)} %pad_maximum_fusion.refs_5_.refs_7_), channel_id=1, source_target_pairs={{0,8},{1,3},{2,10},{3,5},{4,12},{5,7},{6,14},{7,1},{8,16},{9,11},{... | collective-permute-start | bytes 2555912 | tf_op jit(solution)/shard_map/ppermute | solution.py:44
  19.2 19.4 %collective-permute-start.11 = (bf16[8,2,208,128]{3,2,1,0:T(8,128)(2,1)S(1)}, bf16[8,2,208,128]{3,2,1,0:T(8,128)(2,1)S(1)}, u32[]{:S(2)}, u32[]{:S(2)}) collective-permute-start(bf16[8,2,208,128]{3,2,1,0:T(8,128)(2,1)S(1)} %pad_maximum_fusion.refs_5_.refs_7_), channel_id=1, source_target_pairs={{0,24},{1,7},{2,26},{3,1},{4,28},{5,3},{6,30},{7,5},{8,0},{9,15},{... | collective-permute-start | bytes 2555912 | tf_op jit(solution)/shard_map/ppermute | solution.py:44
  19.9 7.7 collective-permute-start.8
  20.1 7.5 copy-start.9
  20.1 7.6 collective-permute-start.6
  20.2 17.2 %collective-permute-start.7 = (bf16[1024,128]{1,0:T(8,128)(2,1)S(1)}, bf16[1024,128]{1,0:T(8,128)(2,1)S(1)}, u32[]{:S(2)}, u32[]{:S(2)}) collective-permute-start(bf16[1024,128]{1,0:T(8,128)(2,1)S(1)} %copy-done.10), channel_id=1, source_target_pairs={{0,33},{1,32},{2,35},{3,34},{4,37},{5,36},{6,39},{7,38},{8,41},{9,... | collective-permute-start | bytes 786440 | tf_op jit(solution)/shard_map/ppermute | solution.py:44
  27.6 21.0 %collective-permute-start.12 = (bf16[128,2048]{1,0:T(8,128)(2,1)S(1)}, bf16[128,2048]{1,0:T(8,128)(2,1)S(1)}, u32[]{:S(2)}, u32[]{:S(2)}) collective-permute-start(bf16[128,2048]{1,0:T(8,128)(2,1)S(1)} %copy-done.9), channel_id=1, source_target_pairs={{0,32},{1,33},{2,34},{3,35},{4,36},{5,37},{6,38},{7,39},{8,40},{9,... | collective-permute-start | bytes 1572872 | tf_op jit(solution)/shard_map/ppermute | solution.py:44
  27.7 18.0 %copy-start.1 = (bf16[1024,128]{1,0:T(8,128)(2,1)}, bf16[1024,128]{1,0:T(8,128)(2,1)S(1)}, u32[]{:S(2)}) copy-start(bf16[1024,128]{1,0:T(8,128)(2,1)S(1)} %collective-permute-done.6.refs_3_) | copy-start | bytes 786436
  27.7 18.0 %collective-permute-start.9 = (bf16[4,2,208,128]{3,2,1,0:T(8,128)(2,1)S(1)}, bf16[4,2,208,128]{3,2,1,0:T(8,128)(2,1)S(1)}, u32[]{:S(2)}, u32[]{:S(2)}) collective-permute-start(bf16[4,2,208,128]{3,2,1,0:T(8,128)(2,1)S(1)} %pad_maximum_fusion.2), channel_id=1, source_target_pairs={{0,6},{1,25},{2,4},{3,27},{4,2},{5,29},{6,0},{7,31},{8,14},{9,17},... | collective-permute-start | bytes 1277960 | tf_op jit(solution)/shard_map/ppermute | solution.py:44
  37.4 8.3 copy-start.3
  37.4 11.8 %collective-permute-start.13 = (bf16[8,2,208,128]{3,2,1,0:T(8,128)(2,1)S(1)}, bf16[8,2,208,128]{3,2,1,0:T(8,128)(2,1)S(1)}, u32[]{:S(2)}, u32[]{:S(2)}) collective-permute-start(bf16[8,2,208,128]{3,2,1,0:T(8,128)(2,1)S(1)} %collective-permute-done.10.refs_5_.refs_8_), channel_id=1, source_target_pairs={{0,8},{1,3},{2,10},{3,5},{4,12},{5,7},{6,14},{7,1},{8,16},{9,11},{... | collective-permute-start | bytes 2555912 | tf_op jit(solution)/shard_map/ppermute | solution.py:44
  45.8 397.8 %collective-permute-start.16 = (bf16[8,2,208,128]{3,2,1,0:T(8,128)(2,1)S(1)}, bf16[8,2,208,128]{3,2,1,0:T(8,128)(2,1)S(1)}, u32[]{:S(2)}, u32[]{:S(2)}) collective-permute-start(bf16[8,2,208,128]{3,2,1,0:T(8,128)(2,1)S(1)} %pad_maximum_fusion.1.refs_5_.refs_7_), channel_id=1, source_target_pairs={{0,24},{1,7},{2,26},{3,1},{4,28},{5,3},{6,30},{7,5},{8,0},{9,15},{... | collective-permute-start | bytes 2555912 | tf_op jit(solution)/shard_map/ppermute | solution.py:44
  45.9 400.8 %collective-permute-start.15 = (bf16[8,2,208,128]{3,2,1,0:T(8,128)(2,1)S(1)}, bf16[8,2,208,128]{3,2,1,0:T(8,128)(2,1)S(1)}, u32[]{:S(2)}, u32[]{:S(2)}) collective-permute-start(bf16[8,2,208,128]{3,2,1,0:T(8,128)(2,1)S(1)} %pad_maximum_fusion.1.refs_5_.refs_7_), channel_id=1, source_target_pairs={{0,8},{1,3},{2,10},{3,5},{4,12},{5,7},{6,14},{7,1},{8,16},{9,11},{... | collective-permute-start | bytes 2555912 | tf_op jit(solution)/shard_map/ppermute | solution.py:44
  48.6 395.1 %copy-start.7 = (bf16[128,2048]{1,0:T(8,128)(2,1)}, bf16[128,2048]{1,0:T(8,128)(2,1)S(1)}, u32[]{:S(2)}) copy-start(bf16[128,2048]{1,0:T(8,128)(2,1)S(1)} %collective-permute-done.12) | copy-start | bytes 1572868
  443.7 1.7 collective-permute-start.14
  443.7 17.7 %collective-permute-start.18 = (bf16[8,2,208,128]{3,2,1,0:T(8,128)(2,1)S(1)}, bf16[8,2,208,128]{3,2,1,0:T(8,128)(2,1)S(1)}, u32[]{:S(2)}, u32[]{:S(2)}) collective-permute-start(bf16[8,2,208,128]{3,2,1,0:T(8,128)(2,1)S(1)} %collective-permute-done.16.refs_7_.refs_9_), channel_id=1, source_target_pairs={{0,24},{1,7},{2,26},{3,1},{4,28},{5,3},{6,30},{7,5},{8,0},{9,15},{... | collective-permute-start | bytes 2555912 | tf_op jit(solution)/shard_map/ppermute | solution.py:44
  446.7 14.7 %collective-permute-start.17 = (bf16[128,2048]{1,0:T(8,128)(2,1)S(1)}, bf16[128,2048]{1,0:T(8,128)(2,1)S(1)}, u32[]{:S(2)}, u32[]{:S(2)}) collective-permute-start(bf16[128,2048]{1,0:T(8,128)(2,1)S(1)} %fusion), channel_id=1, source_target_pairs={{0,32},{1,33},{2,34},{3,35},{4,36},{5,37},{6,38},{7,39},{8,40},{9,... | collective-permute-start | bytes 1572872 | tf_op jit(solution)/shard_map/ppermute | solution.py:44
  446.8 1.0 copy-start.2
  447.7 0.9 copy-start.4
  458.8 397.8 %copy-start.8 = (bf16[128,2048]{1,0:T(8,128)(2,1)S(1)}, bf16[128,2048]{1,0:T(8,128)(2,1)}, u32[]{:S(2)}) copy-start(bf16[128,2048]{1,0:T(8,128)(2,1)} %copy-done.7) | copy-start | bytes 1572868
  854.9 1.6 collective-permute-start.19

commit v7 on v6

--- a/solution.py
+++ b/solution.py
@@ -102,7 +102,7 @@
             refs = refs[len(part) :]
     if last:
         out_refs, refs = refs[:2], refs[2:]
-    total_ref, keys, values, todo = refs[:4]
+    total_ref, keys, values, todo, asked, arrived = refs[:6]
     count = len(rows_of)
     place = own_place()
     core = place[2]
@@ -116,6 +116,12 @@
     def shard_at(row, k, e):
         step = OFFSETS[k] * sign if k in (1, 2) else OFFSETS[k]
         return 2 * chip_of(place, row, step) + (core if e == 0 else 1 - core)
+
+    fetches = []
+    for q in range(2):
+        rows = pl.ds(q_refs[q].shape[0] - ROWS, ROWS)
+        fetches.append(pltpu.make_async_copy(q_refs[q].at[rows, :], asked.at[q], arrived.at[q]))
+        fetches[q].start()
 
     for n in range(count):
         base = n * CHUNK
@@ -142,9 +148,13 @@
 
     for q in range(2):
         mine = 2 * chip + (core if q == 0 else 1 - core)
-        queries = q_refs[q].at[pl.ds(q_refs[q].shape[0] - ROWS, ROWS), :]
+        queries = asked.at[q]
+        fetches[q].wait()
 
         filled = jnp.int32(0)
+        if rows_of[0] == 0:
+            todo[0] = q * TOK
+            filled = jnp.int32(1)
         for n in range(count):
             seen = []
             for k in range(PER):
@@ -172,29 +182,22 @@
         def mix(weights, rows):
             return jnp.dot(weights.astype(jnp.bfloat16), rows, preferred_element_type=jnp.float32)
 
-        if rows_of[0] == 0:
-            at = q * TOK
-            token = lax.broadcasted_iota(jnp.int32, (TOK, TOK), 0)
-            key = lax.broadcasted_iota(jnp.int32, (TOK, TOK), 1)
-            behind = (key <= token)[None]
-            for first in range(0, ROWS, SUB):
-                weights = jnp.exp2(scores_of(first, keys[at : at + TOK, :]) * TO_LOG2)
-                weights = jnp.where(behind, weights.reshape(SUB // TOK, TOK, TOK), 0.0).reshape(SUB, TOK)
-                part = mix(weights, values[at : at + TOK, :])
-                if has_carry:
-                    part = part + carry_ref[q, first : first + SUB, :]
-                total_ref[q, first : first + SUB, :] = part
-        else:
-            total_ref[q] = carry_ref[q]
-
-        def tile(blocks, begin):
+        def tile(blocks, begin, opening=False):
             spots = [pl.multiple_of(todo[begin + b], BLOCK) for b in range(blocks)]
             key_rows = jnp.concatenate([keys[pl.ds(s, BLOCK), :] for s in spots], 0)
             value_rows = jnp.concatenate([values[pl.ds(s, BLOCK), :] for s in spots], 0)
 
             def finish(first, scores):
                 weights = jnp.exp2(scores * TO_LOG2)
-                total_ref[q, first : first + SUB, :] += mix(weights, value_rows)
+                if opening:
+                    token = lax.broadcasted_iota(jnp.int32, (TOK, TOK), 0)
+                    key = lax.broadcasted_iota(jnp.int32, (TOK, TOK), 1)
+                    own = weights[:, :TOK].reshape(SUB // TOK, TOK, TOK)
+                    own = jnp.where((key <= token)[None], own, 0.0).reshape(SUB, TOK)
+                    weights = jnp.concatenate([own, weights[:, TOK:]], 1)
+                    total_ref[q, first : first + SUB, :] = mix(weights, value_rows)
+                else:
+                    total_ref[q, first : first + SUB, :] += mix(weights, value_rows)
 
             held = None
             for first in range(0, ROWS, SUB):
@@ -204,50 +207,63 @@
                 held = (first, scores)
             finish(*held)
 
+        begin = 0
+        if rows_of[0] == 0:
+            tile(TILE_BLOCKS, 0, opening=True)
+            begin = TILE_BLOCKS
+            filled = jnp.maximum(filled - TILE_BLOCKS, 0)
+        else:
+            total_ref[q] = carry_ref[q]
+
         whole = (filled + 1) // TILE_BLOCKS
         rest = filled - whole * TILE_BLOCKS
 
         def whole_tile(step, _):
-            tile(TILE_BLOCKS, step * TILE_BLOCKS)
+            tile(TILE_BLOCKS, begin + step * TILE_BLOCKS)
             return 0
 
         lax.fori_loop(0, whole, whole_tile, 0)
 
         @pl.when(rest > 2)
         def _():
-            tile(4, whole * TILE_BLOCKS)
+            tile(4, begin + whole * TILE_BLOCKS)
 
         left = jnp.where(rest > 2, rest - 4, rest)
 
         @pl.when(left > 0)
         def _():
-            tile(2, filled - left)
-
-        if last:
-            held, top = refs[4:]
-
-            def write_out():
-                for h in range(GROUP):
-                    mixed = total_ref[q, h * TOK : (h + 1) * TOK, :DIM]
-                    total = total_ref[q, h * TOK : (h + 1) * TOK, DIM:]
-                    out_refs[q][:, h * DIM : (h + 1) * DIM] = (mixed / total).astype(jnp.bfloat16)
-
-            write_out()
-            strange = jnp.zeros((TOK, DIM), jnp.float32)
-            largest = jnp.zeros((TOK, DIM), jnp.float32)
+            tile(2, begin + filled - left)
+
+    if last:
+        held, top = refs[6:]
+        strange = jnp.zeros((TOK, DIM), jnp.float32)
+
+        def write_out(q):
+            for h in range(GROUP):
+                mixed = total_ref[q, h * TOK : (h + 1) * TOK, :DIM]
+                total = total_ref[q, h * TOK : (h + 1) * TOK, DIM:]
+                out_refs[q][:, h * DIM : (h + 1) * DIM] = (mixed / total).astype(jnp.bfloat16)
+
+        largest = []
+        for q in range(2):
+            write_out(q)
+            most = jnp.zeros((TOK, DIM), jnp.float32)
             for h in range(GROUP):
                 mixed = jnp.abs(total_ref[q, h * TOK : (h + 1) * TOK, :DIM])
                 total = total_ref[q, h * TOK : (h + 1) * TOK, DIM:]
                 good = (total >= LEAST_TOTAL) & (total <= MOST_TOTAL) & (mixed <= MOST_MIXED)
                 strange = jnp.where(good, strange, 1.0)
-                largest = jnp.maximum(largest, mixed)
-            strange = jnp.where(jnp.max(largest) >= LEAST_MIXED, jnp.max(strange), 1.0)
-
-            @pl.when(strange > 0.0)
-            def _():
+                most = jnp.maximum(most, mixed)
+            largest.append(jnp.max(most))
+        fine = (jnp.max(strange) == 0.0) & (largest[0] >= LEAST_MIXED) & (largest[1] >= LEAST_MIXED)
+
+        @pl.when(jnp.logical_not(fine))
+        def _():
+            for q in range(2):
+                mine = 2 * chip + (core if q == 0 else 1 - core)
                 careful(q, mine, place, sign, first_open, table_ref, len_ref, last, all_refs,
-                        queries, total_ref, held, top)
-                write_out()
+                        asked.at[q], total_ref, held, top)
+                write_out(q)
 
 
 def careful(q, mine, place, sign, first_open, table_ref, len_ref, parts, all_refs, queries, total_ref, held, top):
@@ -312,7 +328,7 @@
         pieces.append(tuple(part.shape[0] for part in chunks[row]))
     if carry is not None:
         operands.append(carry)
-    specs = [smem] * 3 + [vmem] * (len(operands) - 3)
+    specs = [smem] * 3 + [pl.BlockSpec(memory_space=pltpu.HBM)] * 2 + [vmem] * (len(operands) - 5)
     every = None
     if last:
         every = []
@@ -326,7 +342,9 @@
     scratch = [
         pltpu.VMEM((count * CHUNK + BLOCK, DIM), jnp.bfloat16),
         pltpu.VMEM((count * CHUNK + BLOCK, 2 * DIM), jnp.bfloat16),
-        pltpu.SMEM((count * (PER * 2 + CACHE_ROWS // BLOCK) + TILE_BLOCKS,), jnp.int32),
+        pltpu.SMEM((count * (PER * 2 + CACHE_ROWS // BLOCK) + TILE_BLOCKS + 1,), jnp.int32),
+        pltpu.VMEM((2, ROWS, DIM), jnp.bfloat16),
+        pltpu.SemaphoreType.DMA((2,)),
     ]
     if last:
         out_shape = (jax.ShapeDtypeStruct((TOK, GROUP * DIM), jnp.bfloat16),) * 2
@@ -433,20 +451,22 @@
     near_row = jnp.concatenate([near_unit] + near_pieces)
     near = {0: [near_row], -1: [second_ring(near_row, 1)], 1: [second_ring(near_row, -1)]}
 
-    late_parts, q_same, q_cross = ordered((late_parts, q_same, q_cross), near_row)
+    late_parts, q_same = ordered((late_parts, q_same), near_row)
     late_unit = unit_of(*late_parts)
-    late_q = (up(q_same), up_swapped(q_cross))
+    q_same = up(q_same)
     late_mate = first_exchange(late_unit)
     near_sum = stage((0,), False, scalars, ordered(near_q, late_unit), near)
     late_pair = jnp.concatenate([late_unit, ordered(late_mate, near_sum)])
     late_others = second_exchange(late_pair)
-    late_stream = up(ordered(late_stream, near_sum))
+    q_cross, late_stream = ordered((q_cross, late_stream), near_sum)
+    q_cross, late_stream = up_swapped(q_cross), up(late_stream)
+    late_q = (q_same, q_cross)
     near[-1] = ordered(near[-1], near_sum)
     near[2] = [second_ring(near[-1][0], 1)]
-    near_sum = stage((-1, 1), False, scalars, ordered(near_q, late_q, late_pair), near, near_sum)
+    near_sum = stage((-1, 1), False, scalars, ordered(near_q, late_pair, q_same), near, near_sum)
     late_row = jnp.concatenate([late_pair, ordered(late_others, near_sum)])
     late = {0: [late_row], -1: [second_ring(late_row, 1)], 1: [second_ring(late_row, -1)]}
-    own, other = stage((2,), True, scalars, ordered(near_q, late_row, late_stream), near, near_sum)
+    own, other = stage((2,), True, scalars, ordered(near_q, late_row, late_stream, q_cross), near, near_sum)
     late[1] = ordered(late[1], own)
     late[2] = [second_ring(late[1][0], -1)]
 

time: 871 us -> 872 us (level)
  transfers between devices with their start and end apart: 20 -> 20, of which waited for: 7 -> 8; matrix products, arithmetic and copies ran while one was open for 0% -> 0% of each run, Pallas kernels for 49% -> 49%
where the time goes in v7:
time: 872 us; the launch traced here: 860 us
  Pallas kernels  815 us (93%)
  waiting for transfers between devices  21.3 us (2%)
  starting transfers between devices  16.9 us (2%)
    pallas_call x5, Pallas kernels, stage(): pl.pallas_call(functools.partial(stage_kernel, tuple(rows_of), tuple(piec...  810 us
    ppermute x20, waiting for transfers between devices, moved(): return lax.ppermute(value, AXES, pairs)  21.3 us
  transfers between devices with their start and end apart: 20, of which 8 were waited for; matrix products, arithmetic and copies ran while one was open for 0% of the time, Pallas kernels for 49%

profile of v7, /device:TPU:103, one launch (start us, length us, event | category | flops | bytes accessed | tf_op | source)
XLA Modules:
  0.0 860.4 jit_solution(14174194450304105031)
XLA Ops:
  0.0 2.3 near_kernel.1
  2.3 0.7 collective-permute-start
  3.0 1.5 collective-permute-done.refs_4_
  4.5 0.9 pad_maximum_fusion.3
  5.5 1.5 collective-permute-start.2
  7.0 0.4 collective-permute-start.3
  7.4 1.3 collective-permute-start.4
  8.7 3.4 collective-permute-start.5
  12.1 2.3 late_kernel.1
  14.4 2.8 collective-permute-done.5
  17.3 1.9 collective-permute-start.10
  20.2 4.8 stage_0.1.refs_7_
  25.0 1.2 collective-permute-start.12
  26.2 1.1 collective-permute-done.8
  27.5 4.0 collective-permute-done.10.refs_5_.refs_8_
  31.5 1.0 collective-permute-start.13
  32.5 7.1 stage_3_1.1.refs_6_
  39.7 1.2 collective-permute-start.16
  40.9 2.9 collective-permute-start.15
  43.8 6.7 collective-permute-done.7.refs_4_
  50.5 0.7 copy-done.3
  51.2 394.4 %stage_2.2 = (bf16[128,1024]{1,0:T(8,128)(2,1)S(1)}, bf16[128,1024]{1,0:T(8,128)(2,1)}) custom-call(s32[32,32]{1,0:T(8,128)S(1)} %copy-done.5, s32[32]{0:T(128)S(1)} %copy-done.6, s32[1]{0:T(128)S(6)} %copy.8.refs_2_, bf16[1024,128]{1,0:T(8,128)(2,1)S(1)} %copy-done, bf16[1440,128]{1,0:T(8,128)(2,1)S(1)} %collective-permute-done.refs_4_, ...), custom_call_target="tpu_custom_call" | custom-call | flops 2617245696 | bytes 851968 | tf_op jit(solution)/shard_map/stage_2/pallas_call | solution.py:359
  445.7 0.8 collective-permute-start.18
  446.5 0.9 collective-permute-done.14
  447.4 1.3 fusion
  448.8 0.9 copy-done.2
  449.7 0.9 copy-done.4
  450.7 10.0 %stage_0_3_1.1.refs_6_ = f32[2,1024,256]{2,1,0:T(8,128)S(1)} custom-call(s32[32,32]{1,0:T(8,128)S(1)} %copy-done.5, s32[32]{0:T(128)S(1)} %copy-done.6, s32[1]{0:T(128)S(6)} %copy.8.refs_2_, bf16[1024,128]{1,0:T(8,128)(2,1)S(1)} %copy-done.2, bf16[1024,128]{1,0:T(8,128)(2,1)S(1)} %copy-done.4, ...), custom_call_target="tpu_custom_call" | custom-call | flops 7851737088 | bytes 2555904 | tf_op jit(solution)/shard_map/stage_0_3_1/pallas_call | solution.py:359
  460.7 2.7 collective-permute-done.17
  463.4 393.7 %stage_2.3 = (bf16[128,1024]{1,0:T(8,128)(2,1)S(1)}, bf16[128,1024]{1,0:T(8,128)(2,1)S(1)}) custom-call(s32[32,32]{1,0:T(8,128)S(1)} %copy-done.5, s32[32]{0:T(128)S(1)} %copy-done.6, s32[1]{0:T(128)S(6)} %copy.8.refs_2_, bf16[1024,128]{1,0:T(8,128)(2,1)S(1)} %copy-done.2, bf16[1024,128]{1,0:T(8,128)(2,1)S(1)} %copy-done.4, ...), custom_call_target="tpu_custom_call" | custom-call | flops 2617245696 | bytes 851968 | tf_op jit(solution)/shard_map/stage_2/pallas_call | solution.py:359
  857.2 1.5 collective-permute-done.19
  858.9 1.1 maximum_bitcast_fusion
  (48 shorter events, 1.3 us)
Async XLA Ops:
  2.3 2.2 collective-permute-start
  5.4 11.8 %collective-permute-start.1 = (bf16[2,2,208,128]{3,2,1,0:T(8,128)(2,1)S(1)}, bf16[2,2,208,128]{3,2,1,0:T(8,128)(2,1)S(1)}, u32[]{:S(2)}, u32[]{:S(2)}) collective-permute-start(bf16[2,2,208,128]{3,2,1,0:T(8,128)(2,1)S(1)} %bitcast.17), channel_id=1, source_target_pairs={{0,2},{1,9},{2,4},{3,11},{4,6},{5,13},{6,0},{7,15},{8,10},{9,17},{... | collective-permute-start | bytes 638984 | tf_op jit(solution)/shard_map/ppermute | solution.py:44
  5.5 11.7 %collective-permute-start.2 = (bf16[2,2,208,128]{3,2,1,0:T(8,128)(2,1)S(1)}, bf16[2,2,208,128]{3,2,1,0:T(8,128)(2,1)S(1)}, u32[]{:S(2)}, u32[]{:S(2)}) collective-permute-start(bf16[2,2,208,128]{3,2,1,0:T(8,128)(2,1)S(1)} %bitcast.18), channel_id=1, source_target_pairs={{0,6},{1,25},{2,0},{3,27},{4,2},{5,29},{6,4},{7,31},{8,14},{9,1},{... | collective-permute-start | bytes 638984 | tf_op jit(solution)/shard_map/ppermute | solution.py:44
  7.0 10.2 %collective-permute-start.3 = (bf16[2,2,208,128]{3,2,1,0:T(8,128)(2,1)S(1)}, bf16[2,2,208,128]{3,2,1,0:T(8,128)(2,1)S(1)}, u32[]{:S(2)}, u32[]{:S(2)}) collective-permute-start(bf16[2,2,208,128]{3,2,1,0:T(8,128)(2,1)S(1)} %bitcast.19), channel_id=1, source_target_pairs={{0,4},{1,17},{2,6},{3,19},{4,0},{5,21},{6,2},{7,23},{8,12},{9,25},... | collective-permute-start | bytes 638984 | tf_op jit(solution)/shard_map/ppermute | solution.py:44
  7.4 7.0 collective-permute-start.4
  8.7 8.5 collective-permute-start.5
  12.1 8.1 copy-start
  12.1 8.1 copy-start.5
  12.1 8.1 copy-start.6
  14.4 5.7 copy-start.11
  17.3 14.2 %collective-permute-start.10 = (bf16[8,2,208,128]{3,2,1,0:T(8,128)(2,1)S(1)}, bf16[8,2,208,128]{3,2,1,0:T(8,128)(2,1)S(1)}, u32[]{:S(2)}, u32[]{:S(2)}) collective-permute-start(bf16[8,2,208,128]{3,2,1,0:T(8,128)(2,1)S(1)} %pad_maximum_fusion.refs_5_.refs_7_), channel_id=1, source_target_pairs={{0,8},{1,3},{2,10},{3,5},{4,12},{5,7},{6,14},{7,1},{8,16},{9,11},{... | collective-permute-start | bytes 2555912 | tf_op jit(solution)/shard_map/ppermute | solution.py:44
  19.2 13.3 %collective-permute-start.11 = (bf16[8,2,208,128]{3,2,1,0:T(8,128)(2,1)S(1)}, bf16[8,2,208,128]{3,2,1,0:T(8,128)(2,1)S(1)}, u32[]{:S(2)}, u32[]{:S(2)}) collective-permute-start(bf16[8,2,208,128]{3,2,1,0:T(8,128)(2,1)S(1)} %pad_maximum_fusion.refs_5_.refs_7_), channel_id=1, source_target_pairs={{0,24},{1,7},{2,26},{3,1},{4,28},{5,3},{6,30},{7,5},{8,0},{9,15},{... | collective-permute-start | bytes 2555912 | tf_op jit(solution)/shard_map/ppermute | solution.py:44
  19.9 7.4 collective-permute-start.8
  20.1 4.9 copy-start.9
  20.1 7.4 collective-permute-start.6
  25.0 26.2 %collective-permute-start.12 = (bf16[128,2048]{1,0:T(8,128)(2,1)S(1)}, bf16[128,2048]{1,0:T(8,128)(2,1)S(1)}, u32[]{:S(2)}, u32[]{:S(2)}) collective-permute-start(bf16[128,2048]{1,0:T(8,128)(2,1)S(1)} %copy-done.9), channel_id=1, source_target_pairs={{0,32},{1,33},{2,34},{3,35},{4,36},{5,37},{6,38},{7,39},{8,40},{9,... | collective-permute-start | bytes 1572872 | tf_op jit(solution)/shard_map/ppermute | solution.py:44
  27.3 13.5 %copy-start.10 = (bf16[1024,128]{1,0:T(8,128)(2,1)S(1)}, bf16[1024,128]{1,0:T(8,128)(2,1)}, u32[]{:S(2)}) copy-start(bf16[1024,128]{1,0:T(8,128)(2,1)} %get-tuple-element.67) | copy-start | bytes 786436
  27.4 12.2 %collective-permute-start.9 = (bf16[4,2,208,128]{3,2,1,0:T(8,128)(2,1)S(1)}, bf16[4,2,208,128]{3,2,1,0:T(8,128)(2,1)S(1)}, u32[]{:S(2)}, u32[]{:S(2)}) collective-permute-start(bf16[4,2,208,128]{3,2,1,0:T(8,128)(2,1)S(1)} %pad_maximum_fusion.2), channel_id=1, source_target_pairs={{0,6},{1,25},{2,4},{3,27},{4,2},{5,29},{6,0},{7,31},{8,14},{9,17},... | collective-permute-start | bytes 1277960 | tf_op jit(solution)/shard_map/ppermute | solution.py:44
  27.5 12.1 %copy-start.1 = (bf16[1024,128]{1,0:T(8,128)(2,1)}, bf16[1024,128]{1,0:T(8,128)(2,1)S(1)}, u32[]{:S(2)}) copy-start(bf16[1024,128]{1,0:T(8,128)(2,1)S(1)} %collective-permute-done.6.refs_3_) | copy-start | bytes 786436
  31.5 19.7 %collective-permute-start.13 = (bf16[8,2,208,128]{3,2,1,0:T(8,128)(2,1)S(1)}, bf16[8,2,208,128]{3,2,1,0:T(8,128)(2,1)S(1)}, u32[]{:S(2)}, u32[]{:S(2)}) collective-permute-start(bf16[8,2,208,128]{3,2,1,0:T(8,128)(2,1)S(1)} %collective-permute-done.10.refs_5_.refs_8_), channel_id=1, source_target_pairs={{0,8},{1,3},{2,10},{3,5},{4,12},{5,7},{6,14},{7,1},{8,16},{9,11},{... | collective-permute-start | bytes 2555912 | tf_op jit(solution)/shard_map/ppermute | solution.py:44
  39.7 406.0 %collective-permute-start.16 = (bf16[8,2,208,128]{3,2,1,0:T(8,128)(2,1)S(1)}, bf16[8,2,208,128]{3,2,1,0:T(8,128)(2,1)S(1)}, u32[]{:S(2)}, u32[]{:S(2)}) collective-permute-start(bf16[8,2,208,128]{3,2,1,0:T(8,128)(2,1)S(1)} %pad_maximum_fusion.1.refs_5_.refs_7_), channel_id=1, source_target_pairs={{0,24},{1,7},{2,26},{3,1},{4,28},{5,3},{6,30},{7,5},{8,0},{9,15},{... | collective-permute-start | bytes 2555912 | tf_op jit(solution)/shard_map/ppermute | solution.py:44
  40.9 9.6 %collective-permute-start.7 = (bf16[1024,128]{1,0:T(8,128)(2,1)S(1)}, bf16[1024,128]{1,0:T(8,128)(2,1)S(1)}, u32[]{:S(2)}, u32[]{:S(2)}) collective-permute-start(bf16[1024,128]{1,0:T(8,128)(2,1)S(1)} %copy-done.10), channel_id=1, source_target_pairs={{0,33},{1,32},{2,35},{3,34},{4,37},{5,36},{6,39},{7,38},{8,41},{9,... | collective-permute-start | bytes 786440 | tf_op jit(solution)/shard_map/ppermute | solution.py:44
  40.9 407.9 %collective-permute-start.15 = (bf16[8,2,208,128]{3,2,1,0:T(8,128)(2,1)S(1)}, bf16[8,2,208,128]{3,2,1,0:T(8,128)(2,1)S(1)}, u32[]{:S(2)}, u32[]{:S(2)}) collective-permute-start(bf16[8,2,208,128]{3,2,1,0:T(8,128)(2,1)S(1)} %pad_maximum_fusion.1.refs_5_.refs_7_), channel_id=1, source_target_pairs={{0,8},{1,3},{2,10},{3,5},{4,12},{5,7},{6,14},{7,1},{8,16},{9,11},{... | collective-permute-start | bytes 2555912 | tf_op jit(solution)/shard_map/ppermute | solution.py:44
  50.5 0.7 copy-start.3
  51.2 394.4 %copy-start.7 = (bf16[128,2048]{1,0:T(8,128)(2,1)}, bf16[128,2048]{1,0:T(8,128)(2,1)S(1)}, u32[]{:S(2)}) copy-start(bf16[128,2048]{1,0:T(8,128)(2,1)S(1)} %collective-permute-done.12) | copy-start | bytes 1572868
  445.6 1.8 collective-permute-start.14
  445.7 17.7 %collective-permute-start.18 = (bf16[8,2,208,128]{3,2,1,0:T(8,128)(2,1)S(1)}, bf16[8,2,208,128]{3,2,1,0:T(8,128)(2,1)S(1)}, u32[]{:S(2)}, u32[]{:S(2)}) collective-permute-start(bf16[8,2,208,128]{3,2,1,0:T(8,128)(2,1)S(1)} %collective-permute-done.16.refs_7_.refs_9_), channel_id=1, source_target_pairs={{0,24},{1,7},{2,26},{3,1},{4,28},{5,3},{6,30},{7,5},{8,0},{9,15},{... | collective-permute-start | bytes 2555912 | tf_op jit(solution)/shard_map/ppermute | solution.py:44
  448.7 14.7 %collective-permute-start.17 = (bf16[128,2048]{1,0:T(8,128)(2,1)S(1)}, bf16[128,2048]{1,0:T(8,128)(2,1)S(1)}, u32[]{:S(2)}, u32[]{:S(2)}) collective-permute-start(bf16[128,2048]{1,0:T(8,128)(2,1)S(1)} %fusion), channel_id=1, source_target_pairs={{0,32},{1,33},{2,34},{3,35},{4,36},{5,37},{6,38},{7,39},{8,40},{9,... | collective-permute-start | bytes 1572872 | tf_op jit(solution)/shard_map/ppermute | solution.py:44
  448.8 1.0 copy-start.2
  449.7 0.9 copy-start.4
  460.7 398.0 %copy-start.8 = (bf16[128,2048]{1,0:T(8,128)(2,1)S(1)}, bf16[128,2048]{1,0:T(8,128)(2,1)}, u32[]{:S(2)}) copy-start(bf16[128,2048]{1,0:T(8,128)(2,1)} %copy-done.7) | copy-start | bytes 1572868
  857.1 1.6 collective-permute-start.19

commit v8 on v7

--- a/solution.py
+++ b/solution.py
@@ -362,7 +362,7 @@
         in_specs=specs,
         out_specs=out_specs,
         scratch_shapes=scratch,
-        compiler_params=pltpu.CompilerParams(vmem_limit_bytes=40 * 1024 * 1024),
+        compiler_params=pltpu.CompilerParams(vmem_limit_bytes=24 * 1024 * 1024),
         cost_estimate=pl.CostEstimate(
             flops=count * 2 * ROWS * CHUNK * DIM * 6,
             bytes_accessed=count * CHUNK * DIM * 4,
@@ -458,13 +458,13 @@
     near_sum = stage((0,), False, scalars, ordered(near_q, late_unit), near)
     late_pair = jnp.concatenate([late_unit, ordered(late_mate, near_sum)])
     late_others = second_exchange(late_pair)
-    q_cross, late_stream = ordered((q_cross, late_stream), near_sum)
-    q_cross, late_stream = up_swapped(q_cross), up(late_stream)
+    q_cross = up_swapped(ordered(q_cross, near_sum))
+    late_stream = up(ordered(late_stream, near_sum, q_same))
     late_q = (q_same, q_cross)
     near[-1] = ordered(near[-1], near_sum)
     near[2] = [second_ring(near[-1][0], 1)]
     near_sum = stage((-1, 1), False, scalars, ordered(near_q, late_pair, q_same), near, near_sum)
-    late_row = jnp.concatenate([late_pair, ordered(late_others, near_sum)])
+    late_row = jnp.concatenate([late_pair, ordered(late_others, near_sum, q_cross)])
     late = {0: [late_row], -1: [second_ring(late_row, 1)], 1: [second_ring(late_row, -1)]}
     own, other = stage((2,), True, scalars, ordered(near_q, late_row, late_stream, q_cross), near, near_sum)
     late[1] = ordered(late[1], own)
@@ -479,7 +479,7 @@
 
     near_done = added(own, other, stream[0, :, : 2 * width])
     near_out = up(near_done)
-    late_sum = stage((0, -1, 1), False, scalars, ordered(late_q, near_done), late, paired=True)
+    late_sum = stage((0, -1, 1), False, ordered(scalars, near_done), late_q, late, paired=True)
     late_sum, near_out = lax.optimization_barrier((late_sum, near_out))
     own, other = stage((2,), True, scalars, late_q, late, late_sum, paired=True)
     late_out = added(own, other, late_stream)

time: 872 us -> 869 us (level)
  waiting for transfers between devices: 21.3 us -> 10.3 us
    ppermute x20, waiting for transfers between devices: 21.3 us -> 10.3 us  [moved(): return lax.ppermute(value, AXES, pairs)]
  transfers between devices with their start and end apart: 20 -> 20, of which waited for: 8 -> 6; matrix products, arithmetic and copies ran while one was open for 0% -> 0% of each run, Pallas kernels for 49% -> 49%
where the time goes in v8:
time: 869 us; the launch traced here: 859 us
  Pallas kernels  820 us (94%)
  starting transfers between devices  21.4 us (2%)
  waiting for transfers between devices  10.3 us (1%)
    pallas_call x5, Pallas kernels, stage(): pl.pallas_call(functools.partial(stage_kernel, tuple(rows_of), tuple(piec...  816 us
    ppermute x20, starting transfers between devices, moved(): return lax.ppermute(value, AXES, pairs)  21.4 us
  transfers between devices with their start and end apart: 20, of which 6 were waited for; matrix products, arithmetic and copies ran while one was open for 0% of the time, Pallas kernels for 49%

profile of v8, /device:TPU:103, one launch (start us, length us, event | category | flops | bytes accessed | tf_op | source)
XLA Modules:
  0.0 858.9 jit_solution(4333646117033017012)
XLA Ops:
  0.0 2.3 near_kernel.1
  2.3 0.7 collective-permute-start
  3.0 1.5 collective-permute-done.refs_4_
  4.5 0.9 pad_maximum_fusion.3
  5.5 1.5 collective-permute-start.2
  7.0 0.4 collective-permute-start.3
  7.4 1.3 collective-permute-start.4
  8.7 3.4 collective-permute-start.5
  12.1 2.3 late_kernel.1
  14.4 2.8 collective-permute-done.5
  17.3 1.9 collective-permute-start.9
  20.2 5.0 stage_0.1.refs_7_
  25.2 3.0 collective-permute-start.11
  28.3 1.8 collective-permute-start.7
  30.1 1.2 collective-permute-start.12
  31.5 0.7 collective-permute-start.13
  32.3 8.6 %stage_3_1.1.refs_6_ = f32[2,1024,256]{2,1,0:T(8,128)S(1)} custom-call(s32[32,32]{1,0:T(8,128)S(1)} %copy-done.5, s32[32]{0:T(128)S(1)} %copy-done.6, s32[1]{0:T(128)S(6)} %copy.8.refs_2_, bf16[1024,128]{1,0:T(8,128)(2,1)S(1)} %copy-done, bf16[1440,128]{1,0:T(8,128)(2,1)S(1)} %collective-permute-done.refs_4_, ...), custom_call_target="tpu_custom_call" | custom-call | flops 5234491392 | bytes 1703936 | tf_op jit(solution)/shard_map/stage_3_1/pallas_call | solution.py:359
  41.0 1.2 collective-permute-start.16
  42.2 1.5 collective-permute-start.15
  43.7 4.1 collective-permute-done.12
  47.8 395.1 %stage_2.2 = (bf16[128,1024]{1,0:T(8,128)(2,1)S(1)}, bf16[128,1024]{1,0:T(8,128)(2,1)}) custom-call(s32[32,32]{1,0:T(8,128)S(1)} %copy-done.5, s32[32]{0:T(128)S(1)} %copy-done.6, s32[1]{0:T(128)S(6)} %copy.8.refs_2_, bf16[1024,128]{1,0:T(8,128)(2,1)S(1)} %copy-done, bf16[1440,128]{1,0:T(8,128)(2,1)S(1)} %collective-permute-done.refs_4_, ...), custom_call_target="tpu_custom_call" | custom-call | flops 2617245696 | bytes 851968 | tf_op jit(solution)/shard_map/stage_2/pallas_call | solution.py:359
  442.9 0.5 collective-permute-start.14
  443.4 0.8 collective-permute-start.18
  444.2 0.6 collective-permute-done.14
  444.8 1.3 fusion
  446.1 0.9 copy-done.2
  447.1 0.9 copy-done.4
  448.0 12.5 %stage_0_3_1.1.refs_6_ = f32[2,1024,256]{2,1,0:T(8,128)S(1)} custom-call(s32[32,32]{1,0:T(8,128)S(1)} %copy-done.5, s32[32]{0:T(128)S(1)} %copy-done.6, s32[1]{0:T(128)S(6)} %copy.8.refs_2_, bf16[1024,128]{1,0:T(8,128)(2,1)S(1)} %copy-done.2, bf16[1024,128]{1,0:T(8,128)(2,1)S(1)} %copy-done.4, ...), custom_call_target="tpu_custom_call" | custom-call | flops 7851737088 | bytes 2555904 | tf_op jit(solution)/shard_map/stage_0_3_1/pallas_call | solution.py:359
  460.6 394.4 %stage_2.3 = (bf16[128,1024]{1,0:T(8,128)(2,1)S(1)}, bf16[128,1024]{1,0:T(8,128)(2,1)S(1)}) custom-call(s32[32,32]{1,0:T(8,128)S(1)} %copy-done.5, s32[32]{0:T(128)S(1)} %copy-done.6, s32[1]{0:T(128)S(6)} %copy.8.refs_2_, bf16[1024,128]{1,0:T(8,128)(2,1)S(1)} %copy-done.2, bf16[1024,128]{1,0:T(8,128)(2,1)S(1)} %copy-done.4, ...), custom_call_target="tpu_custom_call" | custom-call | flops 2617245696 | bytes 851968 | tf_op jit(solution)/shard_map/stage_2/pallas_call | solution.py:359
  855.0 0.9 collective-permute-start.19
  856.0 1.2 collective-permute-done.19
  857.4 1.1 maximum_bitcast_fusion
  (48 shorter events, 1.2 us)
Async XLA Ops:
  2.3 2.2 collective-permute-start
  5.4 11.8 %collective-permute-start.1 = (bf16[2,2,208,128]{3,2,1,0:T(8,128)(2,1)S(1)}, bf16[2,2,208,128]{3,2,1,0:T(8,128)(2,1)S(1)}, u32[]{:S(2)}, u32[]{:S(2)}) collective-permute-start(bf16[2,2,208,128]{3,2,1,0:T(8,128)(2,1)S(1)} %bitcast.17), channel_id=1, source_target_pairs={{0,2},{1,9},{2,4},{3,11},{4,6},{5,13},{6,0},{7,15},{8,10},{9,17},{... | collective-permute-start | bytes 638984 | tf_op jit(solution)/shard_map/ppermute | solution.py:44
  5.5 11.7 %collective-permute-start.2 = (bf16[2,2,208,128]{3,2,1,0:T(8,128)(2,1)S(1)}, bf16[2,2,208,128]{3,2,1,0:T(8,128)(2,1)S(1)}, u32[]{:S(2)}, u32[]{:S(2)}) collective-permute-start(bf16[2,2,208,128]{3,2,1,0:T(8,128)(2,1)S(1)} %bitcast.18), channel_id=1, source_target_pairs={{0,6},{1,25},{2,0},{3,27},{4,2},{5,29},{6,4},{7,31},{8,14},{9,1},{... | collective-permute-start | bytes 638984 | tf_op jit(solution)/shard_map/ppermute | solution.py:44
  7.0 10.2 %collective-permute-start.3 = (bf16[2,2,208,128]{3,2,1,0:T(8,128)(2,1)S(1)}, bf16[2,2,208,128]{3,2,1,0:T(8,128)(2,1)S(1)}, u32[]{:S(2)}, u32[]{:S(2)}) collective-permute-start(bf16[2,2,208,128]{3,2,1,0:T(8,128)(2,1)S(1)} %bitcast.19), channel_id=1, source_target_pairs={{0,4},{1,17},{2,6},{3,19},{4,0},{5,21},{6,2},{7,23},{8,12},{9,25},... | collective-permute-start | bytes 638984 | tf_op jit(solution)/shard_map/ppermute | solution.py:44
  7.4 7.0 collective-permute-start.4
  8.7 8.5 collective-permute-start.5
  12.1 8.1 copy-start
  12.1 8.1 copy-start.5
  12.1 8.1 copy-start.6
  14.4 5.7 copy-start.11
  17.3 14.2 %collective-permute-start.9 = (bf16[8,2,208,128]{3,2,1,0:T(8,128)(2,1)S(1)}, bf16[8,2,208,128]{3,2,1,0:T(8,128)(2,1)S(1)}, u32[]{:S(2)}, u32[]{:S(2)}) collective-permute-start(bf16[8,2,208,128]{3,2,1,0:T(8,128)(2,1)S(1)} %pad_maximum_fusion.refs_5_.refs_7_), channel_id=1, source_target_pairs={{0,8},{1,3},{2,10},{3,5},{4,12},{5,7},{6,14},{7,1},{8,16},{9,11},{... | collective-permute-start | bytes 2555912 | tf_op jit(solution)/shard_map/ppermute | solution.py:44
  19.2 13.1 %collective-permute-start.10 = (bf16[8,2,208,128]{3,2,1,0:T(8,128)(2,1)S(1)}, bf16[8,2,208,128]{3,2,1,0:T(8,128)(2,1)S(1)}, u32[]{:S(2)}, u32[]{:S(2)}) collective-permute-start(bf16[8,2,208,128]{3,2,1,0:T(8,128)(2,1)S(1)} %pad_maximum_fusion.refs_5_.refs_7_), channel_id=1, source_target_pairs={{0,24},{1,7},{2,26},{3,1},{4,28},{5,3},{6,30},{7,5},{8,0},{9,15},{... | collective-permute-start | bytes 2555912 | tf_op jit(solution)/shard_map/ppermute | solution.py:44
  19.9 8.3 collective-permute-start.6
  20.1 5.1 copy-start.10
  20.1 10.0 %copy-start.9 = (bf16[128,2048]{1,0:T(8,128)(2,1)S(1)}, bf16[128,2048]{1,0:T(8,128)(2,1)}, u32[]{:S(2)}) copy-start(bf16[128,2048]{1,0:T(8,128)(2,1)} %get-tuple-element.74) | copy-start | bytes 1572868
  20.1 10.0 %collective-permute-start.8 = (bf16[1024,128]{1,0:T(8,128)(2,1)S(1)}, bf16[1024,128]{1,0:T(8,128)(2,1)S(1)}, u32[]{:S(2)}, u32[]{:S(2)}) collective-permute-start(bf16[1024,128]{1,0:T(8,128)(2,1)S(1)} %copy-done.11), channel_id=1, source_target_pairs={{0,32},{1,33},{2,34},{3,35},{4,36},{5,37},{6,38},{7,39},{8,40},{9,... | collective-permute-start | bytes 786440 | tf_op jit(solution)/shard_map/ppermute | solution.py:44
  25.2 15.7 %collective-permute-start.11 = (bf16[1024,128]{1,0:T(8,128)(2,1)S(1)}, bf16[1024,128]{1,0:T(8,128)(2,1)S(1)}, u32[]{:S(2)}, u32[]{:S(2)}) collective-permute-start(bf16[1024,128]{1,0:T(8,128)(2,1)S(1)} %copy-done.10), channel_id=1, source_target_pairs={{0,33},{1,32},{2,35},{3,34},{4,37},{5,36},{6,39},{7,38},{8,41},{9,... | collective-permute-start | bytes 786440 | tf_op jit(solution)/shard_map/ppermute | solution.py:44
  28.3 12.6 %collective-permute-start.7 = (bf16[4,2,208,128]{3,2,1,0:T(8,128)(2,1)S(1)}, bf16[4,2,208,128]{3,2,1,0:T(8,128)(2,1)S(1)}, u32[]{:S(2)}, u32[]{:S(2)}) collective-permute-start(bf16[4,2,208,128]{3,2,1,0:T(8,128)(2,1)S(1)} %pad_maximum_fusion.2), channel_id=1, source_target_pairs={{0,6},{1,25},{2,4},{3,27},{4,2},{5,29},{6,0},{7,31},{8,14},{9,17},... | collective-permute-start | bytes 1277960 | tf_op jit(solution)/shard_map/ppermute | solution.py:44
  30.1 10.8 %copy-start.1 = (bf16[1024,128]{1,0:T(8,128)(2,1)}, bf16[1024,128]{1,0:T(8,128)(2,1)S(1)}, u32[]{:S(2)}) copy-start(bf16[1024,128]{1,0:T(8,128)(2,1)S(1)} %collective-permute-done.8.refs_3_) | copy-start | bytes 786436
  30.1 17.7 %collective-permute-start.12 = (bf16[128,2048]{1,0:T(8,128)(2,1)S(1)}, bf16[128,2048]{1,0:T(8,128)(2,1)S(1)}, u32[]{:S(2)}, u32[]{:S(2)}) collective-permute-start(bf16[128,2048]{1,0:T(8,128)(2,1)S(1)} %copy-done.9), channel_id=1, source_target_pairs={{0,32},{1,33},{2,34},{3,35},{4,36},{5,37},{6,38},{7,39},{8,40},{9,... | collective-permute-start | bytes 1572872 | tf_op jit(solution)/shard_map/ppermute | solution.py:44
  31.5 16.3 %collective-permute-start.13 = (bf16[8,2,208,128]{3,2,1,0:T(8,128)(2,1)S(1)}, bf16[8,2,208,128]{3,2,1,0:T(8,128)(2,1)S(1)}, u32[]{:S(2)}, u32[]{:S(2)}) collective-permute-start(bf16[8,2,208,128]{3,2,1,0:T(8,128)(2,1)S(1)} %collective-permute-done.9.refs_5_.refs_8_), channel_id=1, source_target_pairs={{0,8},{1,3},{2,10},{3,5},{4,12},{5,7},{6,14},{7,1},{8,16},{9,11},{... | collective-permute-start | bytes 2555912 | tf_op jit(solution)/shard_map/ppermute | solution.py:44
  40.9 402.0 %copy-start.3 = (bf16[1024,128]{1,0:T(8,128)(2,1)}, bf16[1024,128]{1,0:T(8,128)(2,1)S(1)}, u32[]{:S(2)}) copy-start(bf16[1024,128]{1,0:T(8,128)(2,1)S(1)} %collective-permute-done.11.refs_4_) | copy-start | bytes 786436
  41.0 402.4 %collective-permute-start.16 = (bf16[8,2,208,128]{3,2,1,0:T(8,128)(2,1)S(1)}, bf16[8,2,208,128]{3,2,1,0:T(8,128)(2,1)S(1)}, u32[]{:S(2)}, u32[]{:S(2)}) collective-permute-start(bf16[8,2,208,128]{3,2,1,0:T(8,128)(2,1)S(1)} %pad_maximum_fusion.1.refs_5_.refs_7_), channel_id=1, source_target_pairs={{0,24},{1,7},{2,26},{3,1},{4,28},{5,3},{6,30},{7,5},{8,0},{9,15},{... | collective-permute-start | bytes 2555912 | tf_op jit(solution)/shard_map/ppermute | solution.py:44
  42.2 403.9 %collective-permute-start.15 = (bf16[8,2,208,128]{3,2,1,0:T(8,128)(2,1)S(1)}, bf16[8,2,208,128]{3,2,1,0:T(8,128)(2,1)S(1)}, u32[]{:S(2)}, u32[]{:S(2)}) collective-permute-start(bf16[8,2,208,128]{3,2,1,0:T(8,128)(2,1)S(1)} %pad_maximum_fusion.1.refs_5_.refs_7_), channel_id=1, source_target_pairs={{0,8},{1,3},{2,10},{3,5},{4,12},{5,7},{6,14},{7,1},{8,16},{9,11},{... | collective-permute-start | bytes 2555912 | tf_op jit(solution)/shard_map/ppermute | solution.py:44
  47.8 395.1 %copy-start.7 = (bf16[128,2048]{1,0:T(8,128)(2,1)}, bf16[128,2048]{1,0:T(8,128)(2,1)S(1)}, u32[]{:S(2)}) copy-start(bf16[128,2048]{1,0:T(8,128)(2,1)S(1)} %collective-permute-done.12) | copy-start | bytes 1572868
  442.9 1.8 collective-permute-start.14
  443.4 17.2 %collective-permute-start.18 = (bf16[8,2,208,128]{3,2,1,0:T(8,128)(2,1)S(1)}, bf16[8,2,208,128]{3,2,1,0:T(8,128)(2,1)S(1)}, u32[]{:S(2)}, u32[]{:S(2)}) collective-permute-start(bf16[8,2,208,128]{3,2,1,0:T(8,128)(2,1)S(1)} %collective-permute-done.16.refs_7_.refs_9_), channel_id=1, source_target_pairs={{0,24},{1,7},{2,26},{3,1},{4,28},{5,3},{6,30},{7,5},{8,0},{9,15},{... | collective-permute-start | bytes 2555912 | tf_op jit(solution)/shard_map/ppermute | solution.py:44
  446.0 14.5 %collective-permute-start.17 = (bf16[128,2048]{1,0:T(8,128)(2,1)S(1)}, bf16[128,2048]{1,0:T(8,128)(2,1)S(1)}, u32[]{:S(2)}, u32[]{:S(2)}) collective-permute-start(bf16[128,2048]{1,0:T(8,128)(2,1)S(1)} %fusion), channel_id=1, source_target_pairs={{0,32},{1,33},{2,34},{3,35},{4,36},{5,37},{6,38},{7,39},{8,40},{9,... | collective-permute-start | bytes 1572872 | tf_op jit(solution)/shard_map/ppermute | solution.py:44
  446.1 1.0 copy-start.2
  447.1 0.9 copy-start.4
  460.5 396.6 %copy-start.8 = (bf16[128,2048]{1,0:T(8,128)(2,1)S(1)}, bf16[128,2048]{1,0:T(8,128)(2,1)}, u32[]{:S(2)}) copy-start(bf16[128,2048]{1,0:T(8,128)(2,1)} %copy-done.7) | copy-start | bytes 1572868
  855.0 2.1 collective-permute-start.19

commit v9 on v8

--- a/solution.py
+++ b/solution.py
@@ -456,19 +456,20 @@
     q_same = up(q_same)
     late_mate = first_exchange(late_unit)
     near_sum = stage((0,), False, scalars, ordered(near_q, late_unit), near)
-    late_pair = jnp.concatenate([late_unit, ordered(late_mate, near_sum)])
+    late_pair = jnp.concatenate([late_unit, ordered(late_mate, near_sum, q_same)])
     late_others = second_exchange(late_pair)
     q_cross = up_swapped(ordered(q_cross, near_sum))
     late_stream = up(ordered(late_stream, near_sum, q_same))
     late_q = (q_same, q_cross)
     near[-1] = ordered(near[-1], near_sum)
     near[2] = [second_ring(near[-1][0], 1)]
-    near_sum = stage((-1, 1), False, scalars, ordered(near_q, late_pair, q_same), near, near_sum)
-    late_row = jnp.concatenate([late_pair, ordered(late_others, near_sum, q_cross)])
+    near[1] = ordered(near[1], near_sum)
+    late_row = jnp.concatenate([late_pair, ordered(late_others, near[1])])
     late = {0: [late_row], -1: [second_ring(late_row, 1)], 1: [second_ring(late_row, -1)]}
-    own, other = stage((2,), True, scalars, ordered(near_q, late_row, late_stream, q_cross), near, near_sum)
-    late[1] = ordered(late[1], own)
+    near_sum = stage((-1, 1), False, scalars, ordered(near_q, late_row), near, near_sum)
+    late[1] = ordered(late[1], near_sum)
     late[2] = [second_ring(late[1][0], -1)]
+    own, other = stage((2,), True, scalars, ordered(near_q, late[1], late_stream, q_cross), near, near_sum)
 
     def added(own, other, base):
         received = swapped(other)
@@ -479,9 +480,8 @@
 
     near_done = added(own, other, stream[0, :, : 2 * width])
     near_out = up(near_done)
-    late_sum = stage((0, -1, 1), False, ordered(scalars, near_done), late_q, late, paired=True)
-    late_sum, near_out = lax.optimization_barrier((late_sum, near_out))
-    own, other = stage((2,), True, scalars, late_q, late, late_sum, paired=True)
+    own, other = stage(OFFSETS, True, scalars, ordered(late_q, near_done, late[2]), late, paired=True)
+    other = ordered(other, near_out)
     late_out = added(own, other, late_stream)
     return jnp.concatenate([near_out, late_out], 1)[None]
 

time: 869 us -> 892 us (1.026)
  waiting for transfers between devices: 10.3 us -> 24.1 us
  Pallas kernels: 820 us -> 833 us
    ppermute x20, waiting for transfers between devices: 10.3 us -> 24.1 us  [moved(): return lax.ppermute(value, AXES, pairs)]
    pallas_call x5 -> x4, Pallas kernels: 816 us -> 828 us  [stage(): pl.pallas_call(functools.partial(stage_kernel, tuple(rows_of), tuple(piec...]
  transfers between devices with their start and end apart: 20 -> 20, of which waited for: 6 -> 9; matrix products, arithmetic and copies ran while one was open for 0% -> 0% of each run, Pallas kernels for 49% -> 94%
where the time goes in v9:
time: 892 us; the launch traced here: 884 us
  Pallas kernels  833 us (93%)
  waiting for transfers between devices  24.1 us (3%)
  starting transfers between devices  19.5 us (2%)
    pallas_call x4, Pallas kernels, stage(): pl.pallas_call(functools.partial(stage_kernel, tuple(rows_of), tuple(piec...  828 us
    ppermute x20, waiting for transfers between devices, moved(): return lax.ppermute(value, AXES, pairs)  24.1 us
    ppermute x20, starting transfers between devices, moved(): return lax.ppermute(value, AXES, pairs)  19.5 us
  transfers between devices with their start and end apart: 20, of which 9 were waited for; matrix products, arithmetic and copies ran while one was open for 0% of the time, Pallas kernels for 94%

profile of v9, /device:TPU:103, one launch (start us, length us, event | category | flops | bytes accessed | tf_op | source)
XLA Modules:
  0.0 884.4 jit_solution(17865525713861611707)
XLA Ops:
  0.0 2.3 near_kernel.1
  2.3 0.7 collective-permute-start
  3.0 1.5 collective-permute-done.refs_4_
  4.5 0.9 pad_maximum_fusion.3
  5.5 1.5 collective-permute-start.2
  7.0 0.4 collective-permute-start.3
  7.4 1.3 collective-permute-start.4
  8.7 3.4 collective-permute-start.5
  12.8 2.3 late_kernel.1
  15.1 2.1 collective-permute-done.5
  17.3 0.9 collective-permute-start.9
  18.2 1.8 collective-permute-start.11
  20.4 5.0 stage_0.1.refs_7_
  25.4 2.2 collective-permute-done.6
  27.6 0.8 collective-permute-done.7.refs_3_
  28.6 1.8 collective-permute-done.9.refs_6_.refs_9_
  30.4 6.5 collective-permute-done.8
  37.3 2.7 collective-permute-start.14
  40.0 0.4 collective-permute-start.12
  40.4 4.1 collective-permute-start.13
  44.5 1.2 collective-permute-start.18
  45.7 9.2 %stage_3_1.1.refs_6_ = f32[2,1024,256]{2,1,0:T(8,128)S(1)} custom-call(s32[32,32]{1,0:T(8,128)S(1)} %copy-done.5, s32[32]{0:T(128)S(1)} %copy-done.6, s32[1]{0:T(128)S(6)} %copy.8.refs_2_, bf16[1024,128]{1,0:T(8,128)(2,1)S(1)} %copy-done, bf16[1440,128]{1,0:T(8,128)(2,1)S(1)} %collective-permute-done.refs_4_, ...), custom_call_target="tpu_custom_call" | custom-call | flops 5234491392 | bytes 1703936 | tf_op jit(solution)/shard_map/stage_3_1/pallas_call | solution.py:359
  55.0 5.9 collective-permute-done.13.refs_4_
  60.8 0.7 copy-done.3
  61.5 395.3 %stage_2.1 = (bf16[128,1024]{1,0:T(8,128)(2,1)S(1)}, bf16[128,1024]{1,0:T(8,128)(2,1)}) custom-call(s32[32,32]{1,0:T(8,128)S(1)} %copy-done.5, s32[32]{0:T(128)S(1)} %copy-done.6, s32[1]{0:T(128)S(6)} %copy.8.refs_2_, bf16[1024,128]{1,0:T(8,128)(2,1)S(1)} %copy-done, bf16[1440,128]{1,0:T(8,128)(2,1)S(1)} %collective-permute-done.refs_4_, ...), custom_call_target="tpu_custom_call" | custom-call | flops 2617245696 | bytes 851968 | tf_op jit(solution)/shard_map/stage_2/pallas_call | solution.py:359
  457.0 1.7 collective-permute-done.15
  458.7 1.4 fusion
  460.2 0.9 copy-done.2
  461.1 0.9 copy-done.4
  462.0 419.0 %stage_0_3_1_2.1 = (bf16[128,1024]{1,0:T(8,128)(2,1)S(1)}, bf16[128,1024]{1,0:T(8,128)(2,1)S(1)}) custom-call(s32[32,32]{1,0:T(8,128)S(1)} %copy-done.5, s32[32]{0:T(128)S(1)} %copy-done.6, s32[1]{0:T(128)S(6)} %copy.8.refs_2_, bf16[1024,128]{1,0:T(8,128)(2,1)S(1)} %copy-done.2, bf16[1024,128]{1,0:T(8,128)(2,1)S(1)} %copy-done.4, ...), custom_call_target="tpu_custom_call" | custom-call | flops 10468982784 | bytes 3407872 | tf_op jit(solution)/shard_map/stage_0_3_1_2/pallas_call | solution.py:359
  881.1 1.5 collective-permute-done.19
  882.9 1.1 maximum_bitcast_fusion
  (45 shorter events, 1.7 us)
Async XLA Ops:
  2.3 2.2 collective-permute-start
  5.4 11.8 %collective-permute-start.1 = (bf16[2,2,208,128]{3,2,1,0:T(8,128)(2,1)S(1)}, bf16[2,2,208,128]{3,2,1,0:T(8,128)(2,1)S(1)}, u32[]{:S(2)}, u32[]{:S(2)}) collective-permute-start(bf16[2,2,208,128]{3,2,1,0:T(8,128)(2,1)S(1)} %bitcast.17), channel_id=1, source_target_pairs={{0,2},{1,9},{2,4},{3,11},{4,6},{5,13},{6,0},{7,15},{8,10},{9,17},{... | collective-permute-start | bytes 638984 | tf_op jit(solution)/shard_map/ppermute | solution.py:44
  5.5 11.7 %collective-permute-start.2 = (bf16[2,2,208,128]{3,2,1,0:T(8,128)(2,1)S(1)}, bf16[2,2,208,128]{3,2,1,0:T(8,128)(2,1)S(1)}, u32[]{:S(2)}, u32[]{:S(2)}) collective-permute-start(bf16[2,2,208,128]{3,2,1,0:T(8,128)(2,1)S(1)} %bitcast.18), channel_id=1, source_target_pairs={{0,6},{1,25},{2,0},{3,27},{4,2},{5,29},{6,4},{7,31},{8,14},{9,1},{... | collective-permute-start | bytes 638984 | tf_op jit(solution)/shard_map/ppermute | solution.py:44
  7.0 10.2 %collective-permute-start.3 = (bf16[2,2,208,128]{3,2,1,0:T(8,128)(2,1)S(1)}, bf16[2,2,208,128]{3,2,1,0:T(8,128)(2,1)S(1)}, u32[]{:S(2)}, u32[]{:S(2)}) collective-permute-start(bf16[2,2,208,128]{3,2,1,0:T(8,128)(2,1)S(1)} %bitcast.19), channel_id=1, source_target_pairs={{0,4},{1,17},{2,6},{3,19},{4,0},{5,21},{6,2},{7,23},{8,12},{9,25},... | collective-permute-start | bytes 638984 | tf_op jit(solution)/shard_map/ppermute | solution.py:44
  7.4 7.6 collective-permute-start.4
  8.7 8.5 collective-permute-start.5
  12.7 7.7 copy-start
  12.7 7.6 copy-start.5
  12.8 7.6 copy-start.6
  17.3 13.1 %collective-permute-start.9 = (bf16[8,2,208,128]{3,2,1,0:T(8,128)(2,1)S(1)}, bf16[8,2,208,128]{3,2,1,0:T(8,128)(2,1)S(1)}, u32[]{:S(2)}, u32[]{:S(2)}) collective-permute-start(bf16[8,2,208,128]{3,2,1,0:T(8,128)(2,1)S(1)} %pad_maximum_fusion.refs_5_.refs_7_), channel_id=1, source_target_pairs={{0,24},{1,7},{2,26},{3,1},{4,28},{5,3},{6,30},{7,5},{8,0},{9,15},{... | collective-permute-start | bytes 2555912 | tf_op jit(solution)/shard_map/ppermute | solution.py:44
  18.2 19.0 %collective-permute-start.11 = (bf16[8,2,208,128]{3,2,1,0:T(8,128)(2,1)S(1)}, bf16[8,2,208,128]{3,2,1,0:T(8,128)(2,1)S(1)}, u32[]{:S(2)}, u32[]{:S(2)}) collective-permute-start(bf16[8,2,208,128]{3,2,1,0:T(8,128)(2,1)S(1)} %pad_maximum_fusion.refs_5_.refs_7_), channel_id=1, source_target_pairs={{0,8},{1,3},{2,10},{3,5},{4,12},{5,7},{6,14},{7,1},{8,16},{9,11},{... | collective-permute-start | bytes 2555912 | tf_op jit(solution)/shard_map/ppermute | solution.py:44
  20.1 8.3 collective-permute-start.7
  20.2 7.4 collective-permute-start.6
  25.4 14.6 %copy-start.9 = (bf16[128,2048]{1,0:T(8,128)(2,1)S(1)}, bf16[128,2048]{1,0:T(8,128)(2,1)}, u32[]{:S(2)}) copy-start(bf16[128,2048]{1,0:T(8,128)(2,1)} %get-tuple-element.73) | copy-start | bytes 1572868
  25.4 15.0 %copy-start.10 = (bf16[1024,128]{1,0:T(8,128)(2,1)S(1)}, bf16[1024,128]{1,0:T(8,128)(2,1)}, u32[]{:S(2)}) copy-start(bf16[1024,128]{1,0:T(8,128)(2,1)} %get-tuple-element.75) | copy-start | bytes 786436
  28.3 26.5 %copy-start.1 = (bf16[1024,128]{1,0:T(8,128)(2,1)}, bf16[1024,128]{1,0:T(8,128)(2,1)S(1)}, u32[]{:S(2)}) copy-start(bf16[1024,128]{1,0:T(8,128)(2,1)S(1)} %collective-permute-done.7.refs_3_) | copy-start | bytes 786436
  28.4 8.6 collective-permute-start.8
  37.0 17.8 %collective-permute-start.10 = (bf16[8,2,208,128]{3,2,1,0:T(8,128)(2,1)S(1)}, bf16[8,2,208,128]{3,2,1,0:T(8,128)(2,1)S(1)}, u32[]{:S(2)}, u32[]{:S(2)}) collective-permute-start(bf16[8,2,208,128]{3,2,1,0:T(8,128)(2,1)S(1)} %pad_maximum_fusion.1.refs_5_.refs_9_), channel_id=1, source_target_pairs={{0,24},{1,7},{2,26},{3,1},{4,28},{5,3},{6,30},{7,5},{8,0},{9,15},{... | collective-permute-start | bytes 2555912 | tf_op jit(solution)/shard_map/ppermute | solution.py:44
  37.3 24.2 %collective-permute-start.14 = (bf16[8,2,208,128]{3,2,1,0:T(8,128)(2,1)S(1)}, bf16[8,2,208,128]{3,2,1,0:T(8,128)(2,1)S(1)}, u32[]{:S(2)}, u32[]{:S(2)}) collective-permute-start(bf16[8,2,208,128]{3,2,1,0:T(8,128)(2,1)S(1)} %collective-permute-done.11.refs_5_.refs_8_), channel_id=1, source_target_pairs={{0,8},{1,3},{2,10},{3,5},{4,12},{5,7},{6,14},{7,1},{8,16},{9,11},{... | collective-permute-start | bytes 2555912 | tf_op jit(solution)/shard_map/ppermute | solution.py:44
  40.0 21.6 %collective-permute-start.12 = (bf16[128,2048]{1,0:T(8,128)(2,1)S(1)}, bf16[128,2048]{1,0:T(8,128)(2,1)S(1)}, u32[]{:S(2)}, u32[]{:S(2)}) collective-permute-start(bf16[128,2048]{1,0:T(8,128)(2,1)S(1)} %copy-done.9), channel_id=1, source_target_pairs={{0,32},{1,33},{2,34},{3,35},{4,36},{5,37},{6,38},{7,39},{8,40},{9,... | collective-permute-start | bytes 1572872 | tf_op jit(solution)/shard_map/ppermute | solution.py:44
  40.4 20.5 %collective-permute-start.13 = (bf16[1024,128]{1,0:T(8,128)(2,1)S(1)}, bf16[1024,128]{1,0:T(8,128)(2,1)S(1)}, u32[]{:S(2)}, u32[]{:S(2)}) collective-permute-start(bf16[1024,128]{1,0:T(8,128)(2,1)S(1)} %copy-done.10), channel_id=1, source_target_pairs={{0,33},{1,32},{2,35},{3,34},{4,37},{5,36},{6,39},{7,38},{8,41},{9,... | collective-permute-start | bytes 786440 | tf_op jit(solution)/shard_map/ppermute | solution.py:44
  44.5 415.6 %collective-permute-start.18 = (bf16[8,2,208,128]{3,2,1,0:T(8,128)(2,1)S(1)}, bf16[8,2,208,128]{3,2,1,0:T(8,128)(2,1)S(1)}, u32[]{:S(2)}, u32[]{:S(2)}) collective-permute-start(bf16[8,2,208,128]{3,2,1,0:T(8,128)(2,1)S(1)} %pad_maximum_fusion.1.refs_5_.refs_9_), channel_id=1, source_target_pairs={{0,8},{1,3},{2,10},{3,5},{4,12},{5,7},{6,14},{7,1},{8,16},{9,11},{... | collective-permute-start | bytes 2555912 | tf_op jit(solution)/shard_map/ppermute | solution.py:44
  54.9 405.2 %collective-permute-start.17 = (bf16[8,2,208,128]{3,2,1,0:T(8,128)(2,1)S(1)}, bf16[8,2,208,128]{3,2,1,0:T(8,128)(2,1)}, u32[]{:S(2)}, u32[]{:S(2)}) collective-permute-start(bf16[8,2,208,128]{3,2,1,0:T(8,128)(2,1)S(1)} %collective-permute-done.10.refs_7_.refs_11_), channel_id=1, source_target_pairs={{0,24},{1,7},{2,26},{3,1},{4,28},{5,3},{6,30},{7,5},{8,0},{9,15},{... | collective-permute-start | bytes 2555912 | tf_op jit(solution)/shard_map/ppermute | solution.py:44
  60.8 0.7 copy-start.3
  61.5 395.3 %copy-start.7 = (bf16[128,2048]{1,0:T(8,128)(2,1)}, bf16[128,2048]{1,0:T(8,128)(2,1)S(1)}, u32[]{:S(2)}) copy-start(bf16[128,2048]{1,0:T(8,128)(2,1)S(1)} %collective-permute-done.12) | copy-start | bytes 1572868
  456.8 1.8 collective-permute-start.15
  458.7 424.0 %copy-start.8 = (bf16[128,2048]{1,0:T(8,128)(2,1)S(1)}, bf16[128,2048]{1,0:T(8,128)(2,1)}, u32[]{:S(2)}) copy-start(bf16[128,2048]{1,0:T(8,128)(2,1)} %copy-done.7) | copy-start | bytes 1572868
  460.0 421.0 %collective-permute-start.16 = (bf16[128,2048]{1,0:T(8,128)(2,1)S(1)}, bf16[128,2048]{1,0:T(8,128)(2,1)S(1)}, u32[]{:S(2)}, u32[]{:S(2)}) collective-permute-start(bf16[128,2048]{1,0:T(8,128)(2,1)S(1)} %fusion), channel_id=1, source_target_pairs={{0,32},{1,33},{2,34},{3,35},{4,36},{5,37},{6,38},{7,39},{8,40},{9,... | collective-permute-start | bytes 1572872 | tf_op jit(solution)/shard_map/ppermute | solution.py:44
  460.1 1.0 copy-start.2
  461.1 0.9 copy-start.4
  881.0 1.6 collective-permute-start.19

commit v10 on v8

--- a/solution.py
+++ b/solution.py
@@ -466,9 +466,7 @@
     near_sum = stage((-1, 1), False, scalars, ordered(near_q, late_pair, q_same), near, near_sum)
     late_row = jnp.concatenate([late_pair, ordered(late_others, near_sum, q_cross)])
     late = {0: [late_row], -1: [second_ring(late_row, 1)], 1: [second_ring(late_row, -1)]}
-    own, other = stage((2,), True, scalars, ordered(near_q, late_row, late_stream, q_cross), near, near_sum)
-    late[1] = ordered(late[1], own)
-    late[2] = [second_ring(late[1][0], -1)]
+    own, other = stage((2,), True, scalars, ordered(near_q, late_row, q_cross), near, near_sum)
 
     def added(own, other, base):
         received = swapped(other)
@@ -477,8 +475,11 @@
         )
         return (base.astype(jnp.float32) + both.astype(jnp.float32)).astype(jnp.bfloat16)
 
+    own, late_stream, late[-1] = lax.optimization_barrier((own, late_stream, late[-1]))
     near_done = added(own, other, stream[0, :, : 2 * width])
     near_out = up(near_done)
+    late[1] = ordered(late[1], near_done)
+    late[2] = [second_ring(late[1][0], -1)]
     late_sum = stage((0, -1, 1), False, ordered(scalars, near_done), late_q, late, paired=True)
     late_sum, near_out = lax.optimization_barrier((late_sum, near_out))
     own, other = stage((2,), True, scalars, late_q, late, late_sum, paired=True)

time: 869 us -> 868 us (level)
  transfers between devices with their start and end apart: 20 -> 20, of which waited for: 6 -> 7; matrix products, arithmetic and copies ran while one was open for 0% -> 0% of each run, Pallas kernels for 49% -> 49%
where the time goes in v10:
time: 868 us; the launch traced here: 857 us
  Pallas kernels  816 us (94%)
  waiting for transfers between devices  17.5 us (2%)
  starting transfers between devices  17 us (2%)
    pallas_call x5, Pallas kernels, stage(): pl.pallas_call(functools.partial(stage_kernel, tuple(rows_of), tuple(piec...  811 us
    ppermute x20, waiting for transfers between devices, moved(): return lax.ppermute(value, AXES, pairs)  17.5 us
  transfers between devices with their start and end apart: 20, of which 7 were waited for; matrix products, arithmetic and copies ran while one was open for 0% of the time, Pallas kernels for 49%

profile of v10, /device:TPU:103, one launch (start us, length us, event | category | flops | bytes accessed | tf_op | source)
XLA Modules:
  0.0 857.2 jit_solution(16121809039738016596)
XLA Ops:
  0.0 2.3 near_kernel.1
  2.3 0.7 collective-permute-start
  3.0 1.5 collective-permute-done.refs_4_
  4.5 0.9 pad_maximum_fusion.3
  5.5 1.5 collective-permute-start.2
  7.0 0.4 collective-permute-start.3
  7.4 1.3 collective-permute-start.4
  8.7 3.4 collective-permute-start.5
  12.1 2.3 late_kernel.1
  14.4 2.8 collective-permute-done.5
  17.3 1.9 collective-permute-start.9
  19.9 0.2 collective-permute-start.6
  20.2 4.8 stage_0.1.refs_7_
  25.0 3.0 collective-permute-start.11
  28.1 0.6 collective-permute-start.7
  28.7 2.9 collective-permute-done.9.refs_5_.refs_8_
  31.5 1.0 collective-permute-start.12
  32.5 6.6 stage_3_1.1.refs_6_
  39.2 1.5 collective-permute-start.14
  40.8 0.8 collective-permute-start.16
  41.6 3.8 collective-permute-done.12.refs_5_.refs_10_
  45.4 394.9 %stage_2.2 = (bf16[128,1024]{1,0:T(8,128)(2,1)S(1)}, bf16[128,1024]{1,0:T(8,128)(2,1)}) custom-call(s32[32,32]{1,0:T(8,128)S(1)} %copy-done.4, s32[32]{0:T(128)S(1)} %copy-done.5, s32[1]{0:T(128)S(6)} %copy.8.refs_2_, bf16[1024,128]{1,0:T(8,128)(2,1)S(1)} %copy-done.1, bf16[1440,128]{1,0:T(8,128)(2,1)S(1)} %collective-permute-done.refs_4_, ...), custom_call_target="tpu_custom_call" | custom-call | flops 2617245696 | bytes 851968 | tf_op jit(solution)/shard_map/stage_2/pallas_call | solution.py:359
  440.4 1.7 collective-permute-done.15
  442.1 1.3 fusion
  443.4 0.3 collective-permute-start.18
  443.8 0.9 copy-done.3
  444.7 10.5 %stage_0_3_1.1.refs_6_ = f32[2,1024,256]{2,1,0:T(8,128)S(1)} custom-call(s32[32,32]{1,0:T(8,128)S(1)} %copy-done.4, s32[32]{0:T(128)S(1)} %copy-done.5, s32[1]{0:T(128)S(6)} %copy.8.refs_2_, bf16[1024,128]{1,0:T(8,128)(2,1)S(1)} %collective-permute-done.8.refs_3_, bf16[1024,128]{1,0:T(8,128)(2,1)S(1)} %copy-done.3, ...), custom_call_target="tpu_custom_call" | custom-call | flops 7851737088 | bytes 2555904 | tf_op jit(solution)/shard_map/stage_0_3_1/pallas_call | solution.py:359
  455.2 3.3 collective-permute-done.17
  458.5 394.2 %stage_2.3 = (bf16[128,1024]{1,0:T(8,128)(2,1)S(1)}, bf16[128,1024]{1,0:T(8,128)(2,1)S(1)}) custom-call(s32[32,32]{1,0:T(8,128)S(1)} %copy-done.4, s32[32]{0:T(128)S(1)} %copy-done.5, s32[1]{0:T(128)S(6)} %copy.8.refs_2_, bf16[1024,128]{1,0:T(8,128)(2,1)S(1)} %collective-permute-done.8.refs_3_, bf16[1024,128]{1,0:T(8,128)(2,1)S(1)} %copy-done.3, ...), custom_call_target="tpu_custom_call" | custom-call | flops 2617245696 | bytes 851968 | tf_op jit(solution)/shard_map/stage_2/pallas_call | solution.py:359
  852.8 1.5 collective-permute-done.19
  854.3 1.3 add_convert_fusion
  855.7 1.1 maximum_bitcast_fusion
  (40 shorter events, 0.8 us)
Async XLA Ops:
  2.3 2.2 collective-permute-start
  5.4 11.8 %collective-permute-start.1 = (bf16[2,2,208,128]{3,2,1,0:T(8,128)(2,1)S(1)}, bf16[2,2,208,128]{3,2,1,0:T(8,128)(2,1)S(1)}, u32[]{:S(2)}, u32[]{:S(2)}) collective-permute-start(bf16[2,2,208,128]{3,2,1,0:T(8,128)(2,1)S(1)} %bitcast.17), channel_id=1, source_target_pairs={{0,2},{1,9},{2,4},{3,11},{4,6},{5,13},{6,0},{7,15},{8,10},{9,17},{... | collective-permute-start | bytes 638984 | tf_op jit(solution)/shard_map/ppermute | solution.py:44
  5.5 11.7 %collective-permute-start.2 = (bf16[2,2,208,128]{3,2,1,0:T(8,128)(2,1)S(1)}, bf16[2,2,208,128]{3,2,1,0:T(8,128)(2,1)S(1)}, u32[]{:S(2)}, u32[]{:S(2)}) collective-permute-start(bf16[2,2,208,128]{3,2,1,0:T(8,128)(2,1)S(1)} %bitcast.18), channel_id=1, source_target_pairs={{0,6},{1,25},{2,0},{3,27},{4,2},{5,29},{6,4},{7,31},{8,14},{9,1},{... | collective-permute-start | bytes 638984 | tf_op jit(solution)/shard_map/ppermute | solution.py:44
  7.0 10.2 %collective-permute-start.3 = (bf16[2,2,208,128]{3,2,1,0:T(8,128)(2,1)S(1)}, bf16[2,2,208,128]{3,2,1,0:T(8,128)(2,1)S(1)}, u32[]{:S(2)}, u32[]{:S(2)}) collective-permute-start(bf16[2,2,208,128]{3,2,1,0:T(8,128)(2,1)S(1)} %bitcast.19), channel_id=1, source_target_pairs={{0,4},{1,17},{2,6},{3,19},{4,0},{5,21},{6,2},{7,23},{8,12},{9,25},... | collective-permute-start | bytes 638984 | tf_op jit(solution)/shard_map/ppermute | solution.py:44
  7.4 7.0 collective-permute-start.4
  8.7 8.5 collective-permute-start.5
  12.1 8.1 copy-start
  12.1 8.1 copy-start.4
  12.1 8.1 copy-start.5
  14.4 5.7 copy-start.7
  17.3 14.2 %collective-permute-start.9 = (bf16[8,2,208,128]{3,2,1,0:T(8,128)(2,1)S(1)}, bf16[8,2,208,128]{3,2,1,0:T(8,128)(2,1)S(1)}, u32[]{:S(2)}, u32[]{:S(2)}) collective-permute-start(bf16[8,2,208,128]{3,2,1,0:T(8,128)(2,1)S(1)} %pad_maximum_fusion.refs_5_.refs_7_), channel_id=1, source_target_pairs={{0,8},{1,3},{2,10},{3,5},{4,12},{5,7},{6,14},{7,1},{8,16},{9,11},{... | collective-permute-start | bytes 2555912 | tf_op jit(solution)/shard_map/ppermute | solution.py:44
  19.2 13.3 %collective-permute-start.10 = (bf16[8,2,208,128]{3,2,1,0:T(8,128)(2,1)S(1)}, bf16[8,2,208,128]{3,2,1,0:T(8,128)(2,1)S(1)}, u32[]{:S(2)}, u32[]{:S(2)}) collective-permute-start(bf16[8,2,208,128]{3,2,1,0:T(8,128)(2,1)S(1)} %pad_maximum_fusion.refs_5_.refs_7_), channel_id=1, source_target_pairs={{0,24},{1,7},{2,26},{3,1},{4,28},{5,3},{6,30},{7,5},{8,0},{9,15},{... | collective-permute-start | bytes 2555912 | tf_op jit(solution)/shard_map/ppermute | solution.py:44
  19.9 8.1 collective-permute-start.6
  20.1 4.9 copy-start.6
  20.1 8.6 collective-permute-start.8
  25.0 14.2 %collective-permute-start.11 = (bf16[1024,128]{1,0:T(8,128)(2,1)S(1)}, bf16[1024,128]{1,0:T(8,128)(2,1)S(1)}, u32[]{:S(2)}, u32[]{:S(2)}) collective-permute-start(bf16[1024,128]{1,0:T(8,128)(2,1)S(1)} %copy-done.6), channel_id=1, source_target_pairs={{0,33},{1,32},{2,35},{3,34},{4,37},{5,36},{6,39},{7,38},{8,41},{9,... | collective-permute-start | bytes 786440 | tf_op jit(solution)/shard_map/ppermute | solution.py:44
  28.1 17.3 %copy-start.1 = (bf16[1024,128]{1,0:T(8,128)(2,1)S(1)}, bf16[1024,128]{1,0:T(8,128)(2,1)}, u32[]{:S(2)}) copy-start(bf16[1024,128]{1,0:T(8,128)(2,1)} %get-tuple-element.76.refs_3_) | copy-start | bytes 786436
  28.1 11.1 %collective-permute-start.7 = (bf16[4,2,208,128]{3,2,1,0:T(8,128)(2,1)S(1)}, bf16[4,2,208,128]{3,2,1,0:T(8,128)(2,1)S(1)}, u32[]{:S(2)}, u32[]{:S(2)}) collective-permute-start(bf16[4,2,208,128]{3,2,1,0:T(8,128)(2,1)S(1)} %pad_maximum_fusion.2), channel_id=1, source_target_pairs={{0,6},{1,25},{2,4},{3,27},{4,2},{5,29},{6,0},{7,31},{8,14},{9,17},... | collective-permute-start | bytes 1277960 | tf_op jit(solution)/shard_map/ppermute | solution.py:44
  31.5 13.9 %collective-permute-start.12 = (bf16[8,2,208,128]{3,2,1,0:T(8,128)(2,1)S(1)}, bf16[8,2,208,128]{3,2,1,0:T(8,128)(2,1)S(1)}, u32[]{:S(2)}, u32[]{:S(2)}) collective-permute-start(bf16[8,2,208,128]{3,2,1,0:T(8,128)(2,1)S(1)} %collective-permute-done.9.refs_5_.refs_8_), channel_id=1, source_target_pairs={{0,8},{1,3},{2,10},{3,5},{4,12},{5,7},{6,14},{7,1},{8,16},{9,11},{... | collective-permute-start | bytes 2555912 | tf_op jit(solution)/shard_map/ppermute | solution.py:44
  39.1 401.1 %copy-start.2 = (bf16[1024,128]{1,0:T(8,128)(2,1)}, bf16[1024,128]{1,0:T(8,128)(2,1)S(1)}, u32[]{:S(2)}) copy-start(bf16[1024,128]{1,0:T(8,128)(2,1)S(1)} %collective-permute-done.11.refs_4_) | copy-start | bytes 786436
  39.2 401.1 %collective-permute-start.14 = (bf16[8,2,208,128]{3,2,1,0:T(8,128)(2,1)S(1)}, bf16[8,2,208,128]{3,2,1,0:T(8,128)(2,1)S(1)}, u32[]{:S(2)}, u32[]{:S(2)}) collective-permute-start(bf16[8,2,208,128]{3,2,1,0:T(8,128)(2,1)S(1)} %pad_maximum_fusion.1.refs_5_.refs_7_), channel_id=1, source_target_pairs={{0,8},{1,3},{2,10},{3,5},{4,12},{5,7},{6,14},{7,1},{8,16},{9,11},{... | collective-permute-start | bytes 2555912 | tf_op jit(solution)/shard_map/ppermute | solution.py:44
  40.7 399.7 %collective-permute-start.13 = (bf16[128,2048]{1,0:T(8,128)(2,1)}, bf16[128,2048]{1,0:T(8,128)(2,1)}, u32[]{:S(2)}, u32[]{:S(2)}) collective-permute-start(bf16[128,2048]{1,0:T(8,128)(2,1)} %get-tuple-element.80), channel_id=1, source_target_pairs={{0,32},{1,33},{2,34},{3,35},{4,36},{5,37},{6,38},{7,39},{8,40},{9,... | collective-permute-start | bytes 1572872 | tf_op jit(solution)/shard_map/ppermute | solution.py:44
  40.8 402.6 %collective-permute-start.16 = (bf16[8,2,208,128]{3,2,1,0:T(8,128)(2,1)S(1)}, bf16[8,2,208,128]{3,2,1,0:T(8,128)(2,1)S(1)}, u32[]{:S(2)}, u32[]{:S(2)}) collective-permute-start(bf16[8,2,208,128]{3,2,1,0:T(8,128)(2,1)S(1)} %pad_maximum_fusion.1.refs_5_.refs_7_), channel_id=1, source_target_pairs={{0,24},{1,7},{2,26},{3,1},{4,28},{5,3},{6,30},{7,5},{8,0},{9,15},{... | collective-permute-start | bytes 2555912 | tf_op jit(solution)/shard_map/ppermute | solution.py:44
  440.3 1.8 collective-permute-start.15
  443.4 15.1 %collective-permute-start.18 = (bf16[8,2,208,128]{3,2,1,0:T(8,128)(2,1)S(1)}, bf16[8,2,208,128]{3,2,1,0:T(8,128)(2,1)S(1)}, u32[]{:S(2)}, u32[]{:S(2)}) collective-permute-start(bf16[8,2,208,128]{3,2,1,0:T(8,128)(2,1)S(1)} %collective-permute-done.16.refs_7_.refs_9_), channel_id=1, source_target_pairs={{0,24},{1,7},{2,26},{3,1},{4,28},{5,3},{6,30},{7,5},{8,0},{9,15},{... | collective-permute-start | bytes 2555912 | tf_op jit(solution)/shard_map/ppermute | solution.py:44
  443.7 14.8 %collective-permute-start.17 = (bf16[128,2048]{1,0:T(8,128)(2,1)S(1)}, bf16[128,2048]{1,0:T(8,128)(2,1)S(1)}, u32[]{:S(2)}, u32[]{:S(2)}) collective-permute-start(bf16[128,2048]{1,0:T(8,128)(2,1)S(1)} %fusion), channel_id=1, source_target_pairs={{0,32},{1,33},{2,34},{3,35},{4,36},{5,37},{6,38},{7,39},{8,40},{9,... | collective-permute-start | bytes 1572872 | tf_op jit(solution)/shard_map/ppermute | solution.py:44
  443.8 0.9 copy-start.3
  852.7 1.6 collective-permute-start.19

commit v11 on v8

--- a/solution.py
+++ b/solution.py
@@ -22,7 +22,8 @@
 PAIR = 2 * (TOK + LIVE)
 CHUNK = SPAN_ROWS + CACHE_ROWS
 BLOCK = 128
-TILE_BLOCKS = 8
+TILE_BLOCKS = 16
+OPENING = 8
 SUB = 256
 OFFSETS = (0, -1, 1, 2)
 TO_LOG2 = math.log2(math.e) / math.sqrt(DIM)
@@ -209,9 +210,9 @@
 
         begin = 0
         if rows_of[0] == 0:
-            tile(TILE_BLOCKS, 0, opening=True)
-            begin = TILE_BLOCKS
-            filled = jnp.maximum(filled - TILE_BLOCKS, 0)
+            tile(OPENING, 0, opening=True)
+            begin = OPENING
+            filled = jnp.maximum(filled - OPENING, 0)
         else:
             total_ref[q] = carry_ref[q]
 
@@ -224,9 +225,18 @@
 
         lax.fori_loop(0, whole, whole_tile, 0)
 
+        done = begin + whole * TILE_BLOCKS
+
+        @pl.when(rest > 6)
+        def _():
+            tile(8, done)
+
+        done = jnp.where(rest > 6, done + 8, done)
+        rest = jnp.where(rest > 6, rest - 8, rest)
+
         @pl.when(rest > 2)
         def _():
-            tile(4, begin + whole * TILE_BLOCKS)
+            tile(4, done)
 
         left = jnp.where(rest > 2, rest - 4, rest)
 

time: 869 us -> 869 us (level)
  no operation moved by 1% of the time
where the time goes in v11:
time: 869 us; the launch traced here: 858 us
  Pallas kernels  817 us (94%)
  starting transfers between devices  21.8 us (3%)
  waiting for transfers between devices  12.8 us (1%)
    pallas_call x5, Pallas kernels, stage(): pl.pallas_call(functools.partial(stage_kernel, tuple(rows_of), tuple(piec...  812 us
    ppermute x20, starting transfers between devices, moved(): return lax.ppermute(value, AXES, pairs)  21.8 us
  transfers between devices with their start and end apart: 20, of which 6 were waited for; matrix products, arithmetic and copies ran while one was open for 0% of the time, Pallas kernels for 49%

profile of v11, /device:TPU:103, one launch (start us, length us, event | category | flops | bytes accessed | tf_op | source)
XLA Modules:
  0.0 858.5 jit_solution(12555593345419759900)
XLA Ops:
  0.0 2.3 near_kernel.1
  2.3 0.7 collective-permute-start
  3.0 1.5 collective-permute-done.refs_4_
  4.5 0.9 pad_maximum_fusion.3
  5.5 1.5 collective-permute-start.2
  7.0 0.4 collective-permute-start.3
  7.4 1.3 collective-permute-start.4
  8.7 3.4 collective-permute-start.5
  12.1 2.3 late_kernel.1
  14.4 2.8 collective-permute-done.5
  17.3 1.9 collective-permute-start.9
  20.2 5.2 stage_0.1.refs_7_
  25.5 3.0 collective-permute-start.11
  28.9 1.1 collective-permute-start.12
  30.0 1.5 collective-permute-done.9.refs_5_.refs_8_
  31.5 0.7 collective-permute-start.13
  32.3 8.0 stage_3_1.1.refs_6_
  40.4 1.9 collective-permute-start.16
  42.2 0.9 collective-permute-start.15
  43.1 4.9 collective-permute-done.12
  48.1 393.8 %stage_2.2 = (bf16[128,1024]{1,0:T(8,128)(2,1)S(1)}, bf16[128,1024]{1,0:T(8,128)(2,1)}) custom-call(s32[32,32]{1,0:T(8,128)S(1)} %copy-done.5, s32[32]{0:T(128)S(1)} %copy-done.6, s32[1]{0:T(128)S(6)} %copy.8.refs_2_, bf16[1024,128]{1,0:T(8,128)(2,1)S(1)} %copy-done, bf16[1440,128]{1,0:T(8,128)(2,1)S(1)} %collective-permute-done.refs_4_, ...), custom_call_target="tpu_custom_call" | custom-call | flops 2617245696 | bytes 851968 | tf_op jit(solution)/shard_map/stage_2/pallas_call | solution.py:369
  441.9 1.2 collective-permute-start.14
  443.1 1.3 collective-permute-start.18
  444.5 1.3 fusion
  445.9 0.9 copy-done.2
  446.8 0.9 copy-done.4
  447.7 11.7 %stage_0_3_1.1.refs_6_ = f32[2,1024,256]{2,1,0:T(8,128)S(1)} custom-call(s32[32,32]{1,0:T(8,128)S(1)} %copy-done.5, s32[32]{0:T(128)S(1)} %copy-done.6, s32[1]{0:T(128)S(6)} %copy.8.refs_2_, bf16[1024,128]{1,0:T(8,128)(2,1)S(1)} %copy-done.2, bf16[1024,128]{1,0:T(8,128)(2,1)S(1)} %copy-done.4, ...), custom_call_target="tpu_custom_call" | custom-call | flops 7851737088 | bytes 2555904 | tf_op jit(solution)/shard_map/stage_0_3_1/pallas_call | solution.py:369
  459.5 0.7 collective-permute-done.17
  460.2 393.5 %stage_2.3 = (bf16[128,1024]{1,0:T(8,128)(2,1)S(1)}, bf16[128,1024]{1,0:T(8,128)(2,1)S(1)}) custom-call(s32[32,32]{1,0:T(8,128)S(1)} %copy-done.5, s32[32]{0:T(128)S(1)} %copy-done.6, s32[1]{0:T(128)S(6)} %copy.8.refs_2_, bf16[1024,128]{1,0:T(8,128)(2,1)S(1)} %copy-done.2, bf16[1024,128]{1,0:T(8,128)(2,1)S(1)} %copy-done.4, ...), custom_call_target="tpu_custom_call" | custom-call | flops 2617245696 | bytes 851968 | tf_op jit(solution)/shard_map/stage_2/pallas_call | solution.py:369
  853.7 1.8 collective-permute-start.19
  855.5 1.2 collective-permute-done.19
  856.9 1.1 maximum_bitcast_fusion
  (48 shorter events, 1.5 us)
Async XLA Ops:
  2.3 2.2 collective-permute-start
  5.4 11.8 %collective-permute-start.1 = (bf16[2,2,208,128]{3,2,1,0:T(8,128)(2,1)S(1)}, bf16[2,2,208,128]{3,2,1,0:T(8,128)(2,1)S(1)}, u32[]{:S(2)}, u32[]{:S(2)}) collective-permute-start(bf16[2,2,208,128]{3,2,1,0:T(8,128)(2,1)S(1)} %bitcast.17), channel_id=1, source_target_pairs={{0,2},{1,9},{2,4},{3,11},{4,6},{5,13},{6,0},{7,15},{8,10},{9,17},{... | collective-permute-start | bytes 638984 | tf_op jit(solution)/shard_map/ppermute | solution.py:45
  5.5 11.7 %collective-permute-start.2 = (bf16[2,2,208,128]{3,2,1,0:T(8,128)(2,1)S(1)}, bf16[2,2,208,128]{3,2,1,0:T(8,128)(2,1)S(1)}, u32[]{:S(2)}, u32[]{:S(2)}) collective-permute-start(bf16[2,2,208,128]{3,2,1,0:T(8,128)(2,1)S(1)} %bitcast.18), channel_id=1, source_target_pairs={{0,6},{1,25},{2,0},{3,27},{4,2},{5,29},{6,4},{7,31},{8,14},{9,1},{... | collective-permute-start | bytes 638984 | tf_op jit(solution)/shard_map/ppermute | solution.py:45
  7.0 10.2 %collective-permute-start.3 = (bf16[2,2,208,128]{3,2,1,0:T(8,128)(2,1)S(1)}, bf16[2,2,208,128]{3,2,1,0:T(8,128)(2,1)S(1)}, u32[]{:S(2)}, u32[]{:S(2)}) collective-permute-start(bf16[2,2,208,128]{3,2,1,0:T(8,128)(2,1)S(1)} %bitcast.19), channel_id=1, source_target_pairs={{0,4},{1,17},{2,6},{3,19},{4,0},{5,21},{6,2},{7,23},{8,12},{9,25},... | collective-permute-start | bytes 638984 | tf_op jit(solution)/shard_map/ppermute | solution.py:45
  7.4 7.0 collective-permute-start.4
  8.7 8.5 collective-permute-start.5
  12.1 8.1 copy-start
  12.1 8.1 copy-start.5
  12.1 8.1 copy-start.6
  14.4 5.7 copy-start.11
  17.3 14.2 %collective-permute-start.9 = (bf16[8,2,208,128]{3,2,1,0:T(8,128)(2,1)S(1)}, bf16[8,2,208,128]{3,2,1,0:T(8,128)(2,1)S(1)}, u32[]{:S(2)}, u32[]{:S(2)}) collective-permute-start(bf16[8,2,208,128]{3,2,1,0:T(8,128)(2,1)S(1)} %pad_maximum_fusion.refs_5_.refs_7_), channel_id=1, source_target_pairs={{0,8},{1,3},{2,10},{3,5},{4,12},{5,7},{6,14},{7,1},{8,16},{9,11},{... | collective-permute-start | bytes 2555912 | tf_op jit(solution)/shard_map/ppermute | solution.py:45
  19.2 13.1 %collective-permute-start.10 = (bf16[8,2,208,128]{3,2,1,0:T(8,128)(2,1)S(1)}, bf16[8,2,208,128]{3,2,1,0:T(8,128)(2,1)S(1)}, u32[]{:S(2)}, u32[]{:S(2)}) collective-permute-start(bf16[8,2,208,128]{3,2,1,0:T(8,128)(2,1)S(1)} %pad_maximum_fusion.refs_5_.refs_7_), channel_id=1, source_target_pairs={{0,24},{1,7},{2,26},{3,1},{4,28},{5,3},{6,30},{7,5},{8,0},{9,15},{... | collective-permute-start | bytes 2555912 | tf_op jit(solution)/shard_map/ppermute | solution.py:45
  19.9 8.6 collective-permute-start.6
  20.1 5.4 copy-start.10
  20.1 8.8 %copy-start.9 = (bf16[128,2048]{1,0:T(8,128)(2,1)S(1)}, bf16[128,2048]{1,0:T(8,128)(2,1)}, u32[]{:S(2)}) copy-start(bf16[128,2048]{1,0:T(8,128)(2,1)} %get-tuple-element.74) | copy-start | bytes 1572868
  20.1 8.8 %collective-permute-start.8 = (bf16[1024,128]{1,0:T(8,128)(2,1)S(1)}, bf16[1024,128]{1,0:T(8,128)(2,1)S(1)}, u32[]{:S(2)}, u32[]{:S(2)}) collective-permute-start(bf16[1024,128]{1,0:T(8,128)(2,1)S(1)} %copy-done.11), channel_id=1, source_target_pairs={{0,32},{1,33},{2,34},{3,35},{4,36},{5,37},{6,38},{7,39},{8,40},{9,... | collective-permute-start | bytes 786440 | tf_op jit(solution)/shard_map/ppermute | solution.py:45
  25.5 14.8 %collective-permute-start.11 = (bf16[1024,128]{1,0:T(8,128)(2,1)S(1)}, bf16[1024,128]{1,0:T(8,128)(2,1)S(1)}, u32[]{:S(2)}, u32[]{:S(2)}) collective-permute-start(bf16[1024,128]{1,0:T(8,128)(2,1)S(1)} %copy-done.10), channel_id=1, source_target_pairs={{0,33},{1,32},{2,35},{3,34},{4,37},{5,36},{6,39},{7,38},{8,41},{9,... | collective-permute-start | bytes 786440 | tf_op jit(solution)/shard_map/ppermute | solution.py:45
  28.5 11.8 %collective-permute-start.7 = (bf16[4,2,208,128]{3,2,1,0:T(8,128)(2,1)S(1)}, bf16[4,2,208,128]{3,2,1,0:T(8,128)(2,1)S(1)}, u32[]{:S(2)}, u32[]{:S(2)}) collective-permute-start(bf16[4,2,208,128]{3,2,1,0:T(8,128)(2,1)S(1)} %pad_maximum_fusion.2), channel_id=1, source_target_pairs={{0,6},{1,25},{2,4},{3,27},{4,2},{5,29},{6,0},{7,31},{8,14},{9,17},... | collective-permute-start | bytes 1277960 | tf_op jit(solution)/shard_map/ppermute | solution.py:45
  28.9 11.3 %copy-start.1 = (bf16[1024,128]{1,0:T(8,128)(2,1)}, bf16[1024,128]{1,0:T(8,128)(2,1)S(1)}, u32[]{:S(2)}) copy-start(bf16[1024,128]{1,0:T(8,128)(2,1)S(1)} %collective-permute-done.8.refs_3_) | copy-start | bytes 786436
  28.9 19.2 %collective-permute-start.12 = (bf16[128,2048]{1,0:T(8,128)(2,1)S(1)}, bf16[128,2048]{1,0:T(8,128)(2,1)S(1)}, u32[]{:S(2)}, u32[]{:S(2)}) collective-permute-start(bf16[128,2048]{1,0:T(8,128)(2,1)S(1)} %copy-done.9), channel_id=1, source_target_pairs={{0,32},{1,33},{2,34},{3,35},{4,36},{5,37},{6,38},{7,39},{8,40},{9,... | collective-permute-start | bytes 1572872 | tf_op jit(solution)/shard_map/ppermute | solution.py:45
  31.5 16.6 %collective-permute-start.13 = (bf16[8,2,208,128]{3,2,1,0:T(8,128)(2,1)S(1)}, bf16[8,2,208,128]{3,2,1,0:T(8,128)(2,1)S(1)}, u32[]{:S(2)}, u32[]{:S(2)}) collective-permute-start(bf16[8,2,208,128]{3,2,1,0:T(8,128)(2,1)S(1)} %collective-permute-done.9.refs_5_.refs_8_), channel_id=1, source_target_pairs={{0,8},{1,3},{2,10},{3,5},{4,12},{5,7},{6,14},{7,1},{8,16},{9,11},{... | collective-permute-start | bytes 2555912 | tf_op jit(solution)/shard_map/ppermute | solution.py:45
  40.3 401.6 %copy-start.3 = (bf16[1024,128]{1,0:T(8,128)(2,1)}, bf16[1024,128]{1,0:T(8,128)(2,1)S(1)}, u32[]{:S(2)}) copy-start(bf16[1024,128]{1,0:T(8,128)(2,1)S(1)} %collective-permute-done.11.refs_4_) | copy-start | bytes 786436
  40.4 402.7 %collective-permute-start.16 = (bf16[8,2,208,128]{3,2,1,0:T(8,128)(2,1)S(1)}, bf16[8,2,208,128]{3,2,1,0:T(8,128)(2,1)S(1)}, u32[]{:S(2)}, u32[]{:S(2)}) collective-permute-start(bf16[8,2,208,128]{3,2,1,0:T(8,128)(2,1)S(1)} %pad_maximum_fusion.1.refs_5_.refs_7_), channel_id=1, source_target_pairs={{0,24},{1,7},{2,26},{3,1},{4,28},{5,3},{6,30},{7,5},{8,0},{9,15},{... | collective-permute-start | bytes 2555912 | tf_op jit(solution)/shard_map/ppermute | solution.py:45
  42.2 403.6 %collective-permute-start.15 = (bf16[8,2,208,128]{3,2,1,0:T(8,128)(2,1)S(1)}, bf16[8,2,208,128]{3,2,1,0:T(8,128)(2,1)S(1)}, u32[]{:S(2)}, u32[]{:S(2)}) collective-permute-start(bf16[8,2,208,128]{3,2,1,0:T(8,128)(2,1)S(1)} %pad_maximum_fusion.1.refs_5_.refs_7_), channel_id=1, source_target_pairs={{0,8},{1,3},{2,10},{3,5},{4,12},{5,7},{6,14},{7,1},{8,16},{9,11},{... | collective-permute-start | bytes 2555912 | tf_op jit(solution)/shard_map/ppermute | solution.py:45
  48.1 393.9 %copy-start.7 = (bf16[128,2048]{1,0:T(8,128)(2,1)}, bf16[128,2048]{1,0:T(8,128)(2,1)S(1)}, u32[]{:S(2)}) copy-start(bf16[128,2048]{1,0:T(8,128)(2,1)S(1)} %collective-permute-done.12) | copy-start | bytes 1572868
  441.9 2.6 collective-permute-start.14
  443.1 17.1 %collective-permute-start.18 = (bf16[8,2,208,128]{3,2,1,0:T(8,128)(2,1)S(1)}, bf16[8,2,208,128]{3,2,1,0:T(8,128)(2,1)S(1)}, u32[]{:S(2)}, u32[]{:S(2)}) collective-permute-start(bf16[8,2,208,128]{3,2,1,0:T(8,128)(2,1)S(1)} %collective-permute-done.16.refs_7_.refs_9_), channel_id=1, source_target_pairs={{0,24},{1,7},{2,26},{3,1},{4,28},{5,3},{6,30},{7,5},{8,0},{9,15},{... | collective-permute-start | bytes 2555912 | tf_op jit(solution)/shard_map/ppermute | solution.py:45
  445.8 14.4 %collective-permute-start.17 = (bf16[128,2048]{1,0:T(8,128)(2,1)S(1)}, bf16[128,2048]{1,0:T(8,128)(2,1)S(1)}, u32[]{:S(2)}, u32[]{:S(2)}) collective-permute-start(bf16[128,2048]{1,0:T(8,128)(2,1)S(1)} %fusion), channel_id=1, source_target_pairs={{0,32},{1,33},{2,34},{3,35},{4,36},{5,37},{6,38},{7,39},{8,40},{9,... | collective-permute-start | bytes 1572872 | tf_op jit(solution)/shard_map/ppermute | solution.py:45
  445.8 1.0 copy-start.2
  446.8 0.9 copy-start.4
  459.4 397.2 %copy-start.8 = (bf16[128,2048]{1,0:T(8,128)(2,1)S(1)}, bf16[128,2048]{1,0:T(8,128)(2,1)}, u32[]{:S(2)}) copy-start(bf16[128,2048]{1,0:T(8,128)(2,1)} %copy-done.7) | copy-start | bytes 1572868
  853.7 2.9 collective-permute-start.19
